TPU v7x, 32 devices: a whole 2x2x4 slice. The times are simulated.
32 devices in a mesh: inp: 4 (over y, x), freq: 8 (over z, core).
Axes of the slice: x: 2, y: 2, z: 4, core: 2. Of those that a mesh axis runs over, the one named last changes fastest.
Arguments:
- volts: bfloat16 [16, 2, 2048, 1024], P('freq', None, 'inp'), parts along dimension 0, may hold values from -6 to 6
- position_input: int32 [8, 256], P('inp'), may hold values from 0 to 255, each once within a row
- tile_group: int32 [8, 3, 2], P('inp'), may hold values from 0 to 31
Outputs:
- stacked: float32 [32, 16, 2, 511], P('inp', 'freq'), parts along dimension 1
There are 8 independent parts, one for each index of `freq`. A program takes and returns all parts, laid end to end along the dimension named above; an argument that names none is the same for every part. Nothing has to cross between parts.
Inputs may be any that keep to these rules, and one draw needn't show every extreme that they name: `position_input`: each row holds every position's input index within the block once. `tile_group`: entry [a, l, b] names the row group of the tile of block a with the b-th block of the device at level l of block a's device.
All inputs are finite; a program needn't handle non-finite values.
Results may differ from a plain program's by a relative error of at most 0.0003.
Values may be sent and summed in bfloat16 or wider, within the bound.
No kernel may reach another device: no remote copies, remote signals or barrier semaphores. Data moves between devices by JAX's collectives and lax.ppermute only.
A program may use at most 192 MiB of HBM per device.

v0:
```python
import functools

import jax
import jax.numpy as jnp
from jax import lax
from jax.experimental import pallas as pl
from jax.experimental.pallas import tpu as pltpu
from jax.sharding import PartitionSpec as P

RG_DEV = 8
GROUP_ROWS = 16
HBM = pl.BlockSpec(memory_space=pltpu.HBM)
WHOLE = pl.BlockSpec(memory_space=pltpu.VMEM)


def xor_permute(x, axis, distance):
    return lax.ppermute(x, axis, [(i, i ^ distance) for i in range(lax.axis_size(axis))])


def parity(index, levels):
    bits = index & 1
    for level in range(1, levels):
        bits = bits ^ ((index >> level) & 1)
    return bits


def order_matrix(position_row):
    width = position_row.shape[-1]
    by_position = jnp.transpose(jnp.broadcast_to(position_row, (width, width)))
    inputs = lax.broadcasted_iota(jnp.int32, (width, width), 1)
    return (by_position == inputs).astype(jnp.float32).astype(jnp.bfloat16)


def product(x, y):
    return lax.dot_general(x, y, (((1,), (1,)), ((), ())), preferred_element_type=jnp.float32)


def lag_rows(tiles):
    count, width, _ = tiles.shape
    half = width // 2
    low, high = tiles[:, :half], tiles[:, half:]
    sheared = jnp.concatenate(
        [
            high[:, :, :half],
            high[:, :, half:] + low[:, :, :half],
            low[:, :, half:],
            jnp.zeros((count, half, half), jnp.float32),
        ],
        axis=2,
    )
    rows = half
    while rows > 8:
        rows //= 2
        upper = sheared[:, :rows].reshape(count * rows, 2 * width)
        upper = pltpu.roll(upper, rows, 1).reshape(count, rows, 2 * width)
        sheared = upper + sheared[:, rows:]
    flat = sheared.reshape(count * rows, 2 * width)
    sublane = lax.broadcasted_iota(jnp.int32, flat.shape, 0) % 8
    while rows > 1:
        rows //= 2
        flat = jnp.where((sublane & rows) == 0, pltpu.roll(flat, rows, 1), flat)
    return jnp.sum(flat.reshape(count, 8, 2 * width), axis=1)


def tile_lags(x_re, x_im, y_re, y_im, samples):
    real_part = product(x_re, y_re) + product(x_im, y_im)
    imag_part = product(x_im, y_re) - product(x_re, y_im)
    return lag_rows(jnp.stack([real_part, imag_part])) * (1.0 / samples)


def split_rows(x):
    first = x.astype(jnp.bfloat16).astype(jnp.float32)
    rest = x - first
    second = rest.astype(jnp.bfloat16).astype(jnp.float32)
    return jnp.concatenate([first, second, rest - second], axis=0)


def anti_identity(size):
    place = lax.broadcasted_iota(jnp.int32, (size, size), 0) + lax.broadcasted_iota(
        jnp.int32, (size, size), 1
    )
    return (place == size - 1).astype(jnp.float32).astype(jnp.bfloat16)


def turn_lags(terms):
    count, width = terms.shape
    lanes = 128
    spans = range(0, width, lanes)
    terms = jnp.concatenate([terms[:, first : first + lanes] for first in spans], axis=0)
    terms = jnp.dot(
        terms.astype(jnp.bfloat16), anti_identity(lanes), preferred_element_type=jnp.float32
    )
    blocks = [terms[count * i : count * (i + 1)] for i in reversed(range(len(spans)))]
    return pltpu.roll(jnp.concatenate(blocks, axis=1), width - 1, 1)


def conjugate_lags(lags):
    count = lags.shape[0]
    turned = turn_lags(split_rows(lags))
    turned = turned[:count] + turned[count : 2 * count] + turned[2 * count :]
    odd = lax.broadcasted_iota(jnp.int32, turned.shape, 0) % 2 == 1
    return jnp.where(odd, -turned, turned)


def reversed_lags(lags):
    count, width = lags.shape
    lanes = 128
    rows = jnp.pad(lags, ((0, -count % 8), (0, 0)))
    index = lanes - 1 - lax.broadcasted_iota(jnp.int32, (rows.shape[0], lanes), 1)
    blocks = [
        jnp.take_along_axis(
            rows[:, first : first + lanes], index, axis=1, mode="promise_in_bounds"
        )
        for first in reversed(range(0, width, lanes))
    ]
    return pltpu.roll(jnp.concatenate(blocks, axis=1), width - 1, 1)[:count]


def sheared_eights(tiles):
    count, width, _ = tiles.shape
    half = width // 2
    low, high = tiles[:, :half], tiles[:, half:]
    sheared = jnp.concatenate(
        [
            low[:, :, :half],
            low[:, :, half:] + high[:, :, :half],
            high[:, :, half:],
            jnp.zeros((count, half, half), jnp.float32),
        ],
        axis=2,
    )
    rows = half
    while rows > 8:
        rows //= 2
        lower = sheared[:, rows:].reshape(count * rows, 2 * width)
        lower = pltpu.roll(lower, rows, 1).reshape(count, rows, 2 * width)
        sheared = sheared[:, :rows] + lower
    return [pltpu.roll(sheared[i], 0, 1, stride=1, stride_axis=0) for i in range(count)]


def group_block(groups, columns=128):
    rows = jnp.concatenate([groups[b] for b in range(groups.shape[0])], axis=0)
    lines, lanes = rows.shape
    return jnp.pad(rows, ((0, GROUP_ROWS - lines), (0, columns - lanes)))


def target_rows(groups):
    return groups ^ (lax.axis_index("inp") * RG_DEV)


def pick_matrix(entries, rows):
    count = len(entries)
    shape = (rows, 3 * count)
    row = lax.broadcasted_iota(jnp.int32, shape, 0)
    column = lax.broadcasted_iota(jnp.int32, shape, 1) % count
    pick = jnp.zeros(shape, jnp.float32)
    for j, (targets, line, lane, part) in enumerate(entries):
        target = targets[line : line + 1, lane : lane + 1] + part * (rows // 2)
        target = jnp.broadcast_to(target, shape)
        pick = jnp.where(jnp.logical_and(column == j, row == target), 1.0, pick)
    return pick.astype(jnp.bfloat16)


def row_masks(entries, rows):
    row = lax.broadcasted_iota(jnp.int32, (rows, 128), 0)
    masks = []
    for targets, line, lane, _ in entries:
        target = jnp.broadcast_to(targets[line : line + 1, lane : lane + 1], row.shape)
        masks.append((row == target).astype(jnp.float32))
    return jnp.stack(masks)


def pick_matrices(groups, heads, blocks, out_rows):
    own = target_rows(group_block(groups))
    others = [target_rows(head.astype(jnp.float32).astype(jnp.int32)) for head in heads]
    groups_all = out_rows // 2

    def pairs(b):
        order = [(level, a, p) for level in range(len(heads)) for a in range(blocks) for p in range(2)]
        forward = [(own, a * blocks + b, level + 1, p) for level, a, p in order]
        turned = [(others[level], b * blocks + a, level + 1, p) for level, a, p in order]
        return forward, turned

    forward, turned = zip(*[pairs(b) for b in range(blocks)])
    tiles = [
        [(targets, line, 0, p) for line in range(blocks * blocks) for p in range(2)]
        for targets in (own, others[-1])
    ]
    both = [entry for side in (forward, turned) for block in side for entry in block]
    return [
        pick_matrix(tiles[0], out_rows),
        pick_matrix(tiles[1], out_rows),
        pick_matrix(both, out_rows),
        pick_matrix(forward[-1] + turned[-1], out_rows),
        row_masks(forward[-1][::2] + turned[-1][::2], groups_all),
    ]


def group_sums(pick, lags):
    terms = split_rows(lags).astype(jnp.bfloat16)
    return jnp.dot(pick, terms, preferred_element_type=jnp.float32)


def columns(piece):
    spans, start = [], 0
    for _, first, last in piece:
        spans.append((start, start + last - first))
        start += last - first
    return spans


def piece_shape(piece, width, more):
    return jax.ShapeDtypeStruct((2 * width + more, columns(piece)[-1][1]), jnp.bfloat16)


def load_piece(piece, other, width, volts_ref, raw, in_sem):
    blocks = sorted({block for block, _, _ in piece})
    loads = []
    for i, block in enumerate(blocks):
        start = min(first for b, first, _ in piece if b == block)
        end = max(last for b, _, last in piece if b == block)
        for c in range(2):
            load = pltpu.make_async_copy(
                volts_ref.at[other, c, pl.ds(block * width, width), pl.ds(start, end - start)],
                raw.at[i, c, :, pl.ds(start, end - start)],
                in_sem.at[i, c],
            )
            load.start()
            loads.append((i, block, c, load))
    return loads


def order_piece(piece, loads, position, raw, out_ref):
    width = position.shape[1]
    orders = {
        block: order_matrix(position[block : block + 1, :]) for block in sorted({l[1] for l in loads})
    }
    for i, block, c, load in loads:
        load.wait()
        for (b, first, last), (start, end) in zip(piece, columns(piece)):
            if b == block:
                out_ref[c * width : (c + 1) * width, start:end] = jnp.dot(
                    orders[block], raw[i, c, :, first:last], preferred_element_type=jnp.float32
                ).astype(jnp.bfloat16)


def head_kernel(levels, piece, position_ref, volts_ref, group_ref, head_ref, *scratch):
    position, groups, small_sem, in_sem = scratch
    other = 1 - parity(lax.axis_index("inp"), levels)
    width = position.shape[1]
    ((block, first, last),) = piece
    smalls = [
        pltpu.make_async_copy(position_ref, position, small_sem.at[0]),
        pltpu.make_async_copy(group_ref, groups, small_sem.at[1]),
    ]
    loads = [
        pltpu.make_async_copy(
            volts_ref.at[other, c, pl.ds(block * width, width), pl.ds(first, last - first)],
            head_ref.at[pl.ds(c * width, width), :],
            in_sem.at[c],
        )
        for c in range(2)
    ]
    for copy in smalls + loads:
        copy.start()
    for copy in smalls:
        copy.wait()
    rows = group_block(groups[...], last - first)
    line = lax.broadcasted_iota(jnp.int32, rows.shape, 0)
    own_row = jnp.broadcast_to(position[block : block + 1, :], rows.shape)
    rows = jnp.where(line == groups.shape[0] ** 2, own_row, rows)
    head_ref[2 * width :, :] = rows.astype(jnp.float32).astype(jnp.bfloat16)
    for copy in loads:
        copy.wait()


def on_odd_core():
    return lax.axis_index("freq") % 2 == 1


def load_channel(channel, volts_ref, raw, in_sem):
    blocks, _, width, _ = raw.shape
    loads = []
    for b in range(blocks):
        for c in range(2):
            load = pltpu.make_async_copy(
                volts_ref.at[channel, c, pl.ds(b * width, width)], raw.at[b, c], in_sem.at[b, c]
            )
            load.start()
            loads.append((b, c, load))
    return loads


def own_tiles(loads, position_ref, raw, panel, lags_ref, start):
    blocks, _, width, samples = raw.shape
    orders = [order_matrix(position_ref[b : b + 1, :]) for b in range(blocks)]
    for b, c, load in loads:
        load.wait()
        rows = jnp.dot(orders[b], raw[b, c], preferred_element_type=jnp.float32)
        panel[b, c] = rows.astype(jnp.bfloat16)

    def one_tile(index, carry):
        a = index // blocks
        b = index % blocks
        lags = tile_lags(panel[a, 0], panel[a, 1], panel[b, 0], panel[b, 1], samples)
        center = lax.broadcasted_iota(jnp.int32, lags.shape, 1) == width - 1
        lags_ref[start + index] = jnp.where(jnp.logical_and(center, a == b), 0.0, lags)
        return carry

    lax.fori_loop(0, blocks * blocks, one_tile, 0)


def rest_kernel(levels, piece, position_ref, volts_ref, _, out_ref, panel_ref, lags_ref, *scratch):
    position, raw, small_sem, in_sem = scratch
    mine = parity(lax.axis_index("inp"), levels)
    load_position = pltpu.make_async_copy(position_ref, position, small_sem)
    load_position.start()
    load_position.wait()

    @pl.when(on_odd_core())
    def _():
        loads = load_channel(mine, volts_ref, raw, in_sem)
        own_tiles(loads, position, raw, panel_ref, lags_ref, 0)

    loads = load_piece(piece, 1 - mine, position.shape[1], volts_ref, raw, in_sem)
    order_piece(piece, loads, position, raw, out_ref)


def early_pieces(position_input, volts, groups, head, rest, levels):
    blocks, width = position_input.shape
    samples = volts.shape[3]
    assert columns(head)[-1][1] == width
    in_hbm = [pltpu.with_memory_space_constraint(x, pltpu.HBM) for x in (position_input, volts)]
    position = pltpu.VMEM(position_input.shape, jnp.int32)
    semaphore = pltpu.SemaphoreType.DMA
    sent = pl.pallas_call(
        functools.partial(head_kernel, levels, head),
        out_shape=piece_shape(head, width, GROUP_ROWS),
        in_specs=[HBM] * 3,
        out_specs=WHOLE,
        scratch_shapes=[
            position,
            pltpu.VMEM(groups.shape, jnp.int32),
            semaphore((2,)),
            semaphore((2,)),
        ],
        compiler_params=pltpu.CompilerParams(vmem_limit_bytes=8 << 20),
        cost_estimate=pl.CostEstimate(flops=0, bytes_accessed=1 << 20, transcendentals=0),
        name="first_piece",
    )(*in_hbm, pltpu.with_memory_space_constraint(groups, pltpu.HBM))
    second, early_panel, early_lags = pl.pallas_call(
        functools.partial(rest_kernel, levels, rest),
        out_shape=[
            piece_shape(rest, width, 0),
            jax.ShapeDtypeStruct((blocks, 2, width, samples), jnp.bfloat16),
            jax.ShapeDtypeStruct((blocks * blocks, 2, 2 * width), jnp.float32),
        ],
        in_specs=[HBM, HBM, pl.BlockSpec(memory_space=pl.ANY)],
        out_specs=[WHOLE] * 3,
        scratch_shapes=[
            position,
            pltpu.VMEM((blocks, 2, width, samples), jnp.bfloat16),
            semaphore(()),
            semaphore((blocks, 2)),
        ],
        compiler_params=pltpu.CompilerParams(vmem_limit_bytes=16 << 20),
        cost_estimate=pl.CostEstimate(
            flops=4 * width * width * columns(rest)[-1][1],
            bytes_accessed=4 << 20,
            transcendentals=0,
        ),
        name="second_piece",
    )(*in_hbm, sent)
    return sent, second, early_panel, early_lags


def own_kernel(levels, piece, last, group_ref, position_ref, volts_ref, *refs):
    head_refs, refs = refs[:levels][::-1], refs[levels:]
    early_panel_ref, early_lags_ref, *refs = refs
    panel_ref, sums_ref, *refs, raw, other_raw, other_panel, lags_ref, in_sem, other_sem = refs
    pick_refs, ordered_refs, refs = refs[:4], refs[4 : 4 + levels], refs[4 + levels :]
    more_ref, piece_ref, *last_refs, joined_ref, last_panel_ref = refs
    blocks, _, width, _ = panel_ref.shape
    mine = parity(lax.axis_index("inp"), levels)
    other_loads = load_channel(1 - mine, volts_ref, other_raw, other_sem)

    @pl.when(jnp.logical_not(on_odd_core()))
    def _():
        loads = load_channel(mine, volts_ref, raw, in_sem)
        own_tiles(loads, position_ref, raw, panel_ref, lags_ref, 0)

    @pl.when(on_odd_core())
    def _():
        for b in range(blocks):
            for c in range(2):
                panel_ref[b, c] = early_panel_ref[b, c]
        for i in range(blocks * blocks):
            lags_ref[i] = early_lags_ref[i]

    own_tiles(other_loads, position_ref, other_raw, other_panel, lags_ref, blocks * blocks)
    tiles = blocks * blocks
    lags = jnp.concatenate([lags_ref[i] for i in range(tiles)], axis=0)
    heads = [head_ref[2 * width :, :] for head_ref in head_refs]
    for head, head_ref, ordered_ref in zip(heads, head_refs, ordered_refs):
        positions = head.astype(jnp.float32).astype(jnp.int32)[blocks**2 : blocks**2 + 1]
        order = order_matrix(positions)
        for c in range(2):
            rows = head_ref[c * width : (c + 1) * width, :]
            rows = jnp.dot(order, rows, preferred_element_type=jnp.float32)
            ordered_ref[c * width : (c + 1) * width, :] = rows.astype(jnp.bfloat16)
    own_pick, *picks = pick_matrices(group_ref[...], heads, blocks, sums_ref.shape[0])
    for pick_ref, pick in zip(pick_refs, picks):
        pick_ref[...] = pick
    sums_ref[...] = group_sums(own_pick, lags)
    for (block, first, end), (start, stop) in zip(piece, columns(piece)):
        for c in range(2):
            rows = other_panel[block, c, :, first:end]
            piece_ref[c * width : (c + 1) * width, start:stop] = rows
            more_ref[c * width : (c + 1) * width, start:stop] = rows
    lags = jnp.concatenate([lags_ref[tiles + i] for i in range(tiles)], axis=0)
    high = lags.astype(jnp.bfloat16).astype(jnp.float32)
    terms = jnp.concatenate([high, lags - high], axis=0)
    more_ref[2 * width :, :] = terms.astype(jnp.bfloat16)
    start = 0
    for (block, first, end), last_ref in zip(last, last_refs):
        for c in range(2):
            depth = end - first
            rows = other_panel[block, c, :, first:end]
            last_ref[:, c * depth : (c + 1) * depth] = rows
            joined_ref[:, start : start + depth] = rows
            start += depth
    turn = anti_identity(width)
    for a in range(blocks):
        start = 0
        for _, first, end in last:
            real_part, imag_part = [
                jnp.dot(turn, panel_ref[a, c, :, first:end], preferred_element_type=jnp.float32)
                for c in range(2)
            ]
            middle, stop = start + end - first, start + 2 * (end - first)
            last_panel_ref[a, :width, start:middle] = real_part.astype(jnp.bfloat16)
            last_panel_ref[a, :width, middle:stop] = imag_part.astype(jnp.bfloat16)
            last_panel_ref[a, width:, start:middle] = imag_part.astype(jnp.bfloat16)
            last_panel_ref[a, width:, middle:stop] = (-real_part).astype(jnp.bfloat16)
            start = stop


def own_level(groups, position_input, volts, early, heads, piece, last, out_rows):
    levels = len(heads)
    blocks, width = position_input.shape
    samples = volts.shape[3]
    pairs = 4 * levels * blocks
    tiles = 2 * blocks * blocks
    counts = (3 * tiles, 3 * pairs * blocks, 3 * pairs)
    depths = [2 * (end - first) for _, first, end in last]
    return pl.pallas_call(
        functools.partial(own_kernel, levels, piece, last),
        out_shape=(
            jax.ShapeDtypeStruct((blocks, 2, width, samples), jnp.bfloat16),
            jax.ShapeDtypeStruct((out_rows, 2 * width), jnp.float32),
            *[jax.ShapeDtypeStruct((out_rows, n), jnp.bfloat16) for n in counts],
            jax.ShapeDtypeStruct((pairs // 2, out_rows // 2, 128), jnp.float32),
            *[jax.ShapeDtypeStruct((2 * width, head.shape[1]), jnp.bfloat16) for head in heads],
            piece_shape(piece, width, 2 * tiles),
            piece_shape(piece, width, 0),
            *[jax.ShapeDtypeStruct((width, depth), jnp.bfloat16) for depth in depths],
            jax.ShapeDtypeStruct((width, sum(depths)), jnp.bfloat16),
            jax.ShapeDtypeStruct((blocks, 2 * width, sum(depths)), jnp.bfloat16),
        ),
        in_specs=[WHOLE, WHOLE, HBM] + [WHOLE] * (len(early) + levels),
        out_specs=(WHOLE,) * (7 + len(counts) + levels + len(last)),
        scratch_shapes=[
            pltpu.VMEM((blocks, 2, width, samples), jnp.bfloat16),
            pltpu.VMEM((blocks, 2, width, samples), jnp.bfloat16),
            pltpu.VMEM((blocks, 2, width, samples), jnp.bfloat16),
            pltpu.VMEM((2 * blocks * blocks, 2, 2 * width), jnp.float32),
            pltpu.SemaphoreType.DMA((blocks, 2)),
            pltpu.SemaphoreType.DMA((blocks, 2)),
        ],
        compiler_params=pltpu.CompilerParams(vmem_limit_bytes=16 << 20),
        cost_estimate=pl.CostEstimate(
            flops=64 * blocks * blocks * width * width * samples,
            bytes_accessed=12 * blocks * width * samples,
            transcendentals=0,
        ),
        name="own_level",
    )(groups, position_input, pltpu.with_memory_space_constraint(volts, pltpu.HBM), *heads[::-1], *early)


def add_lags(rows, pick_ref, sums_ref):
    lags = jnp.concatenate(rows, axis=0)
    lags = jnp.concatenate([lags, conjugate_lags(lags)], axis=0)
    return sums_ref[...] + group_sums(pick_ref[...], lags)


def pair_kernel(levels, pieces, passed, pick_ref, sums_ref, panel_ref, *refs):
    count = levels * len(pieces)
    out_ref = refs[-1 - passed]
    partner_refs, more_refs = refs[:count], refs[count : len(refs) - 1 - 2 * passed]
    _, _, width, samples = panel_ref.shape
    rows = []
    for block in sorted({block for piece in pieces for block, _, _ in piece}):
        for level in range(levels):
            for a in range(panel_ref.shape[0]):
                real_part, imag_part = 0.0, 0.0
                for i, piece in enumerate(pieces):
                    partner = partner_refs[level * len(pieces) + i]
                    for (b, first, last), (start, end) in zip(piece, columns(piece)):
                        if b != block:
                            continue
                        x_re, x_im = panel_ref[a, 0, :, first:last], panel_ref[a, 1, :, first:last]
                        y_re = partner[:width, start:end]
                        y_im = partner[width : 2 * width, start:end]
                        real_part = real_part + (product(x_re, y_re) + product(x_im, y_im))
                        imag_part = imag_part + (product(x_im, y_re) - product(x_re, y_im))
                rows.append(lag_rows(jnp.stack([real_part, imag_part])) * (1.0 / samples))
    sums = add_lags(rows, pick_ref, sums_ref)
    for more_ref in more_refs:
        terms = partner_refs[-1][2 * width :, :].astype(jnp.float32)
        half = terms.shape[0] // 2
        sums = sums + group_sums(more_ref[...], terms[:half] + terms[half:])
    out_ref[...] = sums


def last_kernel(parts, samples, mask_ref, sums_ref, panel_ref, *refs):
    partner_refs, out_refs = refs[: len(parts)], refs[len(parts) :]
    blocks, rows_both, _ = panel_ref.shape
    width = rows_both // 2
    rows, tiles_at = [], []
    for (level, first, last), partner_ref in zip(parts, partner_refs):
        for a in range(blocks):
            tiles = product(panel_ref[a, :, first:last], partner_ref[...])
            rows += sheared_eights(tiles.reshape(2, width, width))
            tiles_at.append(level * blocks + a)
    lags = jnp.sum(jnp.stack(rows), axis=1) * (1.0 / samples)
    turned = reversed_lags(lags)
    half = sums_ref.shape[0] // 2
    sums = [sums_ref[:half, :], sums_ref[half:, :]]
    count = mask_ref.shape[0] // 2
    for i, tile in enumerate(tiles_at):
        forward = jnp.concatenate([mask_ref[tile]] * (sums_ref.shape[1] // 128), axis=1)
        back = jnp.concatenate([mask_ref[count + tile]] * (sums_ref.shape[1] // 128), axis=1)
        re, im = 2 * i, 2 * i + 1
        sums[0] = sums[0] + forward * lags[re : re + 1] + back * turned[re : re + 1]
        sums[1] = sums[1] + forward * lags[im : im + 1] - back * turned[im : im + 1]
    share = half // len(out_refs)
    for place, out_ref in enumerate(out_refs):
        for part in range(2):
            rows = sums[part][place * share : (place + 1) * share]
            out_ref[part * share : (part + 1) * share, :] = rows


def pair_call(kernel, inputs, work, shares=1, passed=()):
    rows, width = inputs[1].shape
    any_space = [pl.BlockSpec(memory_space=pl.ANY)] * len(passed)
    return pl.pallas_call(
        kernel,
        out_shape=[jax.ShapeDtypeStruct((rows // shares, width), jnp.float32)] * shares
        + [jax.ShapeDtypeStruct(x.shape, x.dtype) for x in passed],
        in_specs=[WHOLE] * len(inputs) + any_space,
        out_specs=[WHOLE] * shares + any_space,
        input_output_aliases={len(inputs) + i: shares + i for i in range(len(passed))},
        compiler_params=pltpu.CompilerParams(vmem_limit_bytes=16 << 20),
        cost_estimate=pl.CostEstimate(flops=work, bytes_accessed=4 << 20, transcendentals=0),
        name="pair_level",
    )(*inputs, *passed)


def finish_kernel(levels, distances, *refs):
    part_refs, out_ref = refs[:-1], refs[-1]
    mine = parity(lax.axis_index("inp"), levels)
    groups, channels, parts, lags = out_ref.shape
    sums = [None, None]
    for distance, part_ref in zip(distances, part_refs):
        side = distance.bit_count() % 2
        sums[side] = part_ref[...] if sums[side] is None else sums[side] + part_ref[...]
    for f in range(channels):
        total = jnp.where(mine == f, sums[0], sums[1])
        for g in range(groups):
            for part in range(parts):
                row = part * groups + g
                out_ref[g, f, part : part + 1] = total[row : row + 1, :lags]


def finish(parts, distances, levels, lags):
    return pl.pallas_call(
        functools.partial(finish_kernel, levels, distances),
        out_shape=jax.ShapeDtypeStruct((RG_DEV, 2, 2, lags), jnp.float32),
        in_specs=[WHOLE] * len(parts),
        out_specs=WHOLE,
        compiler_params=pltpu.CompilerParams(vmem_limit_bytes=8 << 20),
        name="finish",
    )(*parts)


def on_device(volts, position_input, tile_group):
    blocks, width = position_input.shape
    samples = volts.shape[3]
    devices = lax.axis_size("inp")
    levels = devices.bit_length() - 1
    out_rows = devices * RG_DEV * 2
    eighth = samples // 8
    head = [(0, 0, 2 * eighth)]
    rest = [(0, 2 * eighth, samples), (1, 0, 2 * eighth)]
    tail = [(1, 2 * eighth, 6 * eighth)]
    last = [(1, 6 * eighth, 7 * eighth), (1, 7 * eighth, samples)]
    by_block = tile_group.transpose(0, 2, 1)
    partner_of = [functools.partial(xor_permute, axis="inp", distance=1 << l) for l in range(levels)]
    sent, second, *early = early_pieces(position_input, volts, by_block, head, rest, levels)
    head_arrived = [send(sent) for send in partner_of]
    rest_arrived = [send(second) for send in partner_of]
    panel, sums, neighbour, both, single, masks, *sent = own_level(
        by_block, position_input, volts, early, head_arrived, tail, last, out_rows
    )
    head_ordered, (more, piece, *last_pieces, last_panel) = sent[:levels], sent[levels:]
    tail_arrived = [send(piece) for send in partner_of[:-1]] + [partner_of[-1](more)]

    flops = 8 * levels * blocks * width * width
    arrived = [piece for pair in zip(head_ordered, rest_arrived) for piece in pair]
    sums, *last_pieces = pair_call(
        functools.partial(pair_kernel, levels, [head, rest], len(last_pieces)),
        [both, sums, panel, *arrived],
        flops * 10 * eighth,
        passed=last_pieces,
    )
    *last_pieces, joined = last_pieces
    last_arrived = [[send(piece) for send in partner_of[:-1]] for piece in last_pieces]
    last_arrived[-1].append(partner_of[-1](joined))
    (sums,) = pair_call(
        functools.partial(pair_kernel, levels, [tail], 0),
        [single, sums, panel, *tail_arrived, neighbour],
        flops * 4 * eighth,
    )
    for i, arrived in enumerate(last_arrived):
        final = i == len(last_arrived) - 1
        columns_of = [(2 * eighth * i, 2 * eighth * (i + 1))] * (levels - 1)
        if final:
            columns_of.append((0, joined.shape[1]))
        parts = pair_call(
            functools.partial(
                last_kernel, [(level, *cut) for level, cut in enumerate(columns_of)], samples
            ),
            [masks, sums, last_panel, *arrived],
            flops * eighth,
            devices if final else 1,
        )
        sums = parts[0]
    distances = [1, *range(devices - 1, 1, -1), 0]
    parts = [
        xor_permute(parts[distance], "inp", distance) if distance else parts[0]
        for distance in distances
    ]
    return finish(parts, distances, levels, 2 * width - 1)


def solution(mesh):
    return jax.shard_map(
        on_device,
        mesh=mesh,
        in_specs=(P("freq", None, "inp", None), P("inp", None), P("inp", None, None)),
        out_specs=P("inp", "freq", None, None),
        check_vma=False,
    )
```

profile of v0, /device:TPU:1, one launch (start us, length us, event | category | flops | bytes accessed | tf_op | source)
XLA Modules:
  0.0 59.0 jit_solution(15775124666788418066)
XLA Ops:
  0.0 1.0 %first_piece.1._ = bf16[528,256]{1,0:T(8,128)(2,1)S(1)} custom-call(s32[2,256]{1,0:T(2,128)} %position_ref.5, bf16[2,2,512,1024]{3,2,1,0:T(8,128)(2,1)} %volts_ref.5, s32[2,2,3]{2,1,0:T(2,128)} %bitcast.1), custom_call_target="tpu_custom_call" | custom-call | bytes 1048576 | tf_op jit(solution)/shard_map/first_piece/pallas_call | solution.py:336
  1.0 0.0 copy-start
  1.1 0.0 copy-start.1
  1.1 2.1 %collective-permute-start = (bf16[528,256]{1,0:T(8,128)(2,1)S(1)}, bf16[528,256]{1,0:T(8,128)(2,1)S(1)}, u32[]{:S(2)}, u32[]{:S(2)}) collective-permute-start(bf16[528,256]{1,0:T(8,128)(2,1)S(1)} %first_piece.1._), channel_id=1, source_target_pairs={{0,16},{8,24},{16,0},{24,8},{1,17},{9,25},{17,1},{25,9},{2,18},{10... | collective-permute-start | bytes 811016 | tf_op jit(solution)/shard_map/ppermute | solution.py:17
  3.2 1.2 %collective-permute-start.1 = (bf16[528,256]{1,0:T(8,128)(2,1)S(1)}, bf16[528,256]{1,0:T(8,128)(2,1)S(1)}, u32[]{:S(2)}, u32[]{:S(2)}) collective-permute-start(bf16[528,256]{1,0:T(8,128)(2,1)S(1)} %first_piece.1._), channel_id=1, source_target_pairs={{0,8},{8,0},{16,24},{24,16},{1,9},{9,1},{17,25},{25,17},{2,10},{10... | collective-permute-start | bytes 811016 | tf_op jit(solution)/shard_map/ppermute | solution.py:17
  4.4 10.0 %second_piece.1 = (bf16[512,1024]{1,0:T(8,128)(2,1)S(1)}, bf16[2,2,256,1024]{3,2,1,0:T(8,128)(2,1)S(1)}, f32[4,2,512]{2,1,0:T(2,128)S(1)}) custom-call(s32[2,256]{1,0:T(2,128)} %position_ref.5, bf16[2,2,512,1024]{3,2,1,0:T(8,128)(2,1)} %volts_ref.5, bf16[528,256]{1,0:T(8,128)(2,1)S(1)} %first_piece.1._), custom_call_target="tpu_custom_call" | custom-call | flops 268435456 | bytes 4194304 | tf_op jit(solution)/shard_map/second_piece/pallas_call | solution.py:351
  14.4 0.3 collective-permute-start.2
  14.7 0.1 collective-permute-start.3
  14.8 0.0 collective-permute-done.refs_0_
  14.8 0.0 collective-permute-done.1.refs_1_
  14.8 0.0 copy-done
  14.8 0.0 copy-done.1
  14.8 8.2 %own_level.1 = (bf16[2,2,256,1024]{3,2,1,0:T(8,128)(2,1)S(1)}, f32[64,512]{1,0:T(8,128)S(1)}, bf16[64,24]{1,0:T(8,128)(2,1)S(1)}, bf16[64,96]{1,0:T(8,128)(2,1)S...) custom-call(s32[2,2,3]{2,1,0:T(2,128)S(1)} %bitcast.2, ...), custom_call_target="tpu_custom_call" | custom-call | flops 17179869184 | bytes 6291456 | tf_op jit(solution)/shard_map/own_level/pallas_call | solution.py:456
  23.0 1.5 %collective-permute-start.5 = (bf16[528,512]{1,0:T(8,128)(2,1)S(1)}, bf16[528,512]{1,0:T(8,128)(2,1)S(1)}, u32[]{:S(2)}, u32[]{:S(2)}) collective-permute-start(bf16[528,512]{1,0:T(8,128)(2,1)S(1)} %get-tuple-element.45), channel_id=1, source_target_pairs={{0,16},{8,24},{16,0},{24,8},{1,17},{9,25},{17,1},{25,9},{2,18},{10... | collective-permute-start | bytes 1622024 | tf_op jit(solution)/shard_map/ppermute | solution.py:17
  24.5 1.2 %collective-permute-start.4 = (bf16[512,512]{1,0:T(8,128)(2,1)S(1)}, bf16[512,512]{1,0:T(8,128)(2,1)S(1)}, u32[]{:S(2)}, u32[]{:S(2)}) collective-permute-start(bf16[512,512]{1,0:T(8,128)(2,1)S(1)} %get-tuple-element.44), channel_id=1, source_target_pairs={{0,8},{8,0},{16,24},{24,16},{1,9},{9,1},{17,25},{25,17},{2,10},{10... | collective-permute-start | bytes 1572872 | tf_op jit(solution)/shard_map/ppermute | solution.py:17
  25.7 11.6 %collective-permute-done.2.refs_1_ = bf16[512,1024]{1,0:T(8,128)(2,1)S(1)} collective-permute-done((bf16[512,1024]{1,0:T(8,128)(2,1)S(1)}, bf16[512,1024]{1,0:T(8,128)(2,1)S(1)}, u32[]{:S(2)}, u32[]{:S(2)}) %collective-permute-start.2) | collective-permute-done | bytes 1048608 | tf_op jit(solution)/shard_map/ppermute | solution.py:17
  37.3 1.3 %collective-permute-done.3.refs_3_ = bf16[512,1024]{1,0:T(8,128)(2,1)S(1)} collective-permute-done((bf16[512,1024]{1,0:T(8,128)(2,1)S(1)}, bf16[512,1024]{1,0:T(8,128)(2,1)S(1)}, u32[]{:S(2)}, u32[]{:S(2)}) %collective-permute-start.3) | collective-permute-done | bytes 1048608 | tf_op jit(solution)/shard_map/ppermute | solution.py:17
  38.6 3.9 %pair_level.4 = (f32[64,512]{1,0:T(8,128)S(1)}, bf16[256,256]{1,0:T(8,128)(2,1)S(1)}, bf16[256,256]{1,0:T(8,128)(2,1)S(1)}, bf16[256,512]{1,0:T(8,128)(2,1)S(1)}) custom-call(bf16[64,96]{1,0:T(8,128)(2,1)S(1)} %get-tuple-element.34.pick_ref, f32[64,512]{1,0:T(8,128)S(1)} %get-tuple-element.35.sums_ref, ...), custom_call_target="tpu_custom_call", output_to_operand_aliasing={{1}: (7, {}), {2}: (8, {}), {3}: (9, {})} | custom-call | flops 2684354560 | bytes 4194304 | tf_op jit(solution)/shard_map/pair_level/pallas_call | solution.py:556
  42.5 0.1 collective-permute-start.8
  42.6 1.4 %collective-permute-start.6 = (bf16[256,256]{1,0:T(8,128)(2,1)S(1)}, bf16[256,256]{1,0:T(8,128)(2,1)S(1)}, u32[]{:S(2)}, u32[]{:S(2)}) collective-permute-start(bf16[256,256]{1,0:T(8,128)(2,1)S(1)} %get-tuple-element.48), channel_id=1, source_target_pairs={{0,8},{8,0},{16,24},{24,16},{1,9},{9,1},{17,25},{25,17},{2,10},{10... | collective-permute-start | bytes 393224 | tf_op jit(solution)/shard_map/ppermute | solution.py:17
  44.0 0.1 collective-permute-start.7
  44.1 3.8 %collective-permute-done.4.refs_0_ = bf16[512,512]{1,0:T(8,128)(2,1)S(1)} collective-permute-done((bf16[512,512]{1,0:T(8,128)(2,1)S(1)}, bf16[512,512]{1,0:T(8,128)(2,1)S(1)}, u32[]{:S(2)}, u32[]{:S(2)}) %collective-permute-start.4) | collective-permute-done | bytes 524320 | tf_op jit(solution)/shard_map/ppermute | solution.py:17
  47.9 0.8 %collective-permute-done.5.refs_1_ = bf16[528,512]{1,0:T(8,128)(2,1)S(1)} collective-permute-done((bf16[528,512]{1,0:T(8,128)(2,1)S(1)}, bf16[528,512]{1,0:T(8,128)(2,1)S(1)}, u32[]{:S(2)}, u32[]{:S(2)}) %collective-permute-start.5) | collective-permute-done | bytes 540704 | tf_op jit(solution)/shard_map/ppermute | solution.py:17
  48.8 2.2 %pair_level.5.sums_ref = f32[64,512]{1,0:T(8,128)S(1)} custom-call(bf16[64,48]{1,0:T(8,128)(2,1)S(1)} %get-tuple-element.33.pick_ref, f32[64,512]{1,0:T(8,128)S(1)} %get-tuple-element.43.sums_ref, bf16[2,2,256,1024]{3,2,1,0:T(8,128)(2,1)S(1)} %get-tuple-element.36.panel_ref, bf16[512,512]{1,0:T(8,128)(2,1)S(1)} %collective-permute-done.4.refs_0_, ...), custom_call_target="tpu_custom_call" | custom-call | flops 1073741824 | bytes 4194304 | tf_op jit(solution)/shard_map/pair_level/pallas_call | solution.py:556
  50.9 0.0 collective-permute-done.6.refs_0_
  50.9 0.9 %pair_level.6.sums_ref = f32[64,512]{1,0:T(8,128)S(1)} custom-call(f32[8,32,128]{2,1,0:T(8,128)S(1)} %get-tuple-element.32.mask_ref, f32[64,512]{1,0:T(8,128)S(1)} %pair_level.5.sums_ref, bf16[2,512,512]{2,1,0:T(8,128)(2,1)S(1)} %get-tuple-element.47.panel_ref, bf16[256,256]{1,0:T(8,128)(2,1)S(1)} %collective-permute-done.6.refs_0_), custom_call_target="tpu_custom_call" | custom-call | flops 268435456 | bytes 4194304 | tf_op jit(solution)/shard_map/pair_level/pallas_call | solution.py:556
  51.8 0.0 collective-permute-done.7.refs_0_
  51.8 0.0 collective-permute-done.8.refs_1_
  51.9 1.2 %pair_level.7 = (f32[16,512]{1,0:T(8,128)S(1)}, f32[16,512]{1,0:T(8,128)S(1)}, f32[16,512]{1,0:T(8,128)S(1)}, f32[16,512]{1,0:T(8,128)S(1)}) custom-call(f32[8,32,128]{2,1,0:T(8,128)S(1)} %get-tuple-element.32.mask_ref, f32[64,512]{1,0:T(8,128)S(1)} %pair_level.6.sums_ref, bf16[2,512,512]{2,1,0:T(8,128)(2,1)S(1)} %get-tuple-element.47.panel_ref, ...), custom_call_target="tpu_custom_call" | custom-call | flops 268435456 | bytes 4194304 | tf_op jit(solution)/shard_map/pair_level/pallas_call | solution.py:556
  53.1 1.5 %collective-permute-start.10 = (f32[16,512]{1,0:T(8,128)S(1)}, f32[16,512]{1,0:T(8,128)S(1)}, u32[]{:S(2)}, u32[]{:S(2)}) collective-permute-start(f32[16,512]{1,0:T(8,128)S(1)} %get-tuple-element.52), channel_id=1, source_target_pairs={{0,24},{8,16},{16,8},{24,0},{1,25},{9,17},{17,9},{25,1},{2,26},{10... | collective-permute-start | bytes 98312 | tf_op jit(solution)/shard_map/ppermute | solution.py:17
  54.6 1.0 %collective-permute-start.11 = (f32[16,512]{1,0:T(8,128)S(1)}, f32[16,512]{1,0:T(8,128)S(1)}, u32[]{:S(2)}, u32[]{:S(2)}) collective-permute-start(f32[16,512]{1,0:T(8,128)S(1)} %get-tuple-element.53), channel_id=1, source_target_pairs={{0,16},{8,24},{16,0},{24,8},{1,17},{9,25},{17,1},{25,9},{2,18},{10... | collective-permute-start | bytes 98312 | tf_op jit(solution)/shard_map/ppermute | solution.py:17
  55.6 0.2 collective-permute-start.9
  55.8 1.3 %collective-permute-done.10.refs_1_ = f32[16,512]{1,0:T(8,128)S(1)} collective-permute-done((f32[16,512]{1,0:T(8,128)S(1)}, f32[16,512]{1,0:T(8,128)S(1)}, u32[]{:S(2)}, u32[]{:S(2)}) %collective-permute-start.10) | collective-permute-done | bytes 32800 | tf_op jit(solution)/shard_map/ppermute | solution.py:17
  57.1 0.3 collective-permute-done.11.refs_2_
  57.4 0.9 %collective-permute-done.9.refs_0_ = f32[16,512]{1,0:T(8,128)S(1)} collective-permute-done((f32[16,512]{1,0:T(8,128)S(1)}, f32[16,512]{1,0:T(8,128)S(1)}, u32[]{:S(2)}, u32[]{:S(2)}) %collective-permute-start.9) | collective-permute-done | bytes 32800 | tf_op jit(solution)/shard_map/ppermute | solution.py:17
  58.3 0.7 %finish.1 = f32[8,2,2,511]{3,2,1,0:T(2,128)} custom-call(f32[16,512]{1,0:T(8,128)S(1)} %collective-permute-done.9.refs_0_, f32[16,512]{1,0:T(8,128)S(1)} %collective-permute-done.10.refs_1_, f32[16,512]{1,0:T(8,128)S(1)} %collective-permute-done.11.refs_2_, f32[16,512]{1,0:T(8,128)S(1)} %get-tuple-element.54.refs_3_), custom_call_target="tpu_custom_call" | custom-call | tf_op jit(solution)/shard_map/finish/pallas_call | solution.py:586
Async XLA Ops:
  1.0 13.8 %copy-start = (s32[2,256]{1,0:T(2,128)S(1)}, s32[2,256]{1,0:T(2,128)}, u32[]{:S(2)}) copy-start(s32[2,256]{1,0:T(2,128)} %position_ref.5) | copy-start | bytes 6148
  1.1 13.8 %copy-start.1 = (s32[2,3,2]{1,2,0:T(2,128)S(1)}, s32[2,3,2]{1,2,0:T(2,128)}, u32[]{:S(2)}) copy-start(s32[2,3,2]{1,2,0:T(2,128)} %param.5) | copy-start | bytes 148
  1.1 13.7 %collective-permute-start = (bf16[528,256]{1,0:T(8,128)(2,1)S(1)}, bf16[528,256]{1,0:T(8,128)(2,1)S(1)}, u32[]{:S(2)}, u32[]{:S(2)}) collective-permute-start(bf16[528,256]{1,0:T(8,128)(2,1)S(1)} %first_piece.1._), channel_id=1, source_target_pairs={{0,16},{8,24},{16,0},{24,8},{1,17},{9,25},{17,1},{25,9},{2,18},{10... | collective-permute-start | bytes 811016 | tf_op jit(solution)/shard_map/ppermute | solution.py:17
  3.2 11.6 %collective-permute-start.1 = (bf16[528,256]{1,0:T(8,128)(2,1)S(1)}, bf16[528,256]{1,0:T(8,128)(2,1)S(1)}, u32[]{:S(2)}, u32[]{:S(2)}) collective-permute-start(bf16[528,256]{1,0:T(8,128)(2,1)S(1)} %first_piece.1._), channel_id=1, source_target_pairs={{0,8},{8,0},{16,24},{24,16},{1,9},{9,1},{17,25},{25,17},{2,10},{10... | collective-permute-start | bytes 811016 | tf_op jit(solution)/shard_map/ppermute | solution.py:17
  14.4 22.9 %collective-permute-start.2 = (bf16[512,1024]{1,0:T(8,128)(2,1)S(1)}, bf16[512,1024]{1,0:T(8,128)(2,1)S(1)}, u32[]{:S(2)}, u32[]{:S(2)}) collective-permute-start(bf16[512,1024]{1,0:T(8,128)(2,1)S(1)} %get-tuple-element.38), channel_id=1, source_target_pairs={{0,8},{8,0},{16,24},{24,16},{1,9},{9,1},{17,25},{25,17},{2,10},{10... | collective-permute-start | bytes 3145736 | tf_op jit(solution)/shard_map/ppermute | solution.py:17
  14.7 23.9 %collective-permute-start.3 = (bf16[512,1024]{1,0:T(8,128)(2,1)S(1)}, bf16[512,1024]{1,0:T(8,128)(2,1)S(1)}, u32[]{:S(2)}, u32[]{:S(2)}) collective-permute-start(bf16[512,1024]{1,0:T(8,128)(2,1)S(1)} %get-tuple-element.38), channel_id=1, source_target_pairs={{0,16},{8,24},{16,0},{24,8},{1,17},{9,25},{17,1},{25,9},{2,18},{10... | collective-permute-start | bytes 3145736 | tf_op jit(solution)/shard_map/ppermute | solution.py:17
  23.0 25.8 %collective-permute-start.5 = (bf16[528,512]{1,0:T(8,128)(2,1)S(1)}, bf16[528,512]{1,0:T(8,128)(2,1)S(1)}, u32[]{:S(2)}, u32[]{:S(2)}) collective-permute-start(bf16[528,512]{1,0:T(8,128)(2,1)S(1)} %get-tuple-element.45), channel_id=1, source_target_pairs={{0,16},{8,24},{16,0},{24,8},{1,17},{9,25},{17,1},{25,9},{2,18},{10... | collective-permute-start | bytes 1622024 | tf_op jit(solution)/shard_map/ppermute | solution.py:17
  24.5 23.5 %collective-permute-start.4 = (bf16[512,512]{1,0:T(8,128)(2,1)S(1)}, bf16[512,512]{1,0:T(8,128)(2,1)S(1)}, u32[]{:S(2)}, u32[]{:S(2)}) collective-permute-start(bf16[512,512]{1,0:T(8,128)(2,1)S(1)} %get-tuple-element.44), channel_id=1, source_target_pairs={{0,8},{8,0},{16,24},{24,16},{1,9},{9,1},{17,25},{25,17},{2,10},{10... | collective-permute-start | bytes 1572872 | tf_op jit(solution)/shard_map/ppermute | solution.py:17
  42.5 9.3 %collective-permute-start.8 = (bf16[256,512]{1,0:T(8,128)(2,1)S(1)}, bf16[256,512]{1,0:T(8,128)(2,1)S(1)}, u32[]{:S(2)}, u32[]{:S(2)}) collective-permute-start(bf16[256,512]{1,0:T(8,128)(2,1)S(1)} %get-tuple-element.50), channel_id=1, source_target_pairs={{0,16},{8,24},{16,0},{24,8},{1,17},{9,25},{17,1},{25,9},{2,18},{10... | collective-permute-start | bytes 786440 | tf_op jit(solution)/shard_map/ppermute | solution.py:17
  42.6 8.4 %collective-permute-start.6 = (bf16[256,256]{1,0:T(8,128)(2,1)S(1)}, bf16[256,256]{1,0:T(8,128)(2,1)S(1)}, u32[]{:S(2)}, u32[]{:S(2)}) collective-permute-start(bf16[256,256]{1,0:T(8,128)(2,1)S(1)} %get-tuple-element.48), channel_id=1, source_target_pairs={{0,8},{8,0},{16,24},{24,16},{1,9},{9,1},{17,25},{25,17},{2,10},{10... | collective-permute-start | bytes 393224 | tf_op jit(solution)/shard_map/ppermute | solution.py:17
  44.0 7.8 %collective-permute-start.7 = (bf16[256,256]{1,0:T(8,128)(2,1)S(1)}, bf16[256,256]{1,0:T(8,128)(2,1)S(1)}, u32[]{:S(2)}, u32[]{:S(2)}) collective-permute-start(bf16[256,256]{1,0:T(8,128)(2,1)S(1)} %get-tuple-element.49), channel_id=1, source_target_pairs={{0,8},{8,0},{16,24},{24,16},{1,9},{9,1},{17,25},{25,17},{2,10},{10... | collective-permute-start | bytes 393224 | tf_op jit(solution)/shard_map/ppermute | solution.py:17
  53.1 4.0 %collective-permute-start.10 = (f32[16,512]{1,0:T(8,128)S(1)}, f32[16,512]{1,0:T(8,128)S(1)}, u32[]{:S(2)}, u32[]{:S(2)}) collective-permute-start(f32[16,512]{1,0:T(8,128)S(1)} %get-tuple-element.52), channel_id=1, source_target_pairs={{0,24},{8,16},{16,8},{24,0},{1,25},{9,17},{17,9},{25,1},{2,26},{10... | collective-permute-start | bytes 98312 | tf_op jit(solution)/shard_map/ppermute | solution.py:17
  54.6 2.8 %collective-permute-start.11 = (f32[16,512]{1,0:T(8,128)S(1)}, f32[16,512]{1,0:T(8,128)S(1)}, u32[]{:S(2)}, u32[]{:S(2)}) collective-permute-start(f32[16,512]{1,0:T(8,128)S(1)} %get-tuple-element.53), channel_id=1, source_target_pairs={{0,16},{8,24},{16,0},{24,8},{1,17},{9,25},{17,1},{25,9},{2,18},{10... | collective-permute-start | bytes 98312 | tf_op jit(solution)/shard_map/ppermute | solution.py:17
  55.6 2.8 %collective-permute-start.9 = (f32[16,512]{1,0:T(8,128)S(1)}, f32[16,512]{1,0:T(8,128)S(1)}, u32[]{:S(2)}, u32[]{:S(2)}) collective-permute-start(f32[16,512]{1,0:T(8,128)S(1)} %get-tuple-element.51), channel_id=1, source_target_pairs={{0,8},{8,0},{16,24},{24,16},{1,9},{9,1},{17,25},{25,17},{2,10},{10... | collective-permute-start | bytes 98312 | tf_op jit(solution)/shard_map/ppermute | solution.py:17
where the time goes:
time: 59.2 us; the launch traced here: 59 us
  Pallas kernels  28 us (47%)
  waiting for transfers between devices  20.1 us (34%)
  starting transfers between devices  10.7 us (18%)
    ppermute x12, waiting for transfers between devices, xor_permute(): lax.ppermute(x, axis, [(i, i ^ distance) for i in range(lax.axis_size(axi...  20.1 us
    ppermute x12, starting transfers between devices, xor_permute(): lax.ppermute(x, axis, [(i, i ^ distance) for i in range(lax.axis_size(axi...  10.7 us
    pallas_call x1, Pallas kernels, early_pieces(): pl.pallas_call(functools.partial(rest_kernel, levels, rest), out_shape=[p...  9.97 us
    pallas_call x1, Pallas kernels, own_level(): pl.pallas_call(functools.partial(own_kernel, levels, piece, last), out_sh...  8.18 us
    pallas_call x4, Pallas kernels, pair_call(): pl.pallas_call(kernel, out_shape=[jax.ShapeDtypeStruct((rows // shares, w...  8.15 us
  transfers between devices with their start and end apart: 12, of which 7 were waited for; matrix products, arithmetic and copies ran while one was open for 0% of the time, Pallas kernels for 42%

commit v1 on v0

--- a/solution.py
+++ b/solution.py
@@ -9,6 +9,7 @@
 
 RG_DEV = 8
 GROUP_ROWS = 16
+EARLY_TILES = 3
 HBM = pl.BlockSpec(memory_space=pltpu.HBM)
 WHOLE = pl.BlockSpec(memory_space=pltpu.VMEM)
 
@@ -291,13 +292,17 @@
     return loads
 
 
-def own_tiles(loads, position_ref, raw, panel, lags_ref, start):
-    blocks, _, width, samples = raw.shape
+def order_channel(loads, position_ref, raw, panel):
+    blocks = raw.shape[0]
     orders = [order_matrix(position_ref[b : b + 1, :]) for b in range(blocks)]
     for b, c, load in loads:
         load.wait()
         rows = jnp.dot(orders[b], raw[b, c], preferred_element_type=jnp.float32)
         panel[b, c] = rows.astype(jnp.bfloat16)
+
+
+def own_tiles(panel, lags_ref, start, first, last):
+    blocks, _, width, samples = panel.shape
 
     def one_tile(index, carry):
         a = index // blocks
@@ -307,7 +312,7 @@
         lags_ref[start + index] = jnp.where(jnp.logical_and(center, a == b), 0.0, lags)
         return carry
 
-    lax.fori_loop(0, blocks * blocks, one_tile, 0)
+    lax.fori_loop(first, last, one_tile, 0)
 
 
 def rest_kernel(levels, piece, position_ref, volts_ref, _, out_ref, panel_ref, lags_ref, *scratch):
@@ -320,7 +325,8 @@
     @pl.when(on_odd_core())
     def _():
         loads = load_channel(mine, volts_ref, raw, in_sem)
-        own_tiles(loads, position, raw, panel_ref, lags_ref, 0)
+        order_channel(loads, position, raw, panel_ref)
+        own_tiles(panel_ref, lags_ref, 0, 0, EARLY_TILES)
 
     loads = load_piece(piece, 1 - mine, position.shape[1], volts_ref, raw, in_sem)
     order_piece(piece, loads, position, raw, out_ref)
@@ -387,18 +393,21 @@
     @pl.when(jnp.logical_not(on_odd_core()))
     def _():
         loads = load_channel(mine, volts_ref, raw, in_sem)
-        own_tiles(loads, position_ref, raw, panel_ref, lags_ref, 0)
+        order_channel(loads, position_ref, raw, panel_ref)
+        own_tiles(panel_ref, lags_ref, 0, 0, EARLY_TILES)
 
     @pl.when(on_odd_core())
     def _():
         for b in range(blocks):
             for c in range(2):
                 panel_ref[b, c] = early_panel_ref[b, c]
-        for i in range(blocks * blocks):
+        for i in range(EARLY_TILES):
             lags_ref[i] = early_lags_ref[i]
 
-    own_tiles(other_loads, position_ref, other_raw, other_panel, lags_ref, blocks * blocks)
     tiles = blocks * blocks
+    own_tiles(panel_ref, lags_ref, 0, EARLY_TILES, tiles)
+    order_channel(other_loads, position_ref, other_raw, other_panel)
+    own_tiles(other_panel, lags_ref, tiles, 0, tiles)
     lags = jnp.concatenate([lags_ref[i] for i in range(tiles)], axis=0)
     heads = [head_ref[2 * width :, :] for head_ref in head_refs]
     for head, head_ref, ordered_ref in zip(heads, head_refs, ordered_refs):

time: 59.2 us -> 59.2 us (level)
  Pallas kernels: 28 us -> 27.3 us
  waiting for transfers between devices: 20.1 us -> 20.8 us
    pallas_call x1, Pallas kernels: 9.97 us -> 8.73 us  [early_pieces(): pl.pallas_call(functools.partial(rest_kernel, levels, rest), out_shape=[p...]
    ppermute x12, waiting for transfers between devices: 20.1 us -> 20.8 us  [xor_permute(): lax.ppermute(x, axis, [(i, i ^ distance) for i in range(lax.axis_size(axi...]
  transfers between devices with their start and end apart: 12 -> 12, of which waited for: 7 -> 7; matrix products, arithmetic and copies ran while one was open for 0% -> 0% of each run, Pallas kernels for 42% -> 41%
where the time goes in v1:
time: 59.2 us; the launch traced here: 59 us
  Pallas kernels  27.3 us (46%)
  waiting for transfers between devices  20.8 us (35%)
  starting transfers between devices  10.7 us (18%)
    ppermute x12, waiting for transfers between devices, xor_permute(): lax.ppermute(x, axis, [(i, i ^ distance) for i in range(lax.axis_size(axi...  20.8 us
    ppermute x12, starting transfers between devices, xor_permute(): lax.ppermute(x, axis, [(i, i ^ distance) for i in range(lax.axis_size(axi...  10.7 us
    pallas_call x1, Pallas kernels, own_level(): pl.pallas_call(functools.partial(own_kernel, levels, piece, last), out_sh...  8.75 us
    pallas_call x1, Pallas kernels, early_pieces(): pl.pallas_call(functools.partial(rest_kernel, levels, rest), out_shape=[p...  8.73 us
    pallas_call x4, Pallas kernels, pair_call(): pl.pallas_call(kernel, out_shape=[jax.ShapeDtypeStruct((rows // shares, w...  8.15 us
  transfers between devices with their start and end apart: 12, of which 7 were waited for; matrix products, arithmetic and copies ran while one was open for 0% of the time, Pallas kernels for 41%

profile of v1, /device:TPU:1, one launch (start us, length us, event | category | flops | bytes accessed | tf_op | source)
XLA Modules:
  0.0 59.0 jit_solution(8396273451220106356)
XLA Ops:
  0.0 1.0 %first_piece.1._ = bf16[528,256]{1,0:T(8,128)(2,1)S(1)} custom-call(s32[2,256]{1,0:T(2,128)} %position_ref.5, bf16[2,2,512,1024]{3,2,1,0:T(8,128)(2,1)} %volts_ref.5, s32[2,2,3]{2,1,0:T(2,128)} %bitcast.1), custom_call_target="tpu_custom_call" | custom-call | bytes 1048576 | tf_op jit(solution)/shard_map/first_piece/pallas_call | solution.py:342
  1.0 0.0 copy-start
  1.1 0.0 copy-start.1
  1.1 2.1 %collective-permute-start = (bf16[528,256]{1,0:T(8,128)(2,1)S(1)}, bf16[528,256]{1,0:T(8,128)(2,1)S(1)}, u32[]{:S(2)}, u32[]{:S(2)}) collective-permute-start(bf16[528,256]{1,0:T(8,128)(2,1)S(1)} %first_piece.1._), channel_id=1, source_target_pairs={{0,16},{8,24},{16,0},{24,8},{1,17},{9,25},{17,1},{25,9},{2,18},{10... | collective-permute-start | bytes 811016 | tf_op jit(solution)/shard_map/ppermute | solution.py:18
  3.2 1.2 %collective-permute-start.1 = (bf16[528,256]{1,0:T(8,128)(2,1)S(1)}, bf16[528,256]{1,0:T(8,128)(2,1)S(1)}, u32[]{:S(2)}, u32[]{:S(2)}) collective-permute-start(bf16[528,256]{1,0:T(8,128)(2,1)S(1)} %first_piece.1._), channel_id=1, source_target_pairs={{0,8},{8,0},{16,24},{24,16},{1,9},{9,1},{17,25},{25,17},{2,10},{10... | collective-permute-start | bytes 811016 | tf_op jit(solution)/shard_map/ppermute | solution.py:18
  4.4 8.7 %second_piece.1 = (bf16[512,1024]{1,0:T(8,128)(2,1)S(1)}, bf16[2,2,256,1024]{3,2,1,0:T(8,128)(2,1)S(1)}, f32[4,2,512]{2,1,0:T(2,128)S(1)}) custom-call(s32[2,256]{1,0:T(2,128)} %position_ref.5, bf16[2,2,512,1024]{3,2,1,0:T(8,128)(2,1)} %volts_ref.5, bf16[528,256]{1,0:T(8,128)(2,1)S(1)} %first_piece.1._), custom_call_target="tpu_custom_call" | custom-call | flops 268435456 | bytes 4194304 | tf_op jit(solution)/shard_map/second_piece/pallas_call | solution.py:357
  13.2 0.3 collective-permute-start.2
  13.5 0.1 collective-permute-start.3
  13.6 0.0 collective-permute-done.refs_0_
  13.6 0.0 collective-permute-done.1.refs_1_
  13.6 0.0 copy-done
  13.6 0.0 copy-done.1
  13.6 8.8 %own_level.1 = (bf16[2,2,256,1024]{3,2,1,0:T(8,128)(2,1)S(1)}, f32[64,512]{1,0:T(8,128)S(1)}, bf16[64,24]{1,0:T(8,128)(2,1)S(1)}, bf16[64,96]{1,0:T(8,128)(2,1)S...) custom-call(s32[2,2,3]{2,1,0:T(2,128)S(1)} %bitcast.2, ...), custom_call_target="tpu_custom_call" | custom-call | flops 17179869184 | bytes 6291456 | tf_op jit(solution)/shard_map/own_level/pallas_call | solution.py:465
  22.3 1.5 %collective-permute-start.5 = (bf16[528,512]{1,0:T(8,128)(2,1)S(1)}, bf16[528,512]{1,0:T(8,128)(2,1)S(1)}, u32[]{:S(2)}, u32[]{:S(2)}) collective-permute-start(bf16[528,512]{1,0:T(8,128)(2,1)S(1)} %get-tuple-element.45), channel_id=1, source_target_pairs={{0,16},{8,24},{16,0},{24,8},{1,17},{9,25},{17,1},{25,9},{2,18},{10... | collective-permute-start | bytes 1622024 | tf_op jit(solution)/shard_map/ppermute | solution.py:18
  23.8 1.2 %collective-permute-start.4 = (bf16[512,512]{1,0:T(8,128)(2,1)S(1)}, bf16[512,512]{1,0:T(8,128)(2,1)S(1)}, u32[]{:S(2)}, u32[]{:S(2)}) collective-permute-start(bf16[512,512]{1,0:T(8,128)(2,1)S(1)} %get-tuple-element.44), channel_id=1, source_target_pairs={{0,8},{8,0},{16,24},{24,16},{1,9},{9,1},{17,25},{25,17},{2,10},{10... | collective-permute-start | bytes 1572872 | tf_op jit(solution)/shard_map/ppermute | solution.py:18
  25.0 12.4 %collective-permute-done.2.refs_1_ = bf16[512,1024]{1,0:T(8,128)(2,1)S(1)} collective-permute-done((bf16[512,1024]{1,0:T(8,128)(2,1)S(1)}, bf16[512,1024]{1,0:T(8,128)(2,1)S(1)}, u32[]{:S(2)}, u32[]{:S(2)}) %collective-permute-start.2) | collective-permute-done | bytes 1048608 | tf_op jit(solution)/shard_map/ppermute | solution.py:18
  37.4 1.3 %collective-permute-done.3.refs_3_ = bf16[512,1024]{1,0:T(8,128)(2,1)S(1)} collective-permute-done((bf16[512,1024]{1,0:T(8,128)(2,1)S(1)}, bf16[512,1024]{1,0:T(8,128)(2,1)S(1)}, u32[]{:S(2)}, u32[]{:S(2)}) %collective-permute-start.3) | collective-permute-done | bytes 1048608 | tf_op jit(solution)/shard_map/ppermute | solution.py:18
  38.7 3.9 %pair_level.4 = (f32[64,512]{1,0:T(8,128)S(1)}, bf16[256,256]{1,0:T(8,128)(2,1)S(1)}, bf16[256,256]{1,0:T(8,128)(2,1)S(1)}, bf16[256,512]{1,0:T(8,128)(2,1)S(1)}) custom-call(bf16[64,96]{1,0:T(8,128)(2,1)S(1)} %get-tuple-element.34.pick_ref, f32[64,512]{1,0:T(8,128)S(1)} %get-tuple-element.35.sums_ref, ...), custom_call_target="tpu_custom_call", output_to_operand_aliasing={{1}: (7, {}), {2}: (8, {}), {3}: (9, {})} | custom-call | flops 2684354560 | bytes 4194304 | tf_op jit(solution)/shard_map/pair_level/pallas_call | solution.py:565
  42.6 0.1 collective-permute-start.8
  42.7 1.4 %collective-permute-start.6 = (bf16[256,256]{1,0:T(8,128)(2,1)S(1)}, bf16[256,256]{1,0:T(8,128)(2,1)S(1)}, u32[]{:S(2)}, u32[]{:S(2)}) collective-permute-start(bf16[256,256]{1,0:T(8,128)(2,1)S(1)} %get-tuple-element.48), channel_id=1, source_target_pairs={{0,8},{8,0},{16,24},{24,16},{1,9},{9,1},{17,25},{25,17},{2,10},{10... | collective-permute-start | bytes 393224 | tf_op jit(solution)/shard_map/ppermute | solution.py:18
  44.1 0.1 collective-permute-start.7
  44.2 3.7 %collective-permute-done.4.refs_0_ = bf16[512,512]{1,0:T(8,128)(2,1)S(1)} collective-permute-done((bf16[512,512]{1,0:T(8,128)(2,1)S(1)}, bf16[512,512]{1,0:T(8,128)(2,1)S(1)}, u32[]{:S(2)}, u32[]{:S(2)}) %collective-permute-start.4) | collective-permute-done | bytes 524320 | tf_op jit(solution)/shard_map/ppermute | solution.py:18
  47.9 0.8 %collective-permute-done.5.refs_1_ = bf16[528,512]{1,0:T(8,128)(2,1)S(1)} collective-permute-done((bf16[528,512]{1,0:T(8,128)(2,1)S(1)}, bf16[528,512]{1,0:T(8,128)(2,1)S(1)}, u32[]{:S(2)}, u32[]{:S(2)}) %collective-permute-start.5) | collective-permute-done | bytes 540704 | tf_op jit(solution)/shard_map/ppermute | solution.py:18
  48.8 2.2 %pair_level.5.sums_ref = f32[64,512]{1,0:T(8,128)S(1)} custom-call(bf16[64,48]{1,0:T(8,128)(2,1)S(1)} %get-tuple-element.33.pick_ref, f32[64,512]{1,0:T(8,128)S(1)} %get-tuple-element.43.sums_ref, bf16[2,2,256,1024]{3,2,1,0:T(8,128)(2,1)S(1)} %get-tuple-element.36.panel_ref, bf16[512,512]{1,0:T(8,128)(2,1)S(1)} %collective-permute-done.4.refs_0_, ...), custom_call_target="tpu_custom_call" | custom-call | flops 1073741824 | bytes 4194304 | tf_op jit(solution)/shard_map/pair_level/pallas_call | solution.py:565
  50.9 0.0 collective-permute-done.6.refs_0_
  50.9 0.9 %pair_level.6.sums_ref = f32[64,512]{1,0:T(8,128)S(1)} custom-call(f32[8,32,128]{2,1,0:T(8,128)S(1)} %get-tuple-element.32.mask_ref, f32[64,512]{1,0:T(8,128)S(1)} %pair_level.5.sums_ref, bf16[2,512,512]{2,1,0:T(8,128)(2,1)S(1)} %get-tuple-element.47.panel_ref, bf16[256,256]{1,0:T(8,128)(2,1)S(1)} %collective-permute-done.6.refs_0_), custom_call_target="tpu_custom_call" | custom-call | flops 268435456 | bytes 4194304 | tf_op jit(solution)/shard_map/pair_level/pallas_call | solution.py:565
  51.8 0.0 collective-permute-done.7.refs_0_
  51.8 0.0 collective-permute-done.8.refs_1_
  51.9 1.2 %pair_level.7 = (f32[16,512]{1,0:T(8,128)S(1)}, f32[16,512]{1,0:T(8,128)S(1)}, f32[16,512]{1,0:T(8,128)S(1)}, f32[16,512]{1,0:T(8,128)S(1)}) custom-call(f32[8,32,128]{2,1,0:T(8,128)S(1)} %get-tuple-element.32.mask_ref, f32[64,512]{1,0:T(8,128)S(1)} %pair_level.6.sums_ref, bf16[2,512,512]{2,1,0:T(8,128)(2,1)S(1)} %get-tuple-element.47.panel_ref, ...), custom_call_target="tpu_custom_call" | custom-call | flops 268435456 | bytes 4194304 | tf_op jit(solution)/shard_map/pair_level/pallas_call | solution.py:565
  53.1 1.4 %collective-permute-start.10 = (f32[16,512]{1,0:T(8,128)S(1)}, f32[16,512]{1,0:T(8,128)S(1)}, u32[]{:S(2)}, u32[]{:S(2)}) collective-permute-start(f32[16,512]{1,0:T(8,128)S(1)} %get-tuple-element.52), channel_id=1, source_target_pairs={{0,24},{8,16},{16,8},{24,0},{1,25},{9,17},{17,9},{25,1},{2,26},{10... | collective-permute-start | bytes 98312 | tf_op jit(solution)/shard_map/ppermute | solution.py:18
  54.5 1.0 %collective-permute-start.11 = (f32[16,512]{1,0:T(8,128)S(1)}, f32[16,512]{1,0:T(8,128)S(1)}, u32[]{:S(2)}, u32[]{:S(2)}) collective-permute-start(f32[16,512]{1,0:T(8,128)S(1)} %get-tuple-element.53), channel_id=1, source_target_pairs={{0,16},{8,24},{16,0},{24,8},{1,17},{9,25},{17,1},{25,9},{2,18},{10... | collective-permute-start | bytes 98312 | tf_op jit(solution)/shard_map/ppermute | solution.py:18
  55.6 0.2 collective-permute-start.9
  55.8 1.4 %collective-permute-done.10.refs_1_ = f32[16,512]{1,0:T(8,128)S(1)} collective-permute-done((f32[16,512]{1,0:T(8,128)S(1)}, f32[16,512]{1,0:T(8,128)S(1)}, u32[]{:S(2)}, u32[]{:S(2)}) %collective-permute-start.10) | collective-permute-done | bytes 32800 | tf_op jit(solution)/shard_map/ppermute | solution.py:18
  57.3 0.2 collective-permute-done.11.refs_2_
  57.4 0.9 %collective-permute-done.9.refs_0_ = f32[16,512]{1,0:T(8,128)S(1)} collective-permute-done((f32[16,512]{1,0:T(8,128)S(1)}, f32[16,512]{1,0:T(8,128)S(1)}, u32[]{:S(2)}, u32[]{:S(2)}) %collective-permute-start.9) | collective-permute-done | bytes 32800 | tf_op jit(solution)/shard_map/ppermute | solution.py:18
  58.3 0.7 %finish.1 = f32[8,2,2,511]{3,2,1,0:T(2,128)} custom-call(f32[16,512]{1,0:T(8,128)S(1)} %collective-permute-done.9.refs_0_, f32[16,512]{1,0:T(8,128)S(1)} %collective-permute-done.10.refs_1_, f32[16,512]{1,0:T(8,128)S(1)} %collective-permute-done.11.refs_2_, f32[16,512]{1,0:T(8,128)S(1)} %get-tuple-element.54.refs_3_), custom_call_target="tpu_custom_call" | custom-call | tf_op jit(solution)/shard_map/finish/pallas_call | solution.py:595
Async XLA Ops:
  1.0 12.5 %copy-start = (s32[2,256]{1,0:T(2,128)S(1)}, s32[2,256]{1,0:T(2,128)}, u32[]{:S(2)}) copy-start(s32[2,256]{1,0:T(2,128)} %position_ref.5) | copy-start | bytes 6148
  1.1 12.5 %copy-start.1 = (s32[2,3,2]{1,2,0:T(2,128)S(1)}, s32[2,3,2]{1,2,0:T(2,128)}, u32[]{:S(2)}) copy-start(s32[2,3,2]{1,2,0:T(2,128)} %param.5) | copy-start | bytes 148
  1.1 12.5 %collective-permute-start = (bf16[528,256]{1,0:T(8,128)(2,1)S(1)}, bf16[528,256]{1,0:T(8,128)(2,1)S(1)}, u32[]{:S(2)}, u32[]{:S(2)}) collective-permute-start(bf16[528,256]{1,0:T(8,128)(2,1)S(1)} %first_piece.1._), channel_id=1, source_target_pairs={{0,16},{8,24},{16,0},{24,8},{1,17},{9,25},{17,1},{25,9},{2,18},{10... | collective-permute-start | bytes 811016 | tf_op jit(solution)/shard_map/ppermute | solution.py:18
  3.2 10.4 %collective-permute-start.1 = (bf16[528,256]{1,0:T(8,128)(2,1)S(1)}, bf16[528,256]{1,0:T(8,128)(2,1)S(1)}, u32[]{:S(2)}, u32[]{:S(2)}) collective-permute-start(bf16[528,256]{1,0:T(8,128)(2,1)S(1)} %first_piece.1._), channel_id=1, source_target_pairs={{0,8},{8,0},{16,24},{24,16},{1,9},{9,1},{17,25},{25,17},{2,10},{10... | collective-permute-start | bytes 811016 | tf_op jit(solution)/shard_map/ppermute | solution.py:18
  13.2 24.2 %collective-permute-start.2 = (bf16[512,1024]{1,0:T(8,128)(2,1)S(1)}, bf16[512,1024]{1,0:T(8,128)(2,1)S(1)}, u32[]{:S(2)}, u32[]{:S(2)}) collective-permute-start(bf16[512,1024]{1,0:T(8,128)(2,1)S(1)} %get-tuple-element.38), channel_id=1, source_target_pairs={{0,8},{8,0},{16,24},{24,16},{1,9},{9,1},{17,25},{25,17},{2,10},{10... | collective-permute-start | bytes 3145736 | tf_op jit(solution)/shard_map/ppermute | solution.py:18
  13.5 25.2 %collective-permute-start.3 = (bf16[512,1024]{1,0:T(8,128)(2,1)S(1)}, bf16[512,1024]{1,0:T(8,128)(2,1)S(1)}, u32[]{:S(2)}, u32[]{:S(2)}) collective-permute-start(bf16[512,1024]{1,0:T(8,128)(2,1)S(1)} %get-tuple-element.38), channel_id=1, source_target_pairs={{0,16},{8,24},{16,0},{24,8},{1,17},{9,25},{17,1},{25,9},{2,18},{10... | collective-permute-start | bytes 3145736 | tf_op jit(solution)/shard_map/ppermute | solution.py:18
  22.3 26.4 %collective-permute-start.5 = (bf16[528,512]{1,0:T(8,128)(2,1)S(1)}, bf16[528,512]{1,0:T(8,128)(2,1)S(1)}, u32[]{:S(2)}, u32[]{:S(2)}) collective-permute-start(bf16[528,512]{1,0:T(8,128)(2,1)S(1)} %get-tuple-element.45), channel_id=1, source_target_pairs={{0,16},{8,24},{16,0},{24,8},{1,17},{9,25},{17,1},{25,9},{2,18},{10... | collective-permute-start | bytes 1622024 | tf_op jit(solution)/shard_map/ppermute | solution.py:18
  23.8 24.1 %collective-permute-start.4 = (bf16[512,512]{1,0:T(8,128)(2,1)S(1)}, bf16[512,512]{1,0:T(8,128)(2,1)S(1)}, u32[]{:S(2)}, u32[]{:S(2)}) collective-permute-start(bf16[512,512]{1,0:T(8,128)(2,1)S(1)} %get-tuple-element.44), channel_id=1, source_target_pairs={{0,8},{8,0},{16,24},{24,16},{1,9},{9,1},{17,25},{25,17},{2,10},{10... | collective-permute-start | bytes 1572872 | tf_op jit(solution)/shard_map/ppermute | solution.py:18
  42.6 9.3 %collective-permute-start.8 = (bf16[256,512]{1,0:T(8,128)(2,1)S(1)}, bf16[256,512]{1,0:T(8,128)(2,1)S(1)}, u32[]{:S(2)}, u32[]{:S(2)}) collective-permute-start(bf16[256,512]{1,0:T(8,128)(2,1)S(1)} %get-tuple-element.50), channel_id=1, source_target_pairs={{0,16},{8,24},{16,0},{24,8},{1,17},{9,25},{17,1},{25,9},{2,18},{10... | collective-permute-start | bytes 786440 | tf_op jit(solution)/shard_map/ppermute | solution.py:18
  42.7 8.3 %collective-permute-start.6 = (bf16[256,256]{1,0:T(8,128)(2,1)S(1)}, bf16[256,256]{1,0:T(8,128)(2,1)S(1)}, u32[]{:S(2)}, u32[]{:S(2)}) collective-permute-start(bf16[256,256]{1,0:T(8,128)(2,1)S(1)} %get-tuple-element.48), channel_id=1, source_target_pairs={{0,8},{8,0},{16,24},{24,16},{1,9},{9,1},{17,25},{25,17},{2,10},{10... | collective-permute-start | bytes 393224 | tf_op jit(solution)/shard_map/ppermute | solution.py:18
  44.1 7.7 %collective-permute-start.7 = (bf16[256,256]{1,0:T(8,128)(2,1)S(1)}, bf16[256,256]{1,0:T(8,128)(2,1)S(1)}, u32[]{:S(2)}, u32[]{:S(2)}) collective-permute-start(bf16[256,256]{1,0:T(8,128)(2,1)S(1)} %get-tuple-element.49), channel_id=1, source_target_pairs={{0,8},{8,0},{16,24},{24,16},{1,9},{9,1},{17,25},{25,17},{2,10},{10... | collective-permute-start | bytes 393224 | tf_op jit(solution)/shard_map/ppermute | solution.py:18
  53.1 4.2 %collective-permute-start.10 = (f32[16,512]{1,0:T(8,128)S(1)}, f32[16,512]{1,0:T(8,128)S(1)}, u32[]{:S(2)}, u32[]{:S(2)}) collective-permute-start(f32[16,512]{1,0:T(8,128)S(1)} %get-tuple-element.52), channel_id=1, source_target_pairs={{0,24},{8,16},{16,8},{24,0},{1,25},{9,17},{17,9},{25,1},{2,26},{10... | collective-permute-start | bytes 98312 | tf_op jit(solution)/shard_map/ppermute | solution.py:18
  54.5 2.9 %collective-permute-start.11 = (f32[16,512]{1,0:T(8,128)S(1)}, f32[16,512]{1,0:T(8,128)S(1)}, u32[]{:S(2)}, u32[]{:S(2)}) collective-permute-start(f32[16,512]{1,0:T(8,128)S(1)} %get-tuple-element.53), channel_id=1, source_target_pairs={{0,16},{8,24},{16,0},{24,8},{1,17},{9,25},{17,1},{25,9},{2,18},{10... | collective-permute-start | bytes 98312 | tf_op jit(solution)/shard_map/ppermute | solution.py:18
  55.6 2.8 %collective-permute-start.9 = (f32[16,512]{1,0:T(8,128)S(1)}, f32[16,512]{1,0:T(8,128)S(1)}, u32[]{:S(2)}, u32[]{:S(2)}) collective-permute-start(f32[16,512]{1,0:T(8,128)S(1)} %get-tuple-element.51), channel_id=1, source_target_pairs={{0,8},{8,0},{16,24},{24,16},{1,9},{9,1},{17,25},{25,17},{2,10},{10... | collective-permute-start | bytes 98312 | tf_op jit(solution)/shard_map/ppermute | solution.py:18

commit v2 on v1

--- a/solution.py
+++ b/solution.py
@@ -9,7 +9,7 @@
 
 RG_DEV = 8
 GROUP_ROWS = 16
-EARLY_TILES = 3
+EARLY_TILES = 2
 HBM = pl.BlockSpec(memory_space=pltpu.HBM)
 WHOLE = pl.BlockSpec(memory_space=pltpu.VMEM)
 

time: 59.2 us -> 59.5 us (level)
    pallas_call x1, Pallas kernels: 8.75 us -> 10.1 us  [own_level(): pl.pallas_call(functools.partial(own_kernel, levels, piece, last), out_sh...]
    pallas_call x1, Pallas kernels: 8.73 us -> 7.5 us  [early_pieces(): pl.pallas_call(functools.partial(rest_kernel, levels, rest), out_shape=[p...]
where the time goes in v2:
time: 59.5 us; the launch traced here: 59.3 us
  Pallas kernels  27.4 us (46%)
  waiting for transfers between devices  21 us (35%)
  starting transfers between devices  10.7 us (18%)
    ppermute x12, waiting for transfers between devices, xor_permute(): lax.ppermute(x, axis, [(i, i ^ distance) for i in range(lax.axis_size(axi...  21 us
    ppermute x12, starting transfers between devices, xor_permute(): lax.ppermute(x, axis, [(i, i ^ distance) for i in range(lax.axis_size(axi...  10.7 us
    pallas_call x1, Pallas kernels, own_level(): pl.pallas_call(functools.partial(own_kernel, levels, piece, last), out_sh...  10.1 us
    pallas_call x4, Pallas kernels, pair_call(): pl.pallas_call(kernel, out_shape=[jax.ShapeDtypeStruct((rows // shares, w...  8.15 us
    pallas_call x1, Pallas kernels, early_pieces(): pl.pallas_call(functools.partial(rest_kernel, levels, rest), out_shape=[p...  7.5 us
  transfers between devices with their start and end apart: 12, of which 7 were waited for; matrix products, arithmetic and copies ran while one was open for 0% of the time, Pallas kernels for 41%

profile of v2, /device:TPU:1, one launch (start us, length us, event | category | flops | bytes accessed | tf_op | source)
XLA Modules:
  0.0 59.3 jit_solution(9782738121423949695)
XLA Ops:
  0.0 1.0 %first_piece.1._ = bf16[528,256]{1,0:T(8,128)(2,1)S(1)} custom-call(s32[2,256]{1,0:T(2,128)} %position_ref.5, bf16[2,2,512,1024]{3,2,1,0:T(8,128)(2,1)} %volts_ref.5, s32[2,2,3]{2,1,0:T(2,128)} %bitcast.1), custom_call_target="tpu_custom_call" | custom-call | bytes 1048576 | tf_op jit(solution)/shard_map/first_piece/pallas_call | solution.py:342
  1.0 0.0 copy-start
  1.1 0.0 copy-start.1
  1.1 2.1 %collective-permute-start = (bf16[528,256]{1,0:T(8,128)(2,1)S(1)}, bf16[528,256]{1,0:T(8,128)(2,1)S(1)}, u32[]{:S(2)}, u32[]{:S(2)}) collective-permute-start(bf16[528,256]{1,0:T(8,128)(2,1)S(1)} %first_piece.1._), channel_id=1, source_target_pairs={{0,16},{8,24},{16,0},{24,8},{1,17},{9,25},{17,1},{25,9},{2,18},{10... | collective-permute-start | bytes 811016 | tf_op jit(solution)/shard_map/ppermute | solution.py:18
  3.2 1.2 %collective-permute-start.1 = (bf16[528,256]{1,0:T(8,128)(2,1)S(1)}, bf16[528,256]{1,0:T(8,128)(2,1)S(1)}, u32[]{:S(2)}, u32[]{:S(2)}) collective-permute-start(bf16[528,256]{1,0:T(8,128)(2,1)S(1)} %first_piece.1._), channel_id=1, source_target_pairs={{0,8},{8,0},{16,24},{24,16},{1,9},{9,1},{17,25},{25,17},{2,10},{10... | collective-permute-start | bytes 811016 | tf_op jit(solution)/shard_map/ppermute | solution.py:18
  4.4 7.5 %second_piece.1 = (bf16[512,1024]{1,0:T(8,128)(2,1)S(1)}, bf16[2,2,256,1024]{3,2,1,0:T(8,128)(2,1)S(1)}, f32[4,2,512]{2,1,0:T(2,128)S(1)}) custom-call(s32[2,256]{1,0:T(2,128)} %position_ref.5, bf16[2,2,512,1024]{3,2,1,0:T(8,128)(2,1)} %volts_ref.5, bf16[528,256]{1,0:T(8,128)(2,1)S(1)} %first_piece.1._), custom_call_target="tpu_custom_call" | custom-call | flops 268435456 | bytes 4194304 | tf_op jit(solution)/shard_map/second_piece/pallas_call | solution.py:357
  11.9 0.3 collective-permute-start.2
  12.2 0.1 collective-permute-start.3
  12.3 0.0 collective-permute-done.refs_0_
  12.3 0.0 collective-permute-done.1.refs_1_
  12.3 0.0 copy-done
  12.3 0.0 copy-done.1
  12.3 10.1 %own_level.1 = (bf16[2,2,256,1024]{3,2,1,0:T(8,128)(2,1)S(1)}, f32[64,512]{1,0:T(8,128)S(1)}, bf16[64,24]{1,0:T(8,128)(2,1)S(1)}, bf16[64,96]{1,0:T(8,128)(2,1)S...) custom-call(s32[2,2,3]{2,1,0:T(2,128)S(1)} %bitcast.2, ...), custom_call_target="tpu_custom_call" | custom-call | flops 17179869184 | bytes 6291456 | tf_op jit(solution)/shard_map/own_level/pallas_call | solution.py:465
  22.4 1.5 %collective-permute-start.5 = (bf16[528,512]{1,0:T(8,128)(2,1)S(1)}, bf16[528,512]{1,0:T(8,128)(2,1)S(1)}, u32[]{:S(2)}, u32[]{:S(2)}) collective-permute-start(bf16[528,512]{1,0:T(8,128)(2,1)S(1)} %get-tuple-element.45), channel_id=1, source_target_pairs={{0,16},{8,24},{16,0},{24,8},{1,17},{9,25},{17,1},{25,9},{2,18},{10... | collective-permute-start | bytes 1622024 | tf_op jit(solution)/shard_map/ppermute | solution.py:18
  23.9 1.2 %collective-permute-start.4 = (bf16[512,512]{1,0:T(8,128)(2,1)S(1)}, bf16[512,512]{1,0:T(8,128)(2,1)S(1)}, u32[]{:S(2)}, u32[]{:S(2)}) collective-permute-start(bf16[512,512]{1,0:T(8,128)(2,1)S(1)} %get-tuple-element.44), channel_id=1, source_target_pairs={{0,8},{8,0},{16,24},{24,16},{1,9},{9,1},{17,25},{25,17},{2,10},{10... | collective-permute-start | bytes 1572872 | tf_op jit(solution)/shard_map/ppermute | solution.py:18
  25.1 12.1 %collective-permute-done.2.refs_1_ = bf16[512,1024]{1,0:T(8,128)(2,1)S(1)} collective-permute-done((bf16[512,1024]{1,0:T(8,128)(2,1)S(1)}, bf16[512,1024]{1,0:T(8,128)(2,1)S(1)}, u32[]{:S(2)}, u32[]{:S(2)}) %collective-permute-start.2) | collective-permute-done | bytes 1048608 | tf_op jit(solution)/shard_map/ppermute | solution.py:18
  37.2 0.3 collective-permute-done.3.refs_3_
  37.5 3.9 %pair_level.4 = (f32[64,512]{1,0:T(8,128)S(1)}, bf16[256,256]{1,0:T(8,128)(2,1)S(1)}, bf16[256,256]{1,0:T(8,128)(2,1)S(1)}, bf16[256,512]{1,0:T(8,128)(2,1)S(1)}) custom-call(bf16[64,96]{1,0:T(8,128)(2,1)S(1)} %get-tuple-element.34.pick_ref, f32[64,512]{1,0:T(8,128)S(1)} %get-tuple-element.35.sums_ref, ...), custom_call_target="tpu_custom_call", output_to_operand_aliasing={{1}: (7, {}), {2}: (8, {}), {3}: (9, {})} | custom-call | flops 2684354560 | bytes 4194304 | tf_op jit(solution)/shard_map/pair_level/pallas_call | solution.py:565
  41.4 0.1 collective-permute-start.8
  41.5 1.4 %collective-permute-start.6 = (bf16[256,256]{1,0:T(8,128)(2,1)S(1)}, bf16[256,256]{1,0:T(8,128)(2,1)S(1)}, u32[]{:S(2)}, u32[]{:S(2)}) collective-permute-start(bf16[256,256]{1,0:T(8,128)(2,1)S(1)} %get-tuple-element.48), channel_id=1, source_target_pairs={{0,8},{8,0},{16,24},{24,16},{1,9},{9,1},{17,25},{25,17},{2,10},{10... | collective-permute-start | bytes 393224 | tf_op jit(solution)/shard_map/ppermute | solution.py:18
  42.9 0.1 collective-permute-start.7
  43.0 5.3 %collective-permute-done.4.refs_0_ = bf16[512,512]{1,0:T(8,128)(2,1)S(1)} collective-permute-done((bf16[512,512]{1,0:T(8,128)(2,1)S(1)}, bf16[512,512]{1,0:T(8,128)(2,1)S(1)}, u32[]{:S(2)}, u32[]{:S(2)}) %collective-permute-start.4) | collective-permute-done | bytes 524320 | tf_op jit(solution)/shard_map/ppermute | solution.py:18
  48.2 0.8 %collective-permute-done.5.refs_1_ = bf16[528,512]{1,0:T(8,128)(2,1)S(1)} collective-permute-done((bf16[528,512]{1,0:T(8,128)(2,1)S(1)}, bf16[528,512]{1,0:T(8,128)(2,1)S(1)}, u32[]{:S(2)}, u32[]{:S(2)}) %collective-permute-start.5) | collective-permute-done | bytes 540704 | tf_op jit(solution)/shard_map/ppermute | solution.py:18
  49.0 2.2 %pair_level.5.sums_ref = f32[64,512]{1,0:T(8,128)S(1)} custom-call(bf16[64,48]{1,0:T(8,128)(2,1)S(1)} %get-tuple-element.33.pick_ref, f32[64,512]{1,0:T(8,128)S(1)} %get-tuple-element.43.sums_ref, bf16[2,2,256,1024]{3,2,1,0:T(8,128)(2,1)S(1)} %get-tuple-element.36.panel_ref, bf16[512,512]{1,0:T(8,128)(2,1)S(1)} %collective-permute-done.4.refs_0_, ...), custom_call_target="tpu_custom_call" | custom-call | flops 1073741824 | bytes 4194304 | tf_op jit(solution)/shard_map/pair_level/pallas_call | solution.py:565
  51.2 0.0 collective-permute-done.6.refs_0_
  51.2 0.9 %pair_level.6.sums_ref = f32[64,512]{1,0:T(8,128)S(1)} custom-call(f32[8,32,128]{2,1,0:T(8,128)S(1)} %get-tuple-element.32.mask_ref, f32[64,512]{1,0:T(8,128)S(1)} %pair_level.5.sums_ref, bf16[2,512,512]{2,1,0:T(8,128)(2,1)S(1)} %get-tuple-element.47.panel_ref, bf16[256,256]{1,0:T(8,128)(2,1)S(1)} %collective-permute-done.6.refs_0_), custom_call_target="tpu_custom_call" | custom-call | flops 268435456 | bytes 4194304 | tf_op jit(solution)/shard_map/pair_level/pallas_call | solution.py:565
  52.1 0.0 collective-permute-done.7.refs_0_
  52.1 0.0 collective-permute-done.8.refs_1_
  52.1 1.2 %pair_level.7 = (f32[16,512]{1,0:T(8,128)S(1)}, f32[16,512]{1,0:T(8,128)S(1)}, f32[16,512]{1,0:T(8,128)S(1)}, f32[16,512]{1,0:T(8,128)S(1)}) custom-call(f32[8,32,128]{2,1,0:T(8,128)S(1)} %get-tuple-element.32.mask_ref, f32[64,512]{1,0:T(8,128)S(1)} %pair_level.6.sums_ref, bf16[2,512,512]{2,1,0:T(8,128)(2,1)S(1)} %get-tuple-element.47.panel_ref, ...), custom_call_target="tpu_custom_call" | custom-call | flops 268435456 | bytes 4194304 | tf_op jit(solution)/shard_map/pair_level/pallas_call | solution.py:565
  53.4 1.2 %collective-permute-start.10 = (f32[16,512]{1,0:T(8,128)S(1)}, f32[16,512]{1,0:T(8,128)S(1)}, u32[]{:S(2)}, u32[]{:S(2)}) collective-permute-start(f32[16,512]{1,0:T(8,128)S(1)} %get-tuple-element.52), channel_id=1, source_target_pairs={{0,24},{8,16},{16,8},{24,0},{1,25},{9,17},{17,9},{25,1},{2,26},{10... | collective-permute-start | bytes 98312 | tf_op jit(solution)/shard_map/ppermute | solution.py:18
  54.6 1.2 %collective-permute-start.11 = (f32[16,512]{1,0:T(8,128)S(1)}, f32[16,512]{1,0:T(8,128)S(1)}, u32[]{:S(2)}, u32[]{:S(2)}) collective-permute-start(f32[16,512]{1,0:T(8,128)S(1)} %get-tuple-element.53), channel_id=1, source_target_pairs={{0,16},{8,24},{16,0},{24,8},{1,17},{9,25},{17,1},{25,9},{2,18},{10... | collective-permute-start | bytes 98312 | tf_op jit(solution)/shard_map/ppermute | solution.py:18
  55.9 0.2 collective-permute-start.9
  56.1 1.3 %collective-permute-done.10.refs_1_ = f32[16,512]{1,0:T(8,128)S(1)} collective-permute-done((f32[16,512]{1,0:T(8,128)S(1)}, f32[16,512]{1,0:T(8,128)S(1)}, u32[]{:S(2)}, u32[]{:S(2)}) %collective-permute-start.10) | collective-permute-done | bytes 32800 | tf_op jit(solution)/shard_map/ppermute | solution.py:18
  57.4 0.2 collective-permute-done.11.refs_2_
  57.6 1.0 %collective-permute-done.9.refs_0_ = f32[16,512]{1,0:T(8,128)S(1)} collective-permute-done((f32[16,512]{1,0:T(8,128)S(1)}, f32[16,512]{1,0:T(8,128)S(1)}, u32[]{:S(2)}, u32[]{:S(2)}) %collective-permute-start.9) | collective-permute-done | bytes 32800 | tf_op jit(solution)/shard_map/ppermute | solution.py:18
  58.6 0.7 %finish.1 = f32[8,2,2,511]{3,2,1,0:T(2,128)} custom-call(f32[16,512]{1,0:T(8,128)S(1)} %collective-permute-done.9.refs_0_, f32[16,512]{1,0:T(8,128)S(1)} %collective-permute-done.10.refs_1_, f32[16,512]{1,0:T(8,128)S(1)} %collective-permute-done.11.refs_2_, f32[16,512]{1,0:T(8,128)S(1)} %get-tuple-element.54.refs_3_), custom_call_target="tpu_custom_call" | custom-call | tf_op jit(solution)/shard_map/finish/pallas_call | solution.py:595
Async XLA Ops:
  1.0 11.3 %copy-start = (s32[2,256]{1,0:T(2,128)S(1)}, s32[2,256]{1,0:T(2,128)}, u32[]{:S(2)}) copy-start(s32[2,256]{1,0:T(2,128)} %position_ref.5) | copy-start | bytes 6148
  1.1 11.3 %copy-start.1 = (s32[2,3,2]{1,2,0:T(2,128)S(1)}, s32[2,3,2]{1,2,0:T(2,128)}, u32[]{:S(2)}) copy-start(s32[2,3,2]{1,2,0:T(2,128)} %param.5) | copy-start | bytes 148
  1.1 11.3 %collective-permute-start = (bf16[528,256]{1,0:T(8,128)(2,1)S(1)}, bf16[528,256]{1,0:T(8,128)(2,1)S(1)}, u32[]{:S(2)}, u32[]{:S(2)}) collective-permute-start(bf16[528,256]{1,0:T(8,128)(2,1)S(1)} %first_piece.1._), channel_id=1, source_target_pairs={{0,16},{8,24},{16,0},{24,8},{1,17},{9,25},{17,1},{25,9},{2,18},{10... | collective-permute-start | bytes 811016 | tf_op jit(solution)/shard_map/ppermute | solution.py:18
  3.2 9.1 %collective-permute-start.1 = (bf16[528,256]{1,0:T(8,128)(2,1)S(1)}, bf16[528,256]{1,0:T(8,128)(2,1)S(1)}, u32[]{:S(2)}, u32[]{:S(2)}) collective-permute-start(bf16[528,256]{1,0:T(8,128)(2,1)S(1)} %first_piece.1._), channel_id=1, source_target_pairs={{0,8},{8,0},{16,24},{24,16},{1,9},{9,1},{17,25},{25,17},{2,10},{10... | collective-permute-start | bytes 811016 | tf_op jit(solution)/shard_map/ppermute | solution.py:18
  11.9 25.3 %collective-permute-start.2 = (bf16[512,1024]{1,0:T(8,128)(2,1)S(1)}, bf16[512,1024]{1,0:T(8,128)(2,1)S(1)}, u32[]{:S(2)}, u32[]{:S(2)}) collective-permute-start(bf16[512,1024]{1,0:T(8,128)(2,1)S(1)} %get-tuple-element.38), channel_id=1, source_target_pairs={{0,8},{8,0},{16,24},{24,16},{1,9},{9,1},{17,25},{25,17},{2,10},{10... | collective-permute-start | bytes 3145736 | tf_op jit(solution)/shard_map/ppermute | solution.py:18
  12.2 25.2 %collective-permute-start.3 = (bf16[512,1024]{1,0:T(8,128)(2,1)S(1)}, bf16[512,1024]{1,0:T(8,128)(2,1)S(1)}, u32[]{:S(2)}, u32[]{:S(2)}) collective-permute-start(bf16[512,1024]{1,0:T(8,128)(2,1)S(1)} %get-tuple-element.38), channel_id=1, source_target_pairs={{0,16},{8,24},{16,0},{24,8},{1,17},{9,25},{17,1},{25,9},{2,18},{10... | collective-permute-start | bytes 3145736 | tf_op jit(solution)/shard_map/ppermute | solution.py:18
  22.4 26.6 %collective-permute-start.5 = (bf16[528,512]{1,0:T(8,128)(2,1)S(1)}, bf16[528,512]{1,0:T(8,128)(2,1)S(1)}, u32[]{:S(2)}, u32[]{:S(2)}) collective-permute-start(bf16[528,512]{1,0:T(8,128)(2,1)S(1)} %get-tuple-element.45), channel_id=1, source_target_pairs={{0,16},{8,24},{16,0},{24,8},{1,17},{9,25},{17,1},{25,9},{2,18},{10... | collective-permute-start | bytes 1622024 | tf_op jit(solution)/shard_map/ppermute | solution.py:18
  23.9 24.3 %collective-permute-start.4 = (bf16[512,512]{1,0:T(8,128)(2,1)S(1)}, bf16[512,512]{1,0:T(8,128)(2,1)S(1)}, u32[]{:S(2)}, u32[]{:S(2)}) collective-permute-start(bf16[512,512]{1,0:T(8,128)(2,1)S(1)} %get-tuple-element.44), channel_id=1, source_target_pairs={{0,8},{8,0},{16,24},{24,16},{1,9},{9,1},{17,25},{25,17},{2,10},{10... | collective-permute-start | bytes 1572872 | tf_op jit(solution)/shard_map/ppermute | solution.py:18
  41.4 10.8 %collective-permute-start.8 = (bf16[256,512]{1,0:T(8,128)(2,1)S(1)}, bf16[256,512]{1,0:T(8,128)(2,1)S(1)}, u32[]{:S(2)}, u32[]{:S(2)}) collective-permute-start(bf16[256,512]{1,0:T(8,128)(2,1)S(1)} %get-tuple-element.50), channel_id=1, source_target_pairs={{0,16},{8,24},{16,0},{24,8},{1,17},{9,25},{17,1},{25,9},{2,18},{10... | collective-permute-start | bytes 786440 | tf_op jit(solution)/shard_map/ppermute | solution.py:18
  41.5 9.7 %collective-permute-start.6 = (bf16[256,256]{1,0:T(8,128)(2,1)S(1)}, bf16[256,256]{1,0:T(8,128)(2,1)S(1)}, u32[]{:S(2)}, u32[]{:S(2)}) collective-permute-start(bf16[256,256]{1,0:T(8,128)(2,1)S(1)} %get-tuple-element.48), channel_id=1, source_target_pairs={{0,8},{8,0},{16,24},{24,16},{1,9},{9,1},{17,25},{25,17},{2,10},{10... | collective-permute-start | bytes 393224 | tf_op jit(solution)/shard_map/ppermute | solution.py:18
  42.9 9.3 %collective-permute-start.7 = (bf16[256,256]{1,0:T(8,128)(2,1)S(1)}, bf16[256,256]{1,0:T(8,128)(2,1)S(1)}, u32[]{:S(2)}, u32[]{:S(2)}) collective-permute-start(bf16[256,256]{1,0:T(8,128)(2,1)S(1)} %get-tuple-element.49), channel_id=1, source_target_pairs={{0,8},{8,0},{16,24},{24,16},{1,9},{9,1},{17,25},{25,17},{2,10},{10... | collective-permute-start | bytes 393224 | tf_op jit(solution)/shard_map/ppermute | solution.py:18
  53.4 4.0 %collective-permute-start.10 = (f32[16,512]{1,0:T(8,128)S(1)}, f32[16,512]{1,0:T(8,128)S(1)}, u32[]{:S(2)}, u32[]{:S(2)}) collective-permute-start(f32[16,512]{1,0:T(8,128)S(1)} %get-tuple-element.52), channel_id=1, source_target_pairs={{0,24},{8,16},{16,8},{24,0},{1,25},{9,17},{17,9},{25,1},{2,26},{10... | collective-permute-start | bytes 98312 | tf_op jit(solution)/shard_map/ppermute | solution.py:18
  54.6 3.0 %collective-permute-start.11 = (f32[16,512]{1,0:T(8,128)S(1)}, f32[16,512]{1,0:T(8,128)S(1)}, u32[]{:S(2)}, u32[]{:S(2)}) collective-permute-start(f32[16,512]{1,0:T(8,128)S(1)} %get-tuple-element.53), channel_id=1, source_target_pairs={{0,16},{8,24},{16,0},{24,8},{1,17},{9,25},{17,1},{25,9},{2,18},{10... | collective-permute-start | bytes 98312 | tf_op jit(solution)/shard_map/ppermute | solution.py:18
  55.9 2.8 %collective-permute-start.9 = (f32[16,512]{1,0:T(8,128)S(1)}, f32[16,512]{1,0:T(8,128)S(1)}, u32[]{:S(2)}, u32[]{:S(2)}) collective-permute-start(f32[16,512]{1,0:T(8,128)S(1)} %get-tuple-element.51), channel_id=1, source_target_pairs={{0,8},{8,0},{16,24},{24,16},{1,9},{9,1},{17,25},{25,17},{2,10},{10... | collective-permute-start | bytes 98312 | tf_op jit(solution)/shard_map/ppermute | solution.py:18

commit v3 on v1

--- a/solution.py
+++ b/solution.py
@@ -192,7 +192,6 @@
         pick_matrix(tiles[0], out_rows),
         pick_matrix(tiles[1], out_rows),
         pick_matrix(both, out_rows),
-        pick_matrix(forward[-1] + turned[-1], out_rows),
         row_masks(forward[-1][::2] + turned[-1][::2], groups_all),
     ]
 
@@ -384,7 +383,7 @@
     head_refs, refs = refs[:levels][::-1], refs[levels:]
     early_panel_ref, early_lags_ref, *refs = refs
     panel_ref, sums_ref, *refs, raw, other_raw, other_panel, lags_ref, in_sem, other_sem = refs
-    pick_refs, ordered_refs, refs = refs[:4], refs[4 : 4 + levels], refs[4 + levels :]
+    pick_refs, ordered_refs, refs = refs[:3], refs[3 : 3 + levels], refs[3 + levels :]
     more_ref, piece_ref, *last_refs, joined_ref, last_panel_ref = refs
     blocks, _, width, _ = panel_ref.shape
     mine = parity(lax.axis_index("inp"), levels)
@@ -460,7 +459,7 @@
     samples = volts.shape[3]
     pairs = 4 * levels * blocks
     tiles = 2 * blocks * blocks
-    counts = (3 * tiles, 3 * pairs * blocks, 3 * pairs)
+    counts = (3 * tiles, 3 * pairs * blocks)
     depths = [2 * (end - first) for _, first, end in last]
     return pl.pallas_call(
         functools.partial(own_kernel, levels, piece, last),
@@ -502,6 +501,19 @@
     return sums_ref[...] + group_sums(pick_ref[...], lags)
 
 
+def add_masked(lags, tiles_at, mask_ref, sums_ref):
+    turned = reversed_lags(lags)
+    half, count = sums_ref.shape[0] // 2, mask_ref.shape[0] // 2
+    sums = [sums_ref[:half, :], sums_ref[half:, :]]
+    for i, tile in enumerate(tiles_at):
+        forward = jnp.concatenate([mask_ref[tile]] * (sums_ref.shape[1] // 128), axis=1)
+        back = jnp.concatenate([mask_ref[count + tile]] * (sums_ref.shape[1] // 128), axis=1)
+        re, im = 2 * i, 2 * i + 1
+        sums[0] = sums[0] + forward * lags[re : re + 1] + back * turned[re : re + 1]
+        sums[1] = sums[1] + forward * lags[im : im + 1] - back * turned[im : im + 1]
+    return sums
+
+
 def pair_kernel(levels, pieces, passed, pick_ref, sums_ref, panel_ref, *refs):
     count = levels * len(pieces)
     out_ref = refs[-1 - passed]
@@ -523,7 +535,11 @@
                         real_part = real_part + (product(x_re, y_re) + product(x_im, y_im))
                         imag_part = imag_part + (product(x_im, y_re) - product(x_re, y_im))
                 rows.append(lag_rows(jnp.stack([real_part, imag_part])) * (1.0 / samples))
-    sums = add_lags(rows, pick_ref, sums_ref)
+    if len(pick_ref.shape) == 3:
+        sums = add_masked(jnp.concatenate(rows, axis=0), range(len(rows)), pick_ref, sums_ref)
+        sums = jnp.concatenate(sums, axis=0)
+    else:
+        sums = add_lags(rows, pick_ref, sums_ref)
     for more_ref in more_refs:
         terms = partner_refs[-1][2 * width :, :].astype(jnp.float32)
         half = terms.shape[0] // 2
@@ -542,16 +558,8 @@
             rows += sheared_eights(tiles.reshape(2, width, width))
             tiles_at.append(level * blocks + a)
     lags = jnp.sum(jnp.stack(rows), axis=1) * (1.0 / samples)
-    turned = reversed_lags(lags)
+    sums = add_masked(lags, tiles_at, mask_ref, sums_ref)
     half = sums_ref.shape[0] // 2
-    sums = [sums_ref[:half, :], sums_ref[half:, :]]
-    count = mask_ref.shape[0] // 2
-    for i, tile in enumerate(tiles_at):
-        forward = jnp.concatenate([mask_ref[tile]] * (sums_ref.shape[1] // 128), axis=1)
-        back = jnp.concatenate([mask_ref[count + tile]] * (sums_ref.shape[1] // 128), axis=1)
-        re, im = 2 * i, 2 * i + 1
-        sums[0] = sums[0] + forward * lags[re : re + 1] + back * turned[re : re + 1]
-        sums[1] = sums[1] + forward * lags[im : im + 1] - back * turned[im : im + 1]
     share = half // len(out_refs)
     for place, out_ref in enumerate(out_refs):
         for part in range(2):
@@ -618,7 +626,7 @@
     sent, second, *early = early_pieces(position_input, volts, by_block, head, rest, levels)
     head_arrived = [send(sent) for send in partner_of]
     rest_arrived = [send(second) for send in partner_of]
-    panel, sums, neighbour, both, single, masks, *sent = own_level(
+    panel, sums, neighbour, both, masks, *sent = own_level(
         by_block, position_input, volts, early, head_arrived, tail, last, out_rows
     )
     head_ordered, (more, piece, *last_pieces, last_panel) = sent[:levels], sent[levels:]
@@ -637,7 +645,7 @@
     last_arrived[-1].append(partner_of[-1](joined))
     (sums,) = pair_call(
         functools.partial(pair_kernel, levels, [tail], 0),
-        [single, sums, panel, *tail_arrived, neighbour],
+        [masks, sums, panel, *tail_arrived, neighbour],
         flops * 4 * eighth,
     )
     for i, arrived in enumerate(last_arrived):

time: 59.2 us -> 59 us (level)
  no operation moved by 1% of the time
where the time goes in v3:
time: 59 us; the launch traced here: 58.8 us
  Pallas kernels  27.1 us (46%)
  waiting for transfers between devices  20.8 us (35%)
  starting transfers between devices  10.7 us (18%)
    ppermute x12, waiting for transfers between devices, xor_permute(): lax.ppermute(x, axis, [(i, i ^ distance) for i in range(lax.axis_size(axi...  20.8 us
    ppermute x12, starting transfers between devices, xor_permute(): lax.ppermute(x, axis, [(i, i ^ distance) for i in range(lax.axis_size(axi...  10.7 us
    pallas_call x1, Pallas kernels, own_level(): pl.pallas_call(functools.partial(own_kernel, levels, piece, last), out_sh...  8.74 us
    pallas_call x1, Pallas kernels, early_pieces(): pl.pallas_call(functools.partial(rest_kernel, levels, rest), out_shape=[p...  8.73 us
    pallas_call x4, Pallas kernels, pair_call(): pl.pallas_call(kernel, out_shape=[jax.ShapeDtypeStruct((rows // shares, w...  7.97 us
  transfers between devices with their start and end apart: 12, of which 7 were waited for; matrix products, arithmetic and copies ran while one was open for 0% of the time, Pallas kernels for 41%

profile of v3, /device:TPU:1, one launch (start us, length us, event | category | flops | bytes accessed | tf_op | source)
XLA Modules:
  0.0 58.8 jit_solution(1084793281691034197)
XLA Ops:
  0.0 1.0 %first_piece.1._ = bf16[528,256]{1,0:T(8,128)(2,1)S(1)} custom-call(s32[2,256]{1,0:T(2,128)} %position_ref.5, bf16[2,2,512,1024]{3,2,1,0:T(8,128)(2,1)} %volts_ref.5, s32[2,2,3]{2,1,0:T(2,128)} %bitcast.1), custom_call_target="tpu_custom_call" | custom-call | bytes 1048576 | tf_op jit(solution)/shard_map/first_piece/pallas_call | solution.py:341
  1.0 0.0 copy-start
  1.1 0.0 copy-start.1
  1.1 2.1 %collective-permute-start = (bf16[528,256]{1,0:T(8,128)(2,1)S(1)}, bf16[528,256]{1,0:T(8,128)(2,1)S(1)}, u32[]{:S(2)}, u32[]{:S(2)}) collective-permute-start(bf16[528,256]{1,0:T(8,128)(2,1)S(1)} %first_piece.1._), channel_id=1, source_target_pairs={{0,16},{8,24},{16,0},{24,8},{1,17},{9,25},{17,1},{25,9},{2,18},{10... | collective-permute-start | bytes 811016 | tf_op jit(solution)/shard_map/ppermute | solution.py:18
  3.2 1.2 %collective-permute-start.1 = (bf16[528,256]{1,0:T(8,128)(2,1)S(1)}, bf16[528,256]{1,0:T(8,128)(2,1)S(1)}, u32[]{:S(2)}, u32[]{:S(2)}) collective-permute-start(bf16[528,256]{1,0:T(8,128)(2,1)S(1)} %first_piece.1._), channel_id=1, source_target_pairs={{0,8},{8,0},{16,24},{24,16},{1,9},{9,1},{17,25},{25,17},{2,10},{10... | collective-permute-start | bytes 811016 | tf_op jit(solution)/shard_map/ppermute | solution.py:18
  4.4 8.7 %second_piece.1 = (bf16[512,1024]{1,0:T(8,128)(2,1)S(1)}, bf16[2,2,256,1024]{3,2,1,0:T(8,128)(2,1)S(1)}, f32[4,2,512]{2,1,0:T(2,128)S(1)}) custom-call(s32[2,256]{1,0:T(2,128)} %position_ref.5, bf16[2,2,512,1024]{3,2,1,0:T(8,128)(2,1)} %volts_ref.5, bf16[528,256]{1,0:T(8,128)(2,1)S(1)} %first_piece.1._), custom_call_target="tpu_custom_call" | custom-call | flops 268435456 | bytes 4194304 | tf_op jit(solution)/shard_map/second_piece/pallas_call | solution.py:356
  13.2 0.3 collective-permute-start.2
  13.5 0.1 collective-permute-start.3
  13.6 0.0 collective-permute-done.refs_0_
  13.6 0.0 collective-permute-done.1.refs_1_
  13.6 0.0 copy-done
  13.6 0.0 copy-done.1
  13.6 8.7 %own_level.1 = (bf16[2,2,256,1024]{3,2,1,0:T(8,128)(2,1)S(1)}, f32[64,512]{1,0:T(8,128)S(1)}, bf16[64,24]{1,0:T(8,128)(2,1)S(1)}, bf16[64,96]{1,0:T(8,128)(2,1)S...) custom-call(s32[2,2,3]{2,1,0:T(2,128)S(1)} %bitcast.2, ...), custom_call_target="tpu_custom_call" | custom-call | flops 17179869184 | bytes 6291456 | tf_op jit(solution)/shard_map/own_level/pallas_call | solution.py:464
  22.3 1.4 %collective-permute-start.5 = (bf16[528,512]{1,0:T(8,128)(2,1)S(1)}, bf16[528,512]{1,0:T(8,128)(2,1)S(1)}, u32[]{:S(2)}, u32[]{:S(2)}) collective-permute-start(bf16[528,512]{1,0:T(8,128)(2,1)S(1)} %get-tuple-element.43), channel_id=1, source_target_pairs={{0,16},{8,24},{16,0},{24,8},{1,17},{9,25},{17,1},{25,9},{2,18},{10... | collective-permute-start | bytes 1622024 | tf_op jit(solution)/shard_map/ppermute | solution.py:18
  23.8 1.2 %collective-permute-start.4 = (bf16[512,512]{1,0:T(8,128)(2,1)S(1)}, bf16[512,512]{1,0:T(8,128)(2,1)S(1)}, u32[]{:S(2)}, u32[]{:S(2)}) collective-permute-start(bf16[512,512]{1,0:T(8,128)(2,1)S(1)} %get-tuple-element.42), channel_id=1, source_target_pairs={{0,8},{8,0},{16,24},{24,16},{1,9},{9,1},{17,25},{25,17},{2,10},{10... | collective-permute-start | bytes 1572872 | tf_op jit(solution)/shard_map/ppermute | solution.py:18
  25.0 12.5 %collective-permute-done.2.refs_1_ = bf16[512,1024]{1,0:T(8,128)(2,1)S(1)} collective-permute-done((bf16[512,1024]{1,0:T(8,128)(2,1)S(1)}, bf16[512,1024]{1,0:T(8,128)(2,1)S(1)}, u32[]{:S(2)}, u32[]{:S(2)}) %collective-permute-start.2) | collective-permute-done | bytes 1048608 | tf_op jit(solution)/shard_map/ppermute | solution.py:18
  37.4 1.3 %collective-permute-done.3.refs_3_ = bf16[512,1024]{1,0:T(8,128)(2,1)S(1)} collective-permute-done((bf16[512,1024]{1,0:T(8,128)(2,1)S(1)}, bf16[512,1024]{1,0:T(8,128)(2,1)S(1)}, u32[]{:S(2)}, u32[]{:S(2)}) %collective-permute-start.3) | collective-permute-done | bytes 1048608 | tf_op jit(solution)/shard_map/ppermute | solution.py:18
  38.7 3.9 %pair_level.4 = (f32[64,512]{1,0:T(8,128)S(1)}, bf16[256,256]{1,0:T(8,128)(2,1)S(1)}, bf16[256,256]{1,0:T(8,128)(2,1)S(1)}, bf16[256,512]{1,0:T(8,128)(2,1)S(1)}) custom-call(bf16[64,96]{1,0:T(8,128)(2,1)S(1)} %get-tuple-element.32.pick_ref, f32[64,512]{1,0:T(8,128)S(1)} %get-tuple-element.33.sums_ref, ...), custom_call_target="tpu_custom_call", output_to_operand_aliasing={{1}: (7, {}), {2}: (8, {}), {3}: (9, {})} | custom-call | flops 2684354560 | bytes 4194304 | tf_op jit(solution)/shard_map/pair_level/pallas_call | solution.py:573
  42.6 0.1 collective-permute-start.8
  42.7 1.4 %collective-permute-start.6 = (bf16[256,256]{1,0:T(8,128)(2,1)S(1)}, bf16[256,256]{1,0:T(8,128)(2,1)S(1)}, u32[]{:S(2)}, u32[]{:S(2)}) collective-permute-start(bf16[256,256]{1,0:T(8,128)(2,1)S(1)} %get-tuple-element.46), channel_id=1, source_target_pairs={{0,8},{8,0},{16,24},{24,16},{1,9},{9,1},{17,25},{25,17},{2,10},{10... | collective-permute-start | bytes 393224 | tf_op jit(solution)/shard_map/ppermute | solution.py:18
  44.1 0.1 collective-permute-start.7
  44.2 3.7 %collective-permute-done.4.refs_0_ = bf16[512,512]{1,0:T(8,128)(2,1)S(1)} collective-permute-done((bf16[512,512]{1,0:T(8,128)(2,1)S(1)}, bf16[512,512]{1,0:T(8,128)(2,1)S(1)}, u32[]{:S(2)}, u32[]{:S(2)}) %collective-permute-start.4) | collective-permute-done | bytes 524320 | tf_op jit(solution)/shard_map/ppermute | solution.py:18
  47.9 0.8 %collective-permute-done.5.refs_1_ = bf16[528,512]{1,0:T(8,128)(2,1)S(1)} collective-permute-done((bf16[528,512]{1,0:T(8,128)(2,1)S(1)}, bf16[528,512]{1,0:T(8,128)(2,1)S(1)}, u32[]{:S(2)}, u32[]{:S(2)}) %collective-permute-start.5) | collective-permute-done | bytes 540704 | tf_op jit(solution)/shard_map/ppermute | solution.py:18
  48.8 2.0 %pair_level.5.sums_ref = f32[64,512]{1,0:T(8,128)S(1)} custom-call(f32[8,32,128]{2,1,0:T(8,128)S(1)} %get-tuple-element.31.pick_ref.mask_ref, f32[64,512]{1,0:T(8,128)S(1)} %get-tuple-element.41.sums_ref, bf16[2,2,256,1024]{3,2,1,0:T(8,128)(2,1)S(1)} %get-tuple-element.34.panel_ref, bf16[512,512]{1,0:T(8,128)(2,1)S(1)} %collective-permute-done.4.refs_0_, ...), custom_call_target="tpu_custom_call" | custom-call | flops 1073741824 | bytes 4194304 | tf_op jit(solution)/shard_map/pair_level/pallas_call | solution.py:573
  50.8 0.0 collective-permute-done.6.refs_0_
  50.8 0.9 %pair_level.6.sums_ref = f32[64,512]{1,0:T(8,128)S(1)} custom-call(f32[8,32,128]{2,1,0:T(8,128)S(1)} %get-tuple-element.31.pick_ref.mask_ref, f32[64,512]{1,0:T(8,128)S(1)} %pair_level.5.sums_ref, bf16[2,512,512]{2,1,0:T(8,128)(2,1)S(1)} %get-tuple-element.45.panel_ref, bf16[256,256]{1,0:T(8,128)(2,1)S(1)} %collective-permute-done.6.refs_0_), custom_call_target="tpu_custom_call" | custom-call | flops 268435456 | bytes 4194304 | tf_op jit(solution)/shard_map/pair_level/pallas_call | solution.py:573
  51.7 0.0 collective-permute-done.7.refs_0_
  51.7 0.0 collective-permute-done.8.refs_1_
  51.7 1.2 %pair_level.7 = (f32[16,512]{1,0:T(8,128)S(1)}, f32[16,512]{1,0:T(8,128)S(1)}, f32[16,512]{1,0:T(8,128)S(1)}, f32[16,512]{1,0:T(8,128)S(1)}) custom-call(f32[8,32,128]{2,1,0:T(8,128)S(1)} %get-tuple-element.31.pick_ref.mask_ref, f32[64,512]{1,0:T(8,128)S(1)} %pair_level.6.sums_ref, bf16[2,512,512]{2,1,0:T(8,128)(2,1)S(1)} %get-tuple-element.45.panel_ref, ...), custom_call_target="tpu_custom_call" | custom-call | flops 268435456 | bytes 4194304 | tf_op jit(solution)/shard_map/pair_level/pallas_call | solution.py:573
  52.9 1.4 %collective-permute-start.10 = (f32[16,512]{1,0:T(8,128)S(1)}, f32[16,512]{1,0:T(8,128)S(1)}, u32[]{:S(2)}, u32[]{:S(2)}) collective-permute-start(f32[16,512]{1,0:T(8,128)S(1)} %get-tuple-element.50), channel_id=1, source_target_pairs={{0,24},{8,16},{16,8},{24,0},{1,25},{9,17},{17,9},{25,1},{2,26},{10... | collective-permute-start | bytes 98312 | tf_op jit(solution)/shard_map/ppermute | solution.py:18
  54.3 1.1 %collective-permute-start.11 = (f32[16,512]{1,0:T(8,128)S(1)}, f32[16,512]{1,0:T(8,128)S(1)}, u32[]{:S(2)}, u32[]{:S(2)}) collective-permute-start(f32[16,512]{1,0:T(8,128)S(1)} %get-tuple-element.51), channel_id=1, source_target_pairs={{0,16},{8,24},{16,0},{24,8},{1,17},{9,25},{17,1},{25,9},{2,18},{10... | collective-permute-start | bytes 98312 | tf_op jit(solution)/shard_map/ppermute | solution.py:18
  55.4 0.2 collective-permute-start.9
  55.6 1.2 %collective-permute-done.10.refs_1_ = f32[16,512]{1,0:T(8,128)S(1)} collective-permute-done((f32[16,512]{1,0:T(8,128)S(1)}, f32[16,512]{1,0:T(8,128)S(1)}, u32[]{:S(2)}, u32[]{:S(2)}) %collective-permute-start.10) | collective-permute-done | bytes 32800 | tf_op jit(solution)/shard_map/ppermute | solution.py:18
  56.9 0.3 collective-permute-done.11.refs_2_
  57.2 1.0 %collective-permute-done.9.refs_0_ = f32[16,512]{1,0:T(8,128)S(1)} collective-permute-done((f32[16,512]{1,0:T(8,128)S(1)}, f32[16,512]{1,0:T(8,128)S(1)}, u32[]{:S(2)}, u32[]{:S(2)}) %collective-permute-start.9) | collective-permute-done | bytes 32800 | tf_op jit(solution)/shard_map/ppermute | solution.py:18
  58.2 0.7 %finish.1 = f32[8,2,2,511]{3,2,1,0:T(2,128)} custom-call(f32[16,512]{1,0:T(8,128)S(1)} %collective-permute-done.9.refs_0_, f32[16,512]{1,0:T(8,128)S(1)} %collective-permute-done.10.refs_1_, f32[16,512]{1,0:T(8,128)S(1)} %collective-permute-done.11.refs_2_, f32[16,512]{1,0:T(8,128)S(1)} %get-tuple-element.52.refs_3_), custom_call_target="tpu_custom_call" | custom-call | tf_op jit(solution)/shard_map/finish/pallas_call | solution.py:603
Async XLA Ops:
  1.0 12.5 %copy-start = (s32[2,256]{1,0:T(2,128)S(1)}, s32[2,256]{1,0:T(2,128)}, u32[]{:S(2)}) copy-start(s32[2,256]{1,0:T(2,128)} %position_ref.5) | copy-start | bytes 6148
  1.1 12.5 %copy-start.1 = (s32[2,3,2]{1,2,0:T(2,128)S(1)}, s32[2,3,2]{1,2,0:T(2,128)}, u32[]{:S(2)}) copy-start(s32[2,3,2]{1,2,0:T(2,128)} %param.5) | copy-start | bytes 148
  1.1 12.5 %collective-permute-start = (bf16[528,256]{1,0:T(8,128)(2,1)S(1)}, bf16[528,256]{1,0:T(8,128)(2,1)S(1)}, u32[]{:S(2)}, u32[]{:S(2)}) collective-permute-start(bf16[528,256]{1,0:T(8,128)(2,1)S(1)} %first_piece.1._), channel_id=1, source_target_pairs={{0,16},{8,24},{16,0},{24,8},{1,17},{9,25},{17,1},{25,9},{2,18},{10... | collective-permute-start | bytes 811016 | tf_op jit(solution)/shard_map/ppermute | solution.py:18
  3.2 10.4 %collective-permute-start.1 = (bf16[528,256]{1,0:T(8,128)(2,1)S(1)}, bf16[528,256]{1,0:T(8,128)(2,1)S(1)}, u32[]{:S(2)}, u32[]{:S(2)}) collective-permute-start(bf16[528,256]{1,0:T(8,128)(2,1)S(1)} %first_piece.1._), channel_id=1, source_target_pairs={{0,8},{8,0},{16,24},{24,16},{1,9},{9,1},{17,25},{25,17},{2,10},{10... | collective-permute-start | bytes 811016 | tf_op jit(solution)/shard_map/ppermute | solution.py:18
  13.2 24.3 %collective-permute-start.2 = (bf16[512,1024]{1,0:T(8,128)(2,1)S(1)}, bf16[512,1024]{1,0:T(8,128)(2,1)S(1)}, u32[]{:S(2)}, u32[]{:S(2)}) collective-permute-start(bf16[512,1024]{1,0:T(8,128)(2,1)S(1)} %get-tuple-element.36), channel_id=1, source_target_pairs={{0,8},{8,0},{16,24},{24,16},{1,9},{9,1},{17,25},{25,17},{2,10},{10... | collective-permute-start | bytes 3145736 | tf_op jit(solution)/shard_map/ppermute | solution.py:18
  13.5 25.2 %collective-permute-start.3 = (bf16[512,1024]{1,0:T(8,128)(2,1)S(1)}, bf16[512,1024]{1,0:T(8,128)(2,1)S(1)}, u32[]{:S(2)}, u32[]{:S(2)}) collective-permute-start(bf16[512,1024]{1,0:T(8,128)(2,1)S(1)} %get-tuple-element.36), channel_id=1, source_target_pairs={{0,16},{8,24},{16,0},{24,8},{1,17},{9,25},{17,1},{25,9},{2,18},{10... | collective-permute-start | bytes 3145736 | tf_op jit(solution)/shard_map/ppermute | solution.py:18
  22.3 26.4 %collective-permute-start.5 = (bf16[528,512]{1,0:T(8,128)(2,1)S(1)}, bf16[528,512]{1,0:T(8,128)(2,1)S(1)}, u32[]{:S(2)}, u32[]{:S(2)}) collective-permute-start(bf16[528,512]{1,0:T(8,128)(2,1)S(1)} %get-tuple-element.43), channel_id=1, source_target_pairs={{0,16},{8,24},{16,0},{24,8},{1,17},{9,25},{17,1},{25,9},{2,18},{10... | collective-permute-start | bytes 1622024 | tf_op jit(solution)/shard_map/ppermute | solution.py:18
  23.8 24.2 %collective-permute-start.4 = (bf16[512,512]{1,0:T(8,128)(2,1)S(1)}, bf16[512,512]{1,0:T(8,128)(2,1)S(1)}, u32[]{:S(2)}, u32[]{:S(2)}) collective-permute-start(bf16[512,512]{1,0:T(8,128)(2,1)S(1)} %get-tuple-element.42), channel_id=1, source_target_pairs={{0,8},{8,0},{16,24},{24,16},{1,9},{9,1},{17,25},{25,17},{2,10},{10... | collective-permute-start | bytes 1572872 | tf_op jit(solution)/shard_map/ppermute | solution.py:18
  42.6 9.1 %collective-permute-start.8 = (bf16[256,512]{1,0:T(8,128)(2,1)S(1)}, bf16[256,512]{1,0:T(8,128)(2,1)S(1)}, u32[]{:S(2)}, u32[]{:S(2)}) collective-permute-start(bf16[256,512]{1,0:T(8,128)(2,1)S(1)} %get-tuple-element.48), channel_id=1, source_target_pairs={{0,16},{8,24},{16,0},{24,8},{1,17},{9,25},{17,1},{25,9},{2,18},{10... | collective-permute-start | bytes 786440 | tf_op jit(solution)/shard_map/ppermute | solution.py:18
  42.7 8.1 %collective-permute-start.6 = (bf16[256,256]{1,0:T(8,128)(2,1)S(1)}, bf16[256,256]{1,0:T(8,128)(2,1)S(1)}, u32[]{:S(2)}, u32[]{:S(2)}) collective-permute-start(bf16[256,256]{1,0:T(8,128)(2,1)S(1)} %get-tuple-element.46), channel_id=1, source_target_pairs={{0,8},{8,0},{16,24},{24,16},{1,9},{9,1},{17,25},{25,17},{2,10},{10... | collective-permute-start | bytes 393224 | tf_op jit(solution)/shard_map/ppermute | solution.py:18
  44.1 7.6 %collective-permute-start.7 = (bf16[256,256]{1,0:T(8,128)(2,1)S(1)}, bf16[256,256]{1,0:T(8,128)(2,1)S(1)}, u32[]{:S(2)}, u32[]{:S(2)}) collective-permute-start(bf16[256,256]{1,0:T(8,128)(2,1)S(1)} %get-tuple-element.47), channel_id=1, source_target_pairs={{0,8},{8,0},{16,24},{24,16},{1,9},{9,1},{17,25},{25,17},{2,10},{10... | collective-permute-start | bytes 393224 | tf_op jit(solution)/shard_map/ppermute | solution.py:18
  52.9 4.0 %collective-permute-start.10 = (f32[16,512]{1,0:T(8,128)S(1)}, f32[16,512]{1,0:T(8,128)S(1)}, u32[]{:S(2)}, u32[]{:S(2)}) collective-permute-start(f32[16,512]{1,0:T(8,128)S(1)} %get-tuple-element.50), channel_id=1, source_target_pairs={{0,24},{8,16},{16,8},{24,0},{1,25},{9,17},{17,9},{25,1},{2,26},{10... | collective-permute-start | bytes 98312 | tf_op jit(solution)/shard_map/ppermute | solution.py:18
  54.3 2.8 %collective-permute-start.11 = (f32[16,512]{1,0:T(8,128)S(1)}, f32[16,512]{1,0:T(8,128)S(1)}, u32[]{:S(2)}, u32[]{:S(2)}) collective-permute-start(f32[16,512]{1,0:T(8,128)S(1)} %get-tuple-element.51), channel_id=1, source_target_pairs={{0,16},{8,24},{16,0},{24,8},{1,17},{9,25},{17,1},{25,9},{2,18},{10... | collective-permute-start | bytes 98312 | tf_op jit(solution)/shard_map/ppermute | solution.py:18
  55.4 2.8 %collective-permute-start.9 = (f32[16,512]{1,0:T(8,128)S(1)}, f32[16,512]{1,0:T(8,128)S(1)}, u32[]{:S(2)}, u32[]{:S(2)}) collective-permute-start(f32[16,512]{1,0:T(8,128)S(1)} %get-tuple-element.49), channel_id=1, source_target_pairs={{0,8},{8,0},{16,24},{24,16},{1,9},{9,1},{17,25},{25,17},{2,10},{10... | collective-permute-start | bytes 98312 | tf_op jit(solution)/shard_map/ppermute | solution.py:18

commit v4 on v3

--- a/solution.py
+++ b/solution.py
@@ -9,7 +9,7 @@
 
 RG_DEV = 8
 GROUP_ROWS = 16
-EARLY_TILES = 3
+EARLY_TILES = 1
 HBM = pl.BlockSpec(memory_space=pltpu.HBM)
 WHOLE = pl.BlockSpec(memory_space=pltpu.VMEM)
 

time: 59 us -> 59.9 us (1.015); the launches traced: 58.8 us -> 59 us
    pallas_call x1, Pallas kernels: 8.73 us -> 6.07 us  [early_pieces(): pl.pallas_call(functools.partial(rest_kernel, levels, rest), out_shape=[p...]
    pallas_call x1, Pallas kernels: 8.74 us -> 11.3 us  [own_level(): pl.pallas_call(functools.partial(own_kernel, levels, piece, last), out_sh...]
  transfers between devices with their start and end apart: 12 -> 12, of which waited for: 7 -> 9; matrix products, arithmetic and copies ran while one was open for 0% -> 0% of each run, Pallas kernels for 41% -> 41%
where the time goes in v4:
time: 59.9 us; the launch traced here: 59 us
  Pallas kernels  27 us (45%)
  waiting for transfers between devices  21.1 us (35%)
  starting transfers between devices  10.8 us (18%)
    ppermute x12, waiting for transfers between devices, xor_permute(): lax.ppermute(x, axis, [(i, i ^ distance) for i in range(lax.axis_size(axi...  21.1 us
    pallas_call x1, Pallas kernels, own_level(): pl.pallas_call(functools.partial(own_kernel, levels, piece, last), out_sh...  11.3 us
    ppermute x12, starting transfers between devices, xor_permute(): lax.ppermute(x, axis, [(i, i ^ distance) for i in range(lax.axis_size(axi...  10.8 us
    pallas_call x4, Pallas kernels, pair_call(): pl.pallas_call(kernel, out_shape=[jax.ShapeDtypeStruct((rows // shares, w...  7.98 us
    pallas_call x1, Pallas kernels, early_pieces(): pl.pallas_call(functools.partial(rest_kernel, levels, rest), out_shape=[p...  6.07 us
  transfers between devices with their start and end apart: 12, of which 9 were waited for; matrix products, arithmetic and copies ran while one was open for 0% of the time, Pallas kernels for 41%

profile of v4, /device:TPU:1, one launch (start us, length us, event | category | flops | bytes accessed | tf_op | source)
XLA Modules:
  0.0 59.0 jit_solution(14813100029243891660)
XLA Ops:
  0.0 1.0 %first_piece.1._ = bf16[528,256]{1,0:T(8,128)(2,1)S(1)} custom-call(s32[2,256]{1,0:T(2,128)} %position_ref.5, bf16[2,2,512,1024]{3,2,1,0:T(8,128)(2,1)} %volts_ref.5, s32[2,2,3]{2,1,0:T(2,128)} %bitcast.1), custom_call_target="tpu_custom_call" | custom-call | bytes 1048576 | tf_op jit(solution)/shard_map/first_piece/pallas_call | solution.py:341
  1.0 0.0 copy-start
  1.1 0.0 copy-start.1
  1.1 2.1 %collective-permute-start = (bf16[528,256]{1,0:T(8,128)(2,1)S(1)}, bf16[528,256]{1,0:T(8,128)(2,1)S(1)}, u32[]{:S(2)}, u32[]{:S(2)}) collective-permute-start(bf16[528,256]{1,0:T(8,128)(2,1)S(1)} %first_piece.1._), channel_id=1, source_target_pairs={{0,16},{8,24},{16,0},{24,8},{1,17},{9,25},{17,1},{25,9},{2,18},{10... | collective-permute-start | bytes 811016 | tf_op jit(solution)/shard_map/ppermute | solution.py:18
  3.2 1.2 %collective-permute-start.1 = (bf16[528,256]{1,0:T(8,128)(2,1)S(1)}, bf16[528,256]{1,0:T(8,128)(2,1)S(1)}, u32[]{:S(2)}, u32[]{:S(2)}) collective-permute-start(bf16[528,256]{1,0:T(8,128)(2,1)S(1)} %first_piece.1._), channel_id=1, source_target_pairs={{0,8},{8,0},{16,24},{24,16},{1,9},{9,1},{17,25},{25,17},{2,10},{10... | collective-permute-start | bytes 811016 | tf_op jit(solution)/shard_map/ppermute | solution.py:18
  4.4 6.1 %second_piece.1 = (bf16[512,1024]{1,0:T(8,128)(2,1)S(1)}, bf16[2,2,256,1024]{3,2,1,0:T(8,128)(2,1)S(1)}, f32[4,2,512]{2,1,0:T(2,128)S(1)}) custom-call(s32[2,256]{1,0:T(2,128)} %position_ref.5, bf16[2,2,512,1024]{3,2,1,0:T(8,128)(2,1)} %volts_ref.5, bf16[528,256]{1,0:T(8,128)(2,1)S(1)} %first_piece.1._), custom_call_target="tpu_custom_call" | custom-call | flops 268435456 | bytes 4194304 | tf_op jit(solution)/shard_map/second_piece/pallas_call | solution.py:356
  10.5 0.3 collective-permute-start.2
  10.8 0.1 collective-permute-start.3
  10.9 0.0 collective-permute-done.refs_0_
  10.9 0.0 collective-permute-done.1.refs_1_
  10.9 0.0 copy-done
  10.9 0.0 copy-done.1
  10.9 11.3 %own_level.1 = (bf16[2,2,256,1024]{3,2,1,0:T(8,128)(2,1)S(1)}, f32[64,512]{1,0:T(8,128)S(1)}, bf16[64,24]{1,0:T(8,128)(2,1)S(1)}, bf16[64,96]{1,0:T(8,128)(2,1)S...) custom-call(s32[2,2,3]{2,1,0:T(2,128)S(1)} %bitcast.2, ...), custom_call_target="tpu_custom_call" | custom-call | flops 17179869184 | bytes 6291456 | tf_op jit(solution)/shard_map/own_level/pallas_call | solution.py:464
  22.2 1.4 %collective-permute-start.5 = (bf16[528,512]{1,0:T(8,128)(2,1)S(1)}, bf16[528,512]{1,0:T(8,128)(2,1)S(1)}, u32[]{:S(2)}, u32[]{:S(2)}) collective-permute-start(bf16[528,512]{1,0:T(8,128)(2,1)S(1)} %get-tuple-element.43), channel_id=1, source_target_pairs={{0,16},{8,24},{16,0},{24,8},{1,17},{9,25},{17,1},{25,9},{2,18},{10... | collective-permute-start | bytes 1622024 | tf_op jit(solution)/shard_map/ppermute | solution.py:18
  23.6 1.2 %collective-permute-start.4 = (bf16[512,512]{1,0:T(8,128)(2,1)S(1)}, bf16[512,512]{1,0:T(8,128)(2,1)S(1)}, u32[]{:S(2)}, u32[]{:S(2)}) collective-permute-start(bf16[512,512]{1,0:T(8,128)(2,1)S(1)} %get-tuple-element.42), channel_id=1, source_target_pairs={{0,8},{8,0},{16,24},{24,16},{1,9},{9,1},{17,25},{25,17},{2,10},{10... | collective-permute-start | bytes 1572872 | tf_op jit(solution)/shard_map/ppermute | solution.py:18
  24.9 10.9 %collective-permute-done.2.refs_1_ = bf16[512,1024]{1,0:T(8,128)(2,1)S(1)} collective-permute-done((bf16[512,1024]{1,0:T(8,128)(2,1)S(1)}, bf16[512,1024]{1,0:T(8,128)(2,1)S(1)}, u32[]{:S(2)}, u32[]{:S(2)}) %collective-permute-start.2) | collective-permute-done | bytes 1048608 | tf_op jit(solution)/shard_map/ppermute | solution.py:18
  35.8 0.2 collective-permute-done.3.refs_3_
  36.0 3.9 %pair_level.4 = (f32[64,512]{1,0:T(8,128)S(1)}, bf16[256,256]{1,0:T(8,128)(2,1)S(1)}, bf16[256,256]{1,0:T(8,128)(2,1)S(1)}, bf16[256,512]{1,0:T(8,128)(2,1)S(1)}) custom-call(bf16[64,96]{1,0:T(8,128)(2,1)S(1)} %get-tuple-element.32.pick_ref, f32[64,512]{1,0:T(8,128)S(1)} %get-tuple-element.33.sums_ref, ...), custom_call_target="tpu_custom_call", output_to_operand_aliasing={{1}: (7, {}), {2}: (8, {}), {3}: (9, {})} | custom-call | flops 2684354560 | bytes 4194304 | tf_op jit(solution)/shard_map/pair_level/pallas_call | solution.py:573
  39.9 0.2 collective-permute-start.8
  40.1 1.3 %collective-permute-start.6 = (bf16[256,256]{1,0:T(8,128)(2,1)S(1)}, bf16[256,256]{1,0:T(8,128)(2,1)S(1)}, u32[]{:S(2)}, u32[]{:S(2)}) collective-permute-start(bf16[256,256]{1,0:T(8,128)(2,1)S(1)} %get-tuple-element.46), channel_id=1, source_target_pairs={{0,8},{8,0},{16,24},{24,16},{1,9},{9,1},{17,25},{25,17},{2,10},{10... | collective-permute-start | bytes 393224 | tf_op jit(solution)/shard_map/ppermute | solution.py:18
  41.4 0.1 collective-permute-start.7
  41.5 5.5 %collective-permute-done.4.refs_0_ = bf16[512,512]{1,0:T(8,128)(2,1)S(1)} collective-permute-done((bf16[512,512]{1,0:T(8,128)(2,1)S(1)}, bf16[512,512]{1,0:T(8,128)(2,1)S(1)}, u32[]{:S(2)}, u32[]{:S(2)}) %collective-permute-start.4) | collective-permute-done | bytes 524320 | tf_op jit(solution)/shard_map/ppermute | solution.py:18
  47.0 0.6 collective-permute-done.5.refs_1_
  47.6 2.0 %pair_level.5.sums_ref = f32[64,512]{1,0:T(8,128)S(1)} custom-call(f32[8,32,128]{2,1,0:T(8,128)S(1)} %get-tuple-element.31.pick_ref.mask_ref, f32[64,512]{1,0:T(8,128)S(1)} %get-tuple-element.41.sums_ref, bf16[2,2,256,1024]{3,2,1,0:T(8,128)(2,1)S(1)} %get-tuple-element.34.panel_ref, bf16[512,512]{1,0:T(8,128)(2,1)S(1)} %collective-permute-done.4.refs_0_, ...), custom_call_target="tpu_custom_call" | custom-call | flops 1073741824 | bytes 4194304 | tf_op jit(solution)/shard_map/pair_level/pallas_call | solution.py:573
  49.6 0.0 collective-permute-done.6.refs_0_
  49.6 0.9 %pair_level.6.sums_ref = f32[64,512]{1,0:T(8,128)S(1)} custom-call(f32[8,32,128]{2,1,0:T(8,128)S(1)} %get-tuple-element.31.pick_ref.mask_ref, f32[64,512]{1,0:T(8,128)S(1)} %pair_level.5.sums_ref, bf16[2,512,512]{2,1,0:T(8,128)(2,1)S(1)} %get-tuple-element.45.panel_ref, bf16[256,256]{1,0:T(8,128)(2,1)S(1)} %collective-permute-done.6.refs_0_), custom_call_target="tpu_custom_call" | custom-call | flops 268435456 | bytes 4194304 | tf_op jit(solution)/shard_map/pair_level/pallas_call | solution.py:573
  50.5 0.2 collective-permute-done.7.refs_0_
  50.7 0.8 %collective-permute-done.8.refs_1_ = bf16[256,512]{1,0:T(8,128)(2,1)S(1)} collective-permute-done((bf16[256,512]{1,0:T(8,128)(2,1)S(1)}, bf16[256,512]{1,0:T(8,128)(2,1)S(1)}, u32[]{:S(2)}, u32[]{:S(2)}) %collective-permute-start.8) | collective-permute-done | bytes 262176 | tf_op jit(solution)/shard_map/ppermute | solution.py:18
  51.6 1.2 %pair_level.7 = (f32[16,512]{1,0:T(8,128)S(1)}, f32[16,512]{1,0:T(8,128)S(1)}, f32[16,512]{1,0:T(8,128)S(1)}, f32[16,512]{1,0:T(8,128)S(1)}) custom-call(f32[8,32,128]{2,1,0:T(8,128)S(1)} %get-tuple-element.31.pick_ref.mask_ref, f32[64,512]{1,0:T(8,128)S(1)} %pair_level.6.sums_ref, bf16[2,512,512]{2,1,0:T(8,128)(2,1)S(1)} %get-tuple-element.45.panel_ref, ...), custom_call_target="tpu_custom_call" | custom-call | flops 268435456 | bytes 4194304 | tf_op jit(solution)/shard_map/pair_level/pallas_call | solution.py:573
  52.8 1.2 %collective-permute-start.10 = (f32[16,512]{1,0:T(8,128)S(1)}, f32[16,512]{1,0:T(8,128)S(1)}, u32[]{:S(2)}, u32[]{:S(2)}) collective-permute-start(f32[16,512]{1,0:T(8,128)S(1)} %get-tuple-element.50), channel_id=1, source_target_pairs={{0,24},{8,16},{16,8},{24,0},{1,25},{9,17},{17,9},{25,1},{2,26},{10... | collective-permute-start | bytes 98312 | tf_op jit(solution)/shard_map/ppermute | solution.py:18
  54.0 1.2 %collective-permute-start.11 = (f32[16,512]{1,0:T(8,128)S(1)}, f32[16,512]{1,0:T(8,128)S(1)}, u32[]{:S(2)}, u32[]{:S(2)}) collective-permute-start(f32[16,512]{1,0:T(8,128)S(1)} %get-tuple-element.51), channel_id=1, source_target_pairs={{0,16},{8,24},{16,0},{24,8},{1,17},{9,25},{17,1},{25,9},{2,18},{10... | collective-permute-start | bytes 98312 | tf_op jit(solution)/shard_map/ppermute | solution.py:18
  55.3 0.3 collective-permute-start.9
  55.5 1.2 %collective-permute-done.10.refs_1_ = f32[16,512]{1,0:T(8,128)S(1)} collective-permute-done((f32[16,512]{1,0:T(8,128)S(1)}, f32[16,512]{1,0:T(8,128)S(1)}, u32[]{:S(2)}, u32[]{:S(2)}) %collective-permute-start.10) | collective-permute-done | bytes 32800 | tf_op jit(solution)/shard_map/ppermute | solution.py:18
  56.7 0.9 %collective-permute-done.11.refs_2_ = f32[16,512]{1,0:T(8,128)S(1)} collective-permute-done((f32[16,512]{1,0:T(8,128)S(1)}, f32[16,512]{1,0:T(8,128)S(1)}, u32[]{:S(2)}, u32[]{:S(2)}) %collective-permute-start.11) | collective-permute-done | bytes 32800 | tf_op jit(solution)/shard_map/ppermute | solution.py:18
  57.6 0.7 %collective-permute-done.9.refs_0_ = f32[16,512]{1,0:T(8,128)S(1)} collective-permute-done((f32[16,512]{1,0:T(8,128)S(1)}, f32[16,512]{1,0:T(8,128)S(1)}, u32[]{:S(2)}, u32[]{:S(2)}) %collective-permute-start.9) | collective-permute-done | bytes 32800 | tf_op jit(solution)/shard_map/ppermute | solution.py:18
  58.3 0.7 %finish.1 = f32[8,2,2,511]{3,2,1,0:T(2,128)} custom-call(f32[16,512]{1,0:T(8,128)S(1)} %collective-permute-done.9.refs_0_, f32[16,512]{1,0:T(8,128)S(1)} %collective-permute-done.10.refs_1_, f32[16,512]{1,0:T(8,128)S(1)} %collective-permute-done.11.refs_2_, f32[16,512]{1,0:T(8,128)S(1)} %get-tuple-element.52.refs_3_), custom_call_target="tpu_custom_call" | custom-call | tf_op jit(solution)/shard_map/finish/pallas_call | solution.py:603
Async XLA Ops:
  1.0 9.9 %copy-start = (s32[2,256]{1,0:T(2,128)S(1)}, s32[2,256]{1,0:T(2,128)}, u32[]{:S(2)}) copy-start(s32[2,256]{1,0:T(2,128)} %position_ref.5) | copy-start | bytes 6148
  1.1 9.8 %copy-start.1 = (s32[2,3,2]{1,2,0:T(2,128)S(1)}, s32[2,3,2]{1,2,0:T(2,128)}, u32[]{:S(2)}) copy-start(s32[2,3,2]{1,2,0:T(2,128)} %param.5) | copy-start | bytes 148
  1.1 9.8 %collective-permute-start = (bf16[528,256]{1,0:T(8,128)(2,1)S(1)}, bf16[528,256]{1,0:T(8,128)(2,1)S(1)}, u32[]{:S(2)}, u32[]{:S(2)}) collective-permute-start(bf16[528,256]{1,0:T(8,128)(2,1)S(1)} %first_piece.1._), channel_id=1, source_target_pairs={{0,16},{8,24},{16,0},{24,8},{1,17},{9,25},{17,1},{25,9},{2,18},{10... | collective-permute-start | bytes 811016 | tf_op jit(solution)/shard_map/ppermute | solution.py:18
  3.2 7.7 %collective-permute-start.1 = (bf16[528,256]{1,0:T(8,128)(2,1)S(1)}, bf16[528,256]{1,0:T(8,128)(2,1)S(1)}, u32[]{:S(2)}, u32[]{:S(2)}) collective-permute-start(bf16[528,256]{1,0:T(8,128)(2,1)S(1)} %first_piece.1._), channel_id=1, source_target_pairs={{0,8},{8,0},{16,24},{24,16},{1,9},{9,1},{17,25},{25,17},{2,10},{10... | collective-permute-start | bytes 811016 | tf_op jit(solution)/shard_map/ppermute | solution.py:18
  10.5 25.3 %collective-permute-start.2 = (bf16[512,1024]{1,0:T(8,128)(2,1)S(1)}, bf16[512,1024]{1,0:T(8,128)(2,1)S(1)}, u32[]{:S(2)}, u32[]{:S(2)}) collective-permute-start(bf16[512,1024]{1,0:T(8,128)(2,1)S(1)} %get-tuple-element.36), channel_id=1, source_target_pairs={{0,8},{8,0},{16,24},{24,16},{1,9},{9,1},{17,25},{25,17},{2,10},{10... | collective-permute-start | bytes 3145736 | tf_op jit(solution)/shard_map/ppermute | solution.py:18
  10.8 25.2 %collective-permute-start.3 = (bf16[512,1024]{1,0:T(8,128)(2,1)S(1)}, bf16[512,1024]{1,0:T(8,128)(2,1)S(1)}, u32[]{:S(2)}, u32[]{:S(2)}) collective-permute-start(bf16[512,1024]{1,0:T(8,128)(2,1)S(1)} %get-tuple-element.36), channel_id=1, source_target_pairs={{0,16},{8,24},{16,0},{24,8},{1,17},{9,25},{17,1},{25,9},{2,18},{10... | collective-permute-start | bytes 3145736 | tf_op jit(solution)/shard_map/ppermute | solution.py:18
  22.2 25.4 %collective-permute-start.5 = (bf16[528,512]{1,0:T(8,128)(2,1)S(1)}, bf16[528,512]{1,0:T(8,128)(2,1)S(1)}, u32[]{:S(2)}, u32[]{:S(2)}) collective-permute-start(bf16[528,512]{1,0:T(8,128)(2,1)S(1)} %get-tuple-element.43), channel_id=1, source_target_pairs={{0,16},{8,24},{16,0},{24,8},{1,17},{9,25},{17,1},{25,9},{2,18},{10... | collective-permute-start | bytes 1622024 | tf_op jit(solution)/shard_map/ppermute | solution.py:18
  23.6 23.4 %collective-permute-start.4 = (bf16[512,512]{1,0:T(8,128)(2,1)S(1)}, bf16[512,512]{1,0:T(8,128)(2,1)S(1)}, u32[]{:S(2)}, u32[]{:S(2)}) collective-permute-start(bf16[512,512]{1,0:T(8,128)(2,1)S(1)} %get-tuple-element.42), channel_id=1, source_target_pairs={{0,8},{8,0},{16,24},{24,16},{1,9},{9,1},{17,25},{25,17},{2,10},{10... | collective-permute-start | bytes 1572872 | tf_op jit(solution)/shard_map/ppermute | solution.py:18
  39.9 11.7 %collective-permute-start.8 = (bf16[256,512]{1,0:T(8,128)(2,1)S(1)}, bf16[256,512]{1,0:T(8,128)(2,1)S(1)}, u32[]{:S(2)}, u32[]{:S(2)}) collective-permute-start(bf16[256,512]{1,0:T(8,128)(2,1)S(1)} %get-tuple-element.48), channel_id=1, source_target_pairs={{0,16},{8,24},{16,0},{24,8},{1,17},{9,25},{17,1},{25,9},{2,18},{10... | collective-permute-start | bytes 786440 | tf_op jit(solution)/shard_map/ppermute | solution.py:18
  40.1 9.6 %collective-permute-start.6 = (bf16[256,256]{1,0:T(8,128)(2,1)S(1)}, bf16[256,256]{1,0:T(8,128)(2,1)S(1)}, u32[]{:S(2)}, u32[]{:S(2)}) collective-permute-start(bf16[256,256]{1,0:T(8,128)(2,1)S(1)} %get-tuple-element.46), channel_id=1, source_target_pairs={{0,8},{8,0},{16,24},{24,16},{1,9},{9,1},{17,25},{25,17},{2,10},{10... | collective-permute-start | bytes 393224 | tf_op jit(solution)/shard_map/ppermute | solution.py:18
  41.4 9.3 %collective-permute-start.7 = (bf16[256,256]{1,0:T(8,128)(2,1)S(1)}, bf16[256,256]{1,0:T(8,128)(2,1)S(1)}, u32[]{:S(2)}, u32[]{:S(2)}) collective-permute-start(bf16[256,256]{1,0:T(8,128)(2,1)S(1)} %get-tuple-element.47), channel_id=1, source_target_pairs={{0,8},{8,0},{16,24},{24,16},{1,9},{9,1},{17,25},{25,17},{2,10},{10... | collective-permute-start | bytes 393224 | tf_op jit(solution)/shard_map/ppermute | solution.py:18
  52.8 3.9 %collective-permute-start.10 = (f32[16,512]{1,0:T(8,128)S(1)}, f32[16,512]{1,0:T(8,128)S(1)}, u32[]{:S(2)}, u32[]{:S(2)}) collective-permute-start(f32[16,512]{1,0:T(8,128)S(1)} %get-tuple-element.50), channel_id=1, source_target_pairs={{0,24},{8,16},{16,8},{24,0},{1,25},{9,17},{17,9},{25,1},{2,26},{10... | collective-permute-start | bytes 98312 | tf_op jit(solution)/shard_map/ppermute | solution.py:18
  54.0 3.6 %collective-permute-start.11 = (f32[16,512]{1,0:T(8,128)S(1)}, f32[16,512]{1,0:T(8,128)S(1)}, u32[]{:S(2)}, u32[]{:S(2)}) collective-permute-start(f32[16,512]{1,0:T(8,128)S(1)} %get-tuple-element.51), channel_id=1, source_target_pairs={{0,16},{8,24},{16,0},{24,8},{1,17},{9,25},{17,1},{25,9},{2,18},{10... | collective-permute-start | bytes 98312 | tf_op jit(solution)/shard_map/ppermute | solution.py:18
  55.3 3.1 %collective-permute-start.9 = (f32[16,512]{1,0:T(8,128)S(1)}, f32[16,512]{1,0:T(8,128)S(1)}, u32[]{:S(2)}, u32[]{:S(2)}) collective-permute-start(f32[16,512]{1,0:T(8,128)S(1)} %get-tuple-element.49), channel_id=1, source_target_pairs={{0,8},{8,0},{16,24},{24,16},{1,9},{9,1},{17,25},{25,17},{2,10},{10... | collective-permute-start | bytes 98312 | tf_op jit(solution)/shard_map/ppermute | solution.py:18

commit v5 on v1

--- a/solution.py
+++ b/solution.py
@@ -316,20 +316,20 @@
 
 
 def rest_kernel(levels, piece, position_ref, volts_ref, _, out_ref, panel_ref, lags_ref, *scratch):
-    position, raw, small_sem, in_sem = scratch
+    position, raw, own_raw, small_sem, in_sem, own_sem = scratch
     mine = parity(lax.axis_index("inp"), levels)
     load_position = pltpu.make_async_copy(position_ref, position, small_sem)
     load_position.start()
+    piece_loads = load_piece(piece, 1 - mine, position.shape[1], volts_ref, raw, in_sem)
     load_position.wait()
 
     @pl.when(on_odd_core())
     def _():
-        loads = load_channel(mine, volts_ref, raw, in_sem)
-        order_channel(loads, position, raw, panel_ref)
+        loads = load_channel(mine, volts_ref, own_raw, own_sem)
+        order_channel(loads, position, own_raw, panel_ref)
         own_tiles(panel_ref, lags_ref, 0, 0, EARLY_TILES)
 
-    loads = load_piece(piece, 1 - mine, position.shape[1], volts_ref, raw, in_sem)
-    order_piece(piece, loads, position, raw, out_ref)
+    order_piece(piece, piece_loads, position, raw, out_ref)
 
 
 def early_pieces(position_input, volts, groups, head, rest, levels):
@@ -366,7 +366,9 @@
         scratch_shapes=[
             position,
             pltpu.VMEM((blocks, 2, width, samples), jnp.bfloat16),
+            pltpu.VMEM((blocks, 2, width, samples), jnp.bfloat16),
             semaphore(()),
+            semaphore((blocks, 2)),
             semaphore((blocks, 2)),
         ],
         compiler_params=pltpu.CompilerParams(vmem_limit_bytes=16 << 20),

time: 59.2 us -> 58.8 us (level)
  Pallas kernels: 27.3 us -> 26.6 us
    pallas_call x1, Pallas kernels: 8.73 us -> 7.99 us  [early_pieces(): pl.pallas_call(functools.partial(rest_kernel, levels, rest), out_shape=[p...]
  transfers between devices with their start and end apart: 12 -> 12, of which waited for: 7 -> 7; matrix products, arithmetic and copies ran while one was open for 0% -> 0% of each run, Pallas kernels for 41% -> 40%
where the time goes in v5:
time: 58.8 us; the launch traced here: 58.6 us
  Pallas kernels  26.6 us (45%)
  waiting for transfers between devices  21 us (36%)
  starting transfers between devices  10.9 us (19%)
    ppermute x12, waiting for transfers between devices, xor_permute(): lax.ppermute(x, axis, [(i, i ^ distance) for i in range(lax.axis_size(axi...  21 us
    ppermute x12, starting transfers between devices, xor_permute(): lax.ppermute(x, axis, [(i, i ^ distance) for i in range(lax.axis_size(axi...  10.9 us
    pallas_call x1, Pallas kernels, own_level(): pl.pallas_call(functools.partial(own_kernel, levels, piece, last), out_sh...  8.77 us
    pallas_call x4, Pallas kernels, pair_call(): pl.pallas_call(kernel, out_shape=[jax.ShapeDtypeStruct((rows // shares, w...  8.13 us
    pallas_call x1, Pallas kernels, early_pieces(): pl.pallas_call(functools.partial(rest_kernel, levels, rest), out_shape=[p...  7.99 us
  transfers between devices with their start and end apart: 12, of which 7 were waited for; matrix products, arithmetic and copies ran while one was open for 0% of the time, Pallas kernels for 40%

profile of v5, /device:TPU:1, one launch (start us, length us, event | category | flops | bytes accessed | tf_op | source)
XLA Modules:
  0.0 58.6 jit_solution(9431068994861798770)
XLA Ops:
  0.0 1.0 %first_piece.1._ = bf16[528,256]{1,0:T(8,128)(2,1)S(1)} custom-call(s32[2,256]{1,0:T(2,128)} %position_ref.5, bf16[2,2,512,1024]{3,2,1,0:T(8,128)(2,1)} %volts_ref.5, s32[2,2,3]{2,1,0:T(2,128)} %bitcast.1), custom_call_target="tpu_custom_call" | custom-call | bytes 1048576 | tf_op jit(solution)/shard_map/first_piece/pallas_call | solution.py:342
  1.0 0.0 copy-start
  1.1 0.0 copy-start.1
  1.1 2.1 %collective-permute-start = (bf16[528,256]{1,0:T(8,128)(2,1)S(1)}, bf16[528,256]{1,0:T(8,128)(2,1)S(1)}, u32[]{:S(2)}, u32[]{:S(2)}) collective-permute-start(bf16[528,256]{1,0:T(8,128)(2,1)S(1)} %first_piece.1._), channel_id=1, source_target_pairs={{0,16},{8,24},{16,0},{24,8},{1,17},{9,25},{17,1},{25,9},{2,18},{10... | collective-permute-start | bytes 811016 | tf_op jit(solution)/shard_map/ppermute | solution.py:18
  3.2 1.2 %collective-permute-start.1 = (bf16[528,256]{1,0:T(8,128)(2,1)S(1)}, bf16[528,256]{1,0:T(8,128)(2,1)S(1)}, u32[]{:S(2)}, u32[]{:S(2)}) collective-permute-start(bf16[528,256]{1,0:T(8,128)(2,1)S(1)} %first_piece.1._), channel_id=1, source_target_pairs={{0,8},{8,0},{16,24},{24,16},{1,9},{9,1},{17,25},{25,17},{2,10},{10... | collective-permute-start | bytes 811016 | tf_op jit(solution)/shard_map/ppermute | solution.py:18
  4.4 8.0 %second_piece.1 = (bf16[512,1024]{1,0:T(8,128)(2,1)S(1)}, bf16[2,2,256,1024]{3,2,1,0:T(8,128)(2,1)S(1)}, f32[4,2,512]{2,1,0:T(2,128)S(1)}) custom-call(s32[2,256]{1,0:T(2,128)} %position_ref.5, bf16[2,2,512,1024]{3,2,1,0:T(8,128)(2,1)} %volts_ref.5, bf16[528,256]{1,0:T(8,128)(2,1)S(1)} %first_piece.1._), custom_call_target="tpu_custom_call" | custom-call | flops 268435456 | bytes 4194304 | tf_op jit(solution)/shard_map/second_piece/pallas_call | solution.py:357
  12.4 0.3 collective-permute-start.2
  12.7 0.1 collective-permute-start.3
  12.8 0.0 collective-permute-done.refs_0_
  12.8 0.0 collective-permute-done.1.refs_1_
  12.8 0.0 copy-done
  12.8 0.0 copy-done.1
  12.8 8.8 %own_level.1 = (bf16[2,2,256,1024]{3,2,1,0:T(8,128)(2,1)S(1)}, f32[64,512]{1,0:T(8,128)S(1)}, bf16[64,24]{1,0:T(8,128)(2,1)S(1)}, bf16[64,96]{1,0:T(8,128)(2,1)S...) custom-call(s32[2,2,3]{2,1,0:T(2,128)S(1)} %bitcast.2, ...), custom_call_target="tpu_custom_call" | custom-call | flops 17179869184 | bytes 6291456 | tf_op jit(solution)/shard_map/own_level/pallas_call | solution.py:467
  21.6 1.5 %collective-permute-start.5 = (bf16[528,512]{1,0:T(8,128)(2,1)S(1)}, bf16[528,512]{1,0:T(8,128)(2,1)S(1)}, u32[]{:S(2)}, u32[]{:S(2)}) collective-permute-start(bf16[528,512]{1,0:T(8,128)(2,1)S(1)} %get-tuple-element.45), channel_id=1, source_target_pairs={{0,16},{8,24},{16,0},{24,8},{1,17},{9,25},{17,1},{25,9},{2,18},{10... | collective-permute-start | bytes 1622024 | tf_op jit(solution)/shard_map/ppermute | solution.py:18
  23.1 1.2 %collective-permute-start.4 = (bf16[512,512]{1,0:T(8,128)(2,1)S(1)}, bf16[512,512]{1,0:T(8,128)(2,1)S(1)}, u32[]{:S(2)}, u32[]{:S(2)}) collective-permute-start(bf16[512,512]{1,0:T(8,128)(2,1)S(1)} %get-tuple-element.44), channel_id=1, source_target_pairs={{0,8},{8,0},{16,24},{24,16},{1,9},{9,1},{17,25},{25,17},{2,10},{10... | collective-permute-start | bytes 1572872 | tf_op jit(solution)/shard_map/ppermute | solution.py:18
  24.3 13.1 %collective-permute-done.2.refs_1_ = bf16[512,1024]{1,0:T(8,128)(2,1)S(1)} collective-permute-done((bf16[512,1024]{1,0:T(8,128)(2,1)S(1)}, bf16[512,1024]{1,0:T(8,128)(2,1)S(1)}, u32[]{:S(2)}, u32[]{:S(2)}) %collective-permute-start.2) | collective-permute-done | bytes 1048608 | tf_op jit(solution)/shard_map/ppermute | solution.py:18
  37.4 0.1 collective-permute-done.3.refs_3_
  37.4 3.9 %pair_level.4 = (f32[64,512]{1,0:T(8,128)S(1)}, bf16[256,256]{1,0:T(8,128)(2,1)S(1)}, bf16[256,256]{1,0:T(8,128)(2,1)S(1)}, bf16[256,512]{1,0:T(8,128)(2,1)S(1)}) custom-call(bf16[64,96]{1,0:T(8,128)(2,1)S(1)} %get-tuple-element.34.pick_ref, f32[64,512]{1,0:T(8,128)S(1)} %get-tuple-element.35.sums_ref, ...), custom_call_target="tpu_custom_call", output_to_operand_aliasing={{1}: (7, {}), {2}: (8, {}), {3}: (9, {})} | custom-call | flops 2684354560 | bytes 4194304 | tf_op jit(solution)/shard_map/pair_level/pallas_call | solution.py:567
  41.3 0.3 collective-permute-start.8
  41.6 1.2 %collective-permute-start.6 = (bf16[256,256]{1,0:T(8,128)(2,1)S(1)}, bf16[256,256]{1,0:T(8,128)(2,1)S(1)}, u32[]{:S(2)}, u32[]{:S(2)}) collective-permute-start(bf16[256,256]{1,0:T(8,128)(2,1)S(1)} %get-tuple-element.48), channel_id=1, source_target_pairs={{0,8},{8,0},{16,24},{24,16},{1,9},{9,1},{17,25},{25,17},{2,10},{10... | collective-permute-start | bytes 393224 | tf_op jit(solution)/shard_map/ppermute | solution.py:18
  42.8 0.2 collective-permute-start.7
  43.1 4.9 %collective-permute-done.4.refs_0_ = bf16[512,512]{1,0:T(8,128)(2,1)S(1)} collective-permute-done((bf16[512,512]{1,0:T(8,128)(2,1)S(1)}, bf16[512,512]{1,0:T(8,128)(2,1)S(1)}, u32[]{:S(2)}, u32[]{:S(2)}) %collective-permute-start.4) | collective-permute-done | bytes 524320 | tf_op jit(solution)/shard_map/ppermute | solution.py:18
  47.9 0.2 collective-permute-done.5.refs_1_
  48.1 2.2 %pair_level.5.sums_ref = f32[64,512]{1,0:T(8,128)S(1)} custom-call(bf16[64,48]{1,0:T(8,128)(2,1)S(1)} %get-tuple-element.33.pick_ref, f32[64,512]{1,0:T(8,128)S(1)} %get-tuple-element.43.sums_ref, bf16[2,2,256,1024]{3,2,1,0:T(8,128)(2,1)S(1)} %get-tuple-element.36.panel_ref, bf16[512,512]{1,0:T(8,128)(2,1)S(1)} %collective-permute-done.4.refs_0_, ...), custom_call_target="tpu_custom_call" | custom-call | flops 1073741824 | bytes 4194304 | tf_op jit(solution)/shard_map/pair_level/pallas_call | solution.py:567
  50.3 0.0 collective-permute-done.6.refs_0_
  50.3 0.9 %pair_level.6.sums_ref = f32[64,512]{1,0:T(8,128)S(1)} custom-call(f32[8,32,128]{2,1,0:T(8,128)S(1)} %get-tuple-element.32.mask_ref, f32[64,512]{1,0:T(8,128)S(1)} %pair_level.5.sums_ref, bf16[2,512,512]{2,1,0:T(8,128)(2,1)S(1)} %get-tuple-element.47.panel_ref, bf16[256,256]{1,0:T(8,128)(2,1)S(1)} %collective-permute-done.6.refs_0_), custom_call_target="tpu_custom_call" | custom-call | flops 268435456 | bytes 4194304 | tf_op jit(solution)/shard_map/pair_level/pallas_call | solution.py:567
  51.2 0.0 collective-permute-done.7.refs_0_
  51.2 0.0 collective-permute-done.8.refs_1_
  51.2 1.2 %pair_level.7 = (f32[16,512]{1,0:T(8,128)S(1)}, f32[16,512]{1,0:T(8,128)S(1)}, f32[16,512]{1,0:T(8,128)S(1)}, f32[16,512]{1,0:T(8,128)S(1)}) custom-call(f32[8,32,128]{2,1,0:T(8,128)S(1)} %get-tuple-element.32.mask_ref, f32[64,512]{1,0:T(8,128)S(1)} %pair_level.6.sums_ref, bf16[2,512,512]{2,1,0:T(8,128)(2,1)S(1)} %get-tuple-element.47.panel_ref, ...), custom_call_target="tpu_custom_call" | custom-call | flops 268435456 | bytes 4194304 | tf_op jit(solution)/shard_map/pair_level/pallas_call | solution.py:567
  52.5 1.5 %collective-permute-start.10 = (f32[16,512]{1,0:T(8,128)S(1)}, f32[16,512]{1,0:T(8,128)S(1)}, u32[]{:S(2)}, u32[]{:S(2)}) collective-permute-start(f32[16,512]{1,0:T(8,128)S(1)} %get-tuple-element.52), channel_id=1, source_target_pairs={{0,24},{8,16},{16,8},{24,0},{1,25},{9,17},{17,9},{25,1},{2,26},{10... | collective-permute-start | bytes 98312 | tf_op jit(solution)/shard_map/ppermute | solution.py:18
  54.0 1.3 %collective-permute-start.11 = (f32[16,512]{1,0:T(8,128)S(1)}, f32[16,512]{1,0:T(8,128)S(1)}, u32[]{:S(2)}, u32[]{:S(2)}) collective-permute-start(f32[16,512]{1,0:T(8,128)S(1)} %get-tuple-element.53), channel_id=1, source_target_pairs={{0,16},{8,24},{16,0},{24,8},{1,17},{9,25},{17,1},{25,9},{2,18},{10... | collective-permute-start | bytes 98312 | tf_op jit(solution)/shard_map/ppermute | solution.py:18
  55.2 0.0 collective-permute-start.9
  55.2 1.0 %collective-permute-done.10.refs_1_ = f32[16,512]{1,0:T(8,128)S(1)} collective-permute-done((f32[16,512]{1,0:T(8,128)S(1)}, f32[16,512]{1,0:T(8,128)S(1)}, u32[]{:S(2)}, u32[]{:S(2)}) %collective-permute-start.10) | collective-permute-done | bytes 32800 | tf_op jit(solution)/shard_map/ppermute | solution.py:18
  56.2 0.5 collective-permute-done.11.refs_2_
  56.7 1.3 %collective-permute-done.9.refs_0_ = f32[16,512]{1,0:T(8,128)S(1)} collective-permute-done((f32[16,512]{1,0:T(8,128)S(1)}, f32[16,512]{1,0:T(8,128)S(1)}, u32[]{:S(2)}, u32[]{:S(2)}) %collective-permute-start.9) | collective-permute-done | bytes 32800 | tf_op jit(solution)/shard_map/ppermute | solution.py:18
  58.0 0.7 %finish.1 = f32[8,2,2,511]{3,2,1,0:T(2,128)} custom-call(f32[16,512]{1,0:T(8,128)S(1)} %collective-permute-done.9.refs_0_, f32[16,512]{1,0:T(8,128)S(1)} %collective-permute-done.10.refs_1_, f32[16,512]{1,0:T(8,128)S(1)} %collective-permute-done.11.refs_2_, f32[16,512]{1,0:T(8,128)S(1)} %get-tuple-element.54.refs_3_), custom_call_target="tpu_custom_call" | custom-call | tf_op jit(solution)/shard_map/finish/pallas_call | solution.py:597
Async XLA Ops:
  1.0 11.8 %copy-start = (s32[2,256]{1,0:T(2,128)S(1)}, s32[2,256]{1,0:T(2,128)}, u32[]{:S(2)}) copy-start(s32[2,256]{1,0:T(2,128)} %position_ref.5) | copy-start | bytes 6148
  1.1 11.8 %copy-start.1 = (s32[2,3,2]{1,2,0:T(2,128)S(1)}, s32[2,3,2]{1,2,0:T(2,128)}, u32[]{:S(2)}) copy-start(s32[2,3,2]{1,2,0:T(2,128)} %param.5) | copy-start | bytes 148
  1.1 11.7 %collective-permute-start = (bf16[528,256]{1,0:T(8,128)(2,1)S(1)}, bf16[528,256]{1,0:T(8,128)(2,1)S(1)}, u32[]{:S(2)}, u32[]{:S(2)}) collective-permute-start(bf16[528,256]{1,0:T(8,128)(2,1)S(1)} %first_piece.1._), channel_id=1, source_target_pairs={{0,16},{8,24},{16,0},{24,8},{1,17},{9,25},{17,1},{25,9},{2,18},{10... | collective-permute-start | bytes 811016 | tf_op jit(solution)/shard_map/ppermute | solution.py:18
  3.2 9.6 %collective-permute-start.1 = (bf16[528,256]{1,0:T(8,128)(2,1)S(1)}, bf16[528,256]{1,0:T(8,128)(2,1)S(1)}, u32[]{:S(2)}, u32[]{:S(2)}) collective-permute-start(bf16[528,256]{1,0:T(8,128)(2,1)S(1)} %first_piece.1._), channel_id=1, source_target_pairs={{0,8},{8,0},{16,24},{24,16},{1,9},{9,1},{17,25},{25,17},{2,10},{10... | collective-permute-start | bytes 811016 | tf_op jit(solution)/shard_map/ppermute | solution.py:18
  12.4 25.0 %collective-permute-start.2 = (bf16[512,1024]{1,0:T(8,128)(2,1)S(1)}, bf16[512,1024]{1,0:T(8,128)(2,1)S(1)}, u32[]{:S(2)}, u32[]{:S(2)}) collective-permute-start(bf16[512,1024]{1,0:T(8,128)(2,1)S(1)} %get-tuple-element.38), channel_id=1, source_target_pairs={{0,8},{8,0},{16,24},{24,16},{1,9},{9,1},{17,25},{25,17},{2,10},{10... | collective-permute-start | bytes 3145736 | tf_op jit(solution)/shard_map/ppermute | solution.py:18
  12.7 24.7 %collective-permute-start.3 = (bf16[512,1024]{1,0:T(8,128)(2,1)S(1)}, bf16[512,1024]{1,0:T(8,128)(2,1)S(1)}, u32[]{:S(2)}, u32[]{:S(2)}) collective-permute-start(bf16[512,1024]{1,0:T(8,128)(2,1)S(1)} %get-tuple-element.38), channel_id=1, source_target_pairs={{0,16},{8,24},{16,0},{24,8},{1,17},{9,25},{17,1},{25,9},{2,18},{10... | collective-permute-start | bytes 3145736 | tf_op jit(solution)/shard_map/ppermute | solution.py:18
  21.6 26.5 %collective-permute-start.5 = (bf16[528,512]{1,0:T(8,128)(2,1)S(1)}, bf16[528,512]{1,0:T(8,128)(2,1)S(1)}, u32[]{:S(2)}, u32[]{:S(2)}) collective-permute-start(bf16[528,512]{1,0:T(8,128)(2,1)S(1)} %get-tuple-element.45), channel_id=1, source_target_pairs={{0,16},{8,24},{16,0},{24,8},{1,17},{9,25},{17,1},{25,9},{2,18},{10... | collective-permute-start | bytes 1622024 | tf_op jit(solution)/shard_map/ppermute | solution.py:18
  23.1 24.8 %collective-permute-start.4 = (bf16[512,512]{1,0:T(8,128)(2,1)S(1)}, bf16[512,512]{1,0:T(8,128)(2,1)S(1)}, u32[]{:S(2)}, u32[]{:S(2)}) collective-permute-start(bf16[512,512]{1,0:T(8,128)(2,1)S(1)} %get-tuple-element.44), channel_id=1, source_target_pairs={{0,8},{8,0},{16,24},{24,16},{1,9},{9,1},{17,25},{25,17},{2,10},{10... | collective-permute-start | bytes 1572872 | tf_op jit(solution)/shard_map/ppermute | solution.py:18
  41.3 9.9 %collective-permute-start.8 = (bf16[256,512]{1,0:T(8,128)(2,1)S(1)}, bf16[256,512]{1,0:T(8,128)(2,1)S(1)}, u32[]{:S(2)}, u32[]{:S(2)}) collective-permute-start(bf16[256,512]{1,0:T(8,128)(2,1)S(1)} %get-tuple-element.50), channel_id=1, source_target_pairs={{0,16},{8,24},{16,0},{24,8},{1,17},{9,25},{17,1},{25,9},{2,18},{10... | collective-permute-start | bytes 786440 | tf_op jit(solution)/shard_map/ppermute | solution.py:18
  41.6 8.7 %collective-permute-start.6 = (bf16[256,256]{1,0:T(8,128)(2,1)S(1)}, bf16[256,256]{1,0:T(8,128)(2,1)S(1)}, u32[]{:S(2)}, u32[]{:S(2)}) collective-permute-start(bf16[256,256]{1,0:T(8,128)(2,1)S(1)} %get-tuple-element.48), channel_id=1, source_target_pairs={{0,8},{8,0},{16,24},{24,16},{1,9},{9,1},{17,25},{25,17},{2,10},{10... | collective-permute-start | bytes 393224 | tf_op jit(solution)/shard_map/ppermute | solution.py:18
  42.8 8.4 %collective-permute-start.7 = (bf16[256,256]{1,0:T(8,128)(2,1)S(1)}, bf16[256,256]{1,0:T(8,128)(2,1)S(1)}, u32[]{:S(2)}, u32[]{:S(2)}) collective-permute-start(bf16[256,256]{1,0:T(8,128)(2,1)S(1)} %get-tuple-element.49), channel_id=1, source_target_pairs={{0,8},{8,0},{16,24},{24,16},{1,9},{9,1},{17,25},{25,17},{2,10},{10... | collective-permute-start | bytes 393224 | tf_op jit(solution)/shard_map/ppermute | solution.py:18
  52.5 3.7 %collective-permute-start.10 = (f32[16,512]{1,0:T(8,128)S(1)}, f32[16,512]{1,0:T(8,128)S(1)}, u32[]{:S(2)}, u32[]{:S(2)}) collective-permute-start(f32[16,512]{1,0:T(8,128)S(1)} %get-tuple-element.52), channel_id=1, source_target_pairs={{0,24},{8,16},{16,8},{24,0},{1,25},{9,17},{17,9},{25,1},{2,26},{10... | collective-permute-start | bytes 98312 | tf_op jit(solution)/shard_map/ppermute | solution.py:18
  54.0 2.8 %collective-permute-start.11 = (f32[16,512]{1,0:T(8,128)S(1)}, f32[16,512]{1,0:T(8,128)S(1)}, u32[]{:S(2)}, u32[]{:S(2)}) collective-permute-start(f32[16,512]{1,0:T(8,128)S(1)} %get-tuple-element.53), channel_id=1, source_target_pairs={{0,16},{8,24},{16,0},{24,8},{1,17},{9,25},{17,1},{25,9},{2,18},{10... | collective-permute-start | bytes 98312 | tf_op jit(solution)/shard_map/ppermute | solution.py:18
  55.2 2.8 %collective-permute-start.9 = (f32[16,512]{1,0:T(8,128)S(1)}, f32[16,512]{1,0:T(8,128)S(1)}, u32[]{:S(2)}, u32[]{:S(2)}) collective-permute-start(f32[16,512]{1,0:T(8,128)S(1)} %get-tuple-element.51), channel_id=1, source_target_pairs={{0,8},{8,0},{16,24},{24,16},{1,9},{9,1},{17,25},{25,17},{2,10},{10... | collective-permute-start | bytes 98312 | tf_op jit(solution)/shard_map/ppermute | solution.py:18

commit v6 on v3

--- a/solution.py
+++ b/solution.py
@@ -315,20 +315,20 @@
 
 
 def rest_kernel(levels, piece, position_ref, volts_ref, _, out_ref, panel_ref, lags_ref, *scratch):
-    position, raw, small_sem, in_sem = scratch
+    position, raw, own_raw, small_sem, in_sem, own_sem = scratch
     mine = parity(lax.axis_index("inp"), levels)
     load_position = pltpu.make_async_copy(position_ref, position, small_sem)
     load_position.start()
+    piece_loads = load_piece(piece, 1 - mine, position.shape[1], volts_ref, raw, in_sem)
     load_position.wait()
 
     @pl.when(on_odd_core())
     def _():
-        loads = load_channel(mine, volts_ref, raw, in_sem)
-        order_channel(loads, position, raw, panel_ref)
+        loads = load_channel(mine, volts_ref, own_raw, own_sem)
+        order_channel(loads, position, own_raw, panel_ref)
         own_tiles(panel_ref, lags_ref, 0, 0, EARLY_TILES)
 
-    loads = load_piece(piece, 1 - mine, position.shape[1], volts_ref, raw, in_sem)
-    order_piece(piece, loads, position, raw, out_ref)
+    order_piece(piece, piece_loads, position, raw, out_ref)
 
 
 def early_pieces(position_input, volts, groups, head, rest, levels):
@@ -365,7 +365,9 @@
         scratch_shapes=[
             position,
             pltpu.VMEM((blocks, 2, width, samples), jnp.bfloat16),
+            pltpu.VMEM((blocks, 2, width, samples), jnp.bfloat16),
             semaphore(()),
+            semaphore((blocks, 2)),
             semaphore((blocks, 2)),
         ],
         compiler_params=pltpu.CompilerParams(vmem_limit_bytes=16 << 20),

time: 59 us -> 58.6 us (level)
  Pallas kernels: 27.1 us -> 26.4 us
    pallas_call x1, Pallas kernels: 8.73 us -> 7.99 us  [early_pieces(): pl.pallas_call(functools.partial(rest_kernel, levels, rest), out_shape=[p...]
  transfers between devices with their start and end apart: 12 -> 12, of which waited for: 7 -> 7; matrix products, arithmetic and copies ran while one was open for 0% -> 0% of each run, Pallas kernels for 41% -> 40%
where the time goes in v6:
time: 58.6 us; the launch traced here: 58.5 us
  Pallas kernels  26.4 us (45%)
  waiting for transfers between devices  21.1 us (36%)
  starting transfers between devices  10.9 us (19%)
    ppermute x12, waiting for transfers between devices, xor_permute(): lax.ppermute(x, axis, [(i, i ^ distance) for i in range(lax.axis_size(axi...  21.1 us
    ppermute x12, starting transfers between devices, xor_permute(): lax.ppermute(x, axis, [(i, i ^ distance) for i in range(lax.axis_size(axi...  10.9 us
    pallas_call x1, Pallas kernels, own_level(): pl.pallas_call(functools.partial(own_kernel, levels, piece, last), out_sh...  8.72 us
    pallas_call x1, Pallas kernels, early_pieces(): pl.pallas_call(functools.partial(rest_kernel, levels, rest), out_shape=[p...  7.99 us
    pallas_call x4, Pallas kernels, pair_call(): pl.pallas_call(kernel, out_shape=[jax.ShapeDtypeStruct((rows // shares, w...  7.96 us
  transfers between devices with their start and end apart: 12, of which 7 were waited for; matrix products, arithmetic and copies ran while one was open for 0% of the time, Pallas kernels for 40%

profile of v6, /device:TPU:1, one launch (start us, length us, event | category | flops | bytes accessed | tf_op | source)
XLA Modules:
  0.0 58.5 jit_solution(13148203477064838962)
XLA Ops:
  0.0 1.0 %first_piece.1._ = bf16[528,256]{1,0:T(8,128)(2,1)S(1)} custom-call(s32[2,256]{1,0:T(2,128)} %position_ref.5, bf16[2,2,512,1024]{3,2,1,0:T(8,128)(2,1)} %volts_ref.5, s32[2,2,3]{2,1,0:T(2,128)} %bitcast.1), custom_call_target="tpu_custom_call" | custom-call | bytes 1048576 | tf_op jit(solution)/shard_map/first_piece/pallas_call | solution.py:341
  1.0 0.0 copy-start
  1.1 0.0 copy-start.1
  1.1 2.1 %collective-permute-start = (bf16[528,256]{1,0:T(8,128)(2,1)S(1)}, bf16[528,256]{1,0:T(8,128)(2,1)S(1)}, u32[]{:S(2)}, u32[]{:S(2)}) collective-permute-start(bf16[528,256]{1,0:T(8,128)(2,1)S(1)} %first_piece.1._), channel_id=1, source_target_pairs={{0,16},{8,24},{16,0},{24,8},{1,17},{9,25},{17,1},{25,9},{2,18},{10... | collective-permute-start | bytes 811016 | tf_op jit(solution)/shard_map/ppermute | solution.py:18
  3.2 1.2 %collective-permute-start.1 = (bf16[528,256]{1,0:T(8,128)(2,1)S(1)}, bf16[528,256]{1,0:T(8,128)(2,1)S(1)}, u32[]{:S(2)}, u32[]{:S(2)}) collective-permute-start(bf16[528,256]{1,0:T(8,128)(2,1)S(1)} %first_piece.1._), channel_id=1, source_target_pairs={{0,8},{8,0},{16,24},{24,16},{1,9},{9,1},{17,25},{25,17},{2,10},{10... | collective-permute-start | bytes 811016 | tf_op jit(solution)/shard_map/ppermute | solution.py:18
  4.4 8.0 %second_piece.1 = (bf16[512,1024]{1,0:T(8,128)(2,1)S(1)}, bf16[2,2,256,1024]{3,2,1,0:T(8,128)(2,1)S(1)}, f32[4,2,512]{2,1,0:T(2,128)S(1)}) custom-call(s32[2,256]{1,0:T(2,128)} %position_ref.5, bf16[2,2,512,1024]{3,2,1,0:T(8,128)(2,1)} %volts_ref.5, bf16[528,256]{1,0:T(8,128)(2,1)S(1)} %first_piece.1._), custom_call_target="tpu_custom_call" | custom-call | flops 268435456 | bytes 4194304 | tf_op jit(solution)/shard_map/second_piece/pallas_call | solution.py:356
  12.4 0.3 collective-permute-start.2
  12.7 0.1 collective-permute-start.3
  12.8 0.0 collective-permute-done.refs_0_
  12.8 0.0 collective-permute-done.1.refs_1_
  12.8 0.0 copy-done
  12.8 0.0 copy-done.1
  12.8 8.7 %own_level.1 = (bf16[2,2,256,1024]{3,2,1,0:T(8,128)(2,1)S(1)}, f32[64,512]{1,0:T(8,128)S(1)}, bf16[64,24]{1,0:T(8,128)(2,1)S(1)}, bf16[64,96]{1,0:T(8,128)(2,1)S...) custom-call(s32[2,2,3]{2,1,0:T(2,128)S(1)} %bitcast.2, ...), custom_call_target="tpu_custom_call" | custom-call | flops 17179869184 | bytes 6291456 | tf_op jit(solution)/shard_map/own_level/pallas_call | solution.py:466
  21.6 1.5 %collective-permute-start.5 = (bf16[528,512]{1,0:T(8,128)(2,1)S(1)}, bf16[528,512]{1,0:T(8,128)(2,1)S(1)}, u32[]{:S(2)}, u32[]{:S(2)}) collective-permute-start(bf16[528,512]{1,0:T(8,128)(2,1)S(1)} %get-tuple-element.43), channel_id=1, source_target_pairs={{0,16},{8,24},{16,0},{24,8},{1,17},{9,25},{17,1},{25,9},{2,18},{10... | collective-permute-start | bytes 1622024 | tf_op jit(solution)/shard_map/ppermute | solution.py:18
  23.0 1.2 %collective-permute-start.4 = (bf16[512,512]{1,0:T(8,128)(2,1)S(1)}, bf16[512,512]{1,0:T(8,128)(2,1)S(1)}, u32[]{:S(2)}, u32[]{:S(2)}) collective-permute-start(bf16[512,512]{1,0:T(8,128)(2,1)S(1)} %get-tuple-element.42), channel_id=1, source_target_pairs={{0,8},{8,0},{16,24},{24,16},{1,9},{9,1},{17,25},{25,17},{2,10},{10... | collective-permute-start | bytes 1572872 | tf_op jit(solution)/shard_map/ppermute | solution.py:18
  24.2 13.2 %collective-permute-done.2.refs_1_ = bf16[512,1024]{1,0:T(8,128)(2,1)S(1)} collective-permute-done((bf16[512,1024]{1,0:T(8,128)(2,1)S(1)}, bf16[512,1024]{1,0:T(8,128)(2,1)S(1)}, u32[]{:S(2)}, u32[]{:S(2)}) %collective-permute-start.2) | collective-permute-done | bytes 1048608 | tf_op jit(solution)/shard_map/ppermute | solution.py:18
  37.4 0.1 collective-permute-done.3.refs_3_
  37.5 3.9 %pair_level.4 = (f32[64,512]{1,0:T(8,128)S(1)}, bf16[256,256]{1,0:T(8,128)(2,1)S(1)}, bf16[256,256]{1,0:T(8,128)(2,1)S(1)}, bf16[256,512]{1,0:T(8,128)(2,1)S(1)}) custom-call(bf16[64,96]{1,0:T(8,128)(2,1)S(1)} %get-tuple-element.32.pick_ref, f32[64,512]{1,0:T(8,128)S(1)} %get-tuple-element.33.sums_ref, ...), custom_call_target="tpu_custom_call", output_to_operand_aliasing={{1}: (7, {}), {2}: (8, {}), {3}: (9, {})} | custom-call | flops 2684354560 | bytes 4194304 | tf_op jit(solution)/shard_map/pair_level/pallas_call | solution.py:575
  41.4 0.3 collective-permute-start.8
  41.6 1.2 %collective-permute-start.6 = (bf16[256,256]{1,0:T(8,128)(2,1)S(1)}, bf16[256,256]{1,0:T(8,128)(2,1)S(1)}, u32[]{:S(2)}, u32[]{:S(2)}) collective-permute-start(bf16[256,256]{1,0:T(8,128)(2,1)S(1)} %get-tuple-element.46), channel_id=1, source_target_pairs={{0,8},{8,0},{16,24},{24,16},{1,9},{9,1},{17,25},{25,17},{2,10},{10... | collective-permute-start | bytes 393224 | tf_op jit(solution)/shard_map/ppermute | solution.py:18
  42.9 0.2 collective-permute-start.7
  43.1 4.8 %collective-permute-done.4.refs_0_ = bf16[512,512]{1,0:T(8,128)(2,1)S(1)} collective-permute-done((bf16[512,512]{1,0:T(8,128)(2,1)S(1)}, bf16[512,512]{1,0:T(8,128)(2,1)S(1)}, u32[]{:S(2)}, u32[]{:S(2)}) %collective-permute-start.4) | collective-permute-done | bytes 524320 | tf_op jit(solution)/shard_map/ppermute | solution.py:18
  47.9 0.2 collective-permute-done.5.refs_1_
  48.1 2.0 %pair_level.5.sums_ref = f32[64,512]{1,0:T(8,128)S(1)} custom-call(f32[8,32,128]{2,1,0:T(8,128)S(1)} %get-tuple-element.31.pick_ref.mask_ref, f32[64,512]{1,0:T(8,128)S(1)} %get-tuple-element.41.sums_ref, bf16[2,2,256,1024]{3,2,1,0:T(8,128)(2,1)S(1)} %get-tuple-element.34.panel_ref, bf16[512,512]{1,0:T(8,128)(2,1)S(1)} %collective-permute-done.4.refs_0_, ...), custom_call_target="tpu_custom_call" | custom-call | flops 1073741824 | bytes 4194304 | tf_op jit(solution)/shard_map/pair_level/pallas_call | solution.py:575
  50.1 0.0 collective-permute-done.6.refs_0_
  50.1 0.9 %pair_level.6.sums_ref = f32[64,512]{1,0:T(8,128)S(1)} custom-call(f32[8,32,128]{2,1,0:T(8,128)S(1)} %get-tuple-element.31.pick_ref.mask_ref, f32[64,512]{1,0:T(8,128)S(1)} %pair_level.5.sums_ref, bf16[2,512,512]{2,1,0:T(8,128)(2,1)S(1)} %get-tuple-element.45.panel_ref, bf16[256,256]{1,0:T(8,128)(2,1)S(1)} %collective-permute-done.6.refs_0_), custom_call_target="tpu_custom_call" | custom-call | flops 268435456 | bytes 4194304 | tf_op jit(solution)/shard_map/pair_level/pallas_call | solution.py:575
  51.0 0.0 collective-permute-done.7.refs_0_
  51.0 0.0 collective-permute-done.8.refs_1_
  51.0 1.2 %pair_level.7 = (f32[16,512]{1,0:T(8,128)S(1)}, f32[16,512]{1,0:T(8,128)S(1)}, f32[16,512]{1,0:T(8,128)S(1)}, f32[16,512]{1,0:T(8,128)S(1)}) custom-call(f32[8,32,128]{2,1,0:T(8,128)S(1)} %get-tuple-element.31.pick_ref.mask_ref, f32[64,512]{1,0:T(8,128)S(1)} %pair_level.6.sums_ref, bf16[2,512,512]{2,1,0:T(8,128)(2,1)S(1)} %get-tuple-element.45.panel_ref, ...), custom_call_target="tpu_custom_call" | custom-call | flops 268435456 | bytes 4194304 | tf_op jit(solution)/shard_map/pair_level/pallas_call | solution.py:575
  52.3 1.5 %collective-permute-start.10 = (f32[16,512]{1,0:T(8,128)S(1)}, f32[16,512]{1,0:T(8,128)S(1)}, u32[]{:S(2)}, u32[]{:S(2)}) collective-permute-start(f32[16,512]{1,0:T(8,128)S(1)} %get-tuple-element.50), channel_id=1, source_target_pairs={{0,24},{8,16},{16,8},{24,0},{1,25},{9,17},{17,9},{25,1},{2,26},{10... | collective-permute-start | bytes 98312 | tf_op jit(solution)/shard_map/ppermute | solution.py:18
  53.8 1.3 %collective-permute-start.11 = (f32[16,512]{1,0:T(8,128)S(1)}, f32[16,512]{1,0:T(8,128)S(1)}, u32[]{:S(2)}, u32[]{:S(2)}) collective-permute-start(f32[16,512]{1,0:T(8,128)S(1)} %get-tuple-element.51), channel_id=1, source_target_pairs={{0,16},{8,24},{16,0},{24,8},{1,17},{9,25},{17,1},{25,9},{2,18},{10... | collective-permute-start | bytes 98312 | tf_op jit(solution)/shard_map/ppermute | solution.py:18
  55.1 0.0 collective-permute-start.9
  55.1 1.0 %collective-permute-done.10.refs_1_ = f32[16,512]{1,0:T(8,128)S(1)} collective-permute-done((f32[16,512]{1,0:T(8,128)S(1)}, f32[16,512]{1,0:T(8,128)S(1)}, u32[]{:S(2)}, u32[]{:S(2)}) %collective-permute-start.10) | collective-permute-done | bytes 32800 | tf_op jit(solution)/shard_map/ppermute | solution.py:18
  56.0 0.6 %collective-permute-done.11.refs_2_ = f32[16,512]{1,0:T(8,128)S(1)} collective-permute-done((f32[16,512]{1,0:T(8,128)S(1)}, f32[16,512]{1,0:T(8,128)S(1)}, u32[]{:S(2)}, u32[]{:S(2)}) %collective-permute-start.11) | collective-permute-done | bytes 32800 | tf_op jit(solution)/shard_map/ppermute | solution.py:18
  56.6 1.2 %collective-permute-done.9.refs_0_ = f32[16,512]{1,0:T(8,128)S(1)} collective-permute-done((f32[16,512]{1,0:T(8,128)S(1)}, f32[16,512]{1,0:T(8,128)S(1)}, u32[]{:S(2)}, u32[]{:S(2)}) %collective-permute-start.9) | collective-permute-done | bytes 32800 | tf_op jit(solution)/shard_map/ppermute | solution.py:18
  57.8 0.7 %finish.1 = f32[8,2,2,511]{3,2,1,0:T(2,128)} custom-call(f32[16,512]{1,0:T(8,128)S(1)} %collective-permute-done.9.refs_0_, f32[16,512]{1,0:T(8,128)S(1)} %collective-permute-done.10.refs_1_, f32[16,512]{1,0:T(8,128)S(1)} %collective-permute-done.11.refs_2_, f32[16,512]{1,0:T(8,128)S(1)} %get-tuple-element.52.refs_3_), custom_call_target="tpu_custom_call" | custom-call | tf_op jit(solution)/shard_map/finish/pallas_call | solution.py:605
Async XLA Ops:
  1.0 11.8 %copy-start = (s32[2,256]{1,0:T(2,128)S(1)}, s32[2,256]{1,0:T(2,128)}, u32[]{:S(2)}) copy-start(s32[2,256]{1,0:T(2,128)} %position_ref.5) | copy-start | bytes 6148
  1.1 11.8 %copy-start.1 = (s32[2,3,2]{1,2,0:T(2,128)S(1)}, s32[2,3,2]{1,2,0:T(2,128)}, u32[]{:S(2)}) copy-start(s32[2,3,2]{1,2,0:T(2,128)} %param.5) | copy-start | bytes 148
  1.1 11.7 %collective-permute-start = (bf16[528,256]{1,0:T(8,128)(2,1)S(1)}, bf16[528,256]{1,0:T(8,128)(2,1)S(1)}, u32[]{:S(2)}, u32[]{:S(2)}) collective-permute-start(bf16[528,256]{1,0:T(8,128)(2,1)S(1)} %first_piece.1._), channel_id=1, source_target_pairs={{0,16},{8,24},{16,0},{24,8},{1,17},{9,25},{17,1},{25,9},{2,18},{10... | collective-permute-start | bytes 811016 | tf_op jit(solution)/shard_map/ppermute | solution.py:18
  3.2 9.6 %collective-permute-start.1 = (bf16[528,256]{1,0:T(8,128)(2,1)S(1)}, bf16[528,256]{1,0:T(8,128)(2,1)S(1)}, u32[]{:S(2)}, u32[]{:S(2)}) collective-permute-start(bf16[528,256]{1,0:T(8,128)(2,1)S(1)} %first_piece.1._), channel_id=1, source_target_pairs={{0,8},{8,0},{16,24},{24,16},{1,9},{9,1},{17,25},{25,17},{2,10},{10... | collective-permute-start | bytes 811016 | tf_op jit(solution)/shard_map/ppermute | solution.py:18
  12.4 25.0 %collective-permute-start.2 = (bf16[512,1024]{1,0:T(8,128)(2,1)S(1)}, bf16[512,1024]{1,0:T(8,128)(2,1)S(1)}, u32[]{:S(2)}, u32[]{:S(2)}) collective-permute-start(bf16[512,1024]{1,0:T(8,128)(2,1)S(1)} %get-tuple-element.36), channel_id=1, source_target_pairs={{0,8},{8,0},{16,24},{24,16},{1,9},{9,1},{17,25},{25,17},{2,10},{10... | collective-permute-start | bytes 3145736 | tf_op jit(solution)/shard_map/ppermute | solution.py:18
  12.7 24.7 %collective-permute-start.3 = (bf16[512,1024]{1,0:T(8,128)(2,1)S(1)}, bf16[512,1024]{1,0:T(8,128)(2,1)S(1)}, u32[]{:S(2)}, u32[]{:S(2)}) collective-permute-start(bf16[512,1024]{1,0:T(8,128)(2,1)S(1)} %get-tuple-element.36), channel_id=1, source_target_pairs={{0,16},{8,24},{16,0},{24,8},{1,17},{9,25},{17,1},{25,9},{2,18},{10... | collective-permute-start | bytes 3145736 | tf_op jit(solution)/shard_map/ppermute | solution.py:18
  21.6 26.6 %collective-permute-start.5 = (bf16[528,512]{1,0:T(8,128)(2,1)S(1)}, bf16[528,512]{1,0:T(8,128)(2,1)S(1)}, u32[]{:S(2)}, u32[]{:S(2)}) collective-permute-start(bf16[528,512]{1,0:T(8,128)(2,1)S(1)} %get-tuple-element.43), channel_id=1, source_target_pairs={{0,16},{8,24},{16,0},{24,8},{1,17},{9,25},{17,1},{25,9},{2,18},{10... | collective-permute-start | bytes 1622024 | tf_op jit(solution)/shard_map/ppermute | solution.py:18
  23.0 24.9 %collective-permute-start.4 = (bf16[512,512]{1,0:T(8,128)(2,1)S(1)}, bf16[512,512]{1,0:T(8,128)(2,1)S(1)}, u32[]{:S(2)}, u32[]{:S(2)}) collective-permute-start(bf16[512,512]{1,0:T(8,128)(2,1)S(1)} %get-tuple-element.42), channel_id=1, source_target_pairs={{0,8},{8,0},{16,24},{24,16},{1,9},{9,1},{17,25},{25,17},{2,10},{10... | collective-permute-start | bytes 1572872 | tf_op jit(solution)/shard_map/ppermute | solution.py:18
  41.4 9.7 %collective-permute-start.8 = (bf16[256,512]{1,0:T(8,128)(2,1)S(1)}, bf16[256,512]{1,0:T(8,128)(2,1)S(1)}, u32[]{:S(2)}, u32[]{:S(2)}) collective-permute-start(bf16[256,512]{1,0:T(8,128)(2,1)S(1)} %get-tuple-element.48), channel_id=1, source_target_pairs={{0,16},{8,24},{16,0},{24,8},{1,17},{9,25},{17,1},{25,9},{2,18},{10... | collective-permute-start | bytes 786440 | tf_op jit(solution)/shard_map/ppermute | solution.py:18
  41.6 8.5 %collective-permute-start.6 = (bf16[256,256]{1,0:T(8,128)(2,1)S(1)}, bf16[256,256]{1,0:T(8,128)(2,1)S(1)}, u32[]{:S(2)}, u32[]{:S(2)}) collective-permute-start(bf16[256,256]{1,0:T(8,128)(2,1)S(1)} %get-tuple-element.46), channel_id=1, source_target_pairs={{0,8},{8,0},{16,24},{24,16},{1,9},{9,1},{17,25},{25,17},{2,10},{10... | collective-permute-start | bytes 393224 | tf_op jit(solution)/shard_map/ppermute | solution.py:18
  42.9 8.2 %collective-permute-start.7 = (bf16[256,256]{1,0:T(8,128)(2,1)S(1)}, bf16[256,256]{1,0:T(8,128)(2,1)S(1)}, u32[]{:S(2)}, u32[]{:S(2)}) collective-permute-start(bf16[256,256]{1,0:T(8,128)(2,1)S(1)} %get-tuple-element.47), channel_id=1, source_target_pairs={{0,8},{8,0},{16,24},{24,16},{1,9},{9,1},{17,25},{25,17},{2,10},{10... | collective-permute-start | bytes 393224 | tf_op jit(solution)/shard_map/ppermute | solution.py:18
  52.3 3.7 %collective-permute-start.10 = (f32[16,512]{1,0:T(8,128)S(1)}, f32[16,512]{1,0:T(8,128)S(1)}, u32[]{:S(2)}, u32[]{:S(2)}) collective-permute-start(f32[16,512]{1,0:T(8,128)S(1)} %get-tuple-element.50), channel_id=1, source_target_pairs={{0,24},{8,16},{16,8},{24,0},{1,25},{9,17},{17,9},{25,1},{2,26},{10... | collective-permute-start | bytes 98312 | tf_op jit(solution)/shard_map/ppermute | solution.py:18
  53.8 2.8 %collective-permute-start.11 = (f32[16,512]{1,0:T(8,128)S(1)}, f32[16,512]{1,0:T(8,128)S(1)}, u32[]{:S(2)}, u32[]{:S(2)}) collective-permute-start(f32[16,512]{1,0:T(8,128)S(1)} %get-tuple-element.51), channel_id=1, source_target_pairs={{0,16},{8,24},{16,0},{24,8},{1,17},{9,25},{17,1},{25,9},{2,18},{10... | collective-permute-start | bytes 98312 | tf_op jit(solution)/shard_map/ppermute | solution.py:18
  55.1 2.8 %collective-permute-start.9 = (f32[16,512]{1,0:T(8,128)S(1)}, f32[16,512]{1,0:T(8,128)S(1)}, u32[]{:S(2)}, u32[]{:S(2)}) collective-permute-start(f32[16,512]{1,0:T(8,128)S(1)} %get-tuple-element.49), channel_id=1, source_target_pairs={{0,8},{8,0},{16,24},{24,16},{1,9},{9,1},{17,25},{25,17},{2,10},{10... | collective-permute-start | bytes 98312 | tf_op jit(solution)/shard_map/ppermute | solution.py:18
